TPU v7x, 256 devices: a whole 4x4x8 slice. The times are simulated.
256 devices in a mesh: row: 32 (over z, y_lo, core), col: 8 (over y_hi, x).
Axes of the slice: x: 4, y: 4 (y_hi: 2, y_lo: 2; y = y_hi * 2 + y_lo), z: 8, core: 2. Of those that a mesh axis runs over, the one named last changes fastest.
Arguments:
- sketches: float32 [10240, 4096], P(('row', 'col')), may hold values from -30 to 30
- targets: float32 [10240, 32], P(('row', 'col')), may hold values from -6 to 6
Outputs:
- weights: float32 [10240, 32], P(('row', 'col'))
- residual: float32 [10240, 32], P(('row', 'col'))
All inputs are finite; a program needn't handle non-finite values.
Results may differ from a plain program's by a relative error of at most 0.0021.
The roundings to bfloat16 on the way count: a program that leaves them out, or rounds other values in their place, can miss the bound.
Values may be sent and summed in bfloat16 or wider, within the bound.
No kernel may reach another device: no remote copies, remote signals or barrier semaphores. Data moves between devices by JAX's collectives and lax.ppermute only.
A program may use at most 64 MiB of HBM per device.

v0:
```python
import jax
import jax.numpy as jnp
from jax import lax
from jax.sharding import PartitionSpec as P

ITERS = 2


sharpness = 4.0
ridge = 1.0


def unit_rows(sketches):
    scale = jnp.sqrt(jnp.sum(sketches * sketches, axis=1, keepdims=True) + 1e-06)
    return (sketches / scale).astype(jnp.bfloat16)


def kernel_block(left, right):
    cosines = jnp.dot(left, right.T, preferred_element_type=jnp.float32)
    return jnp.exp(sharpness * (cosines - 1.0))


def local_gram(first, second):
    return jnp.dot(first.T, second, precision=lax.Precision.HIGHEST)


def solve_small(matrix, rhs_block):
    matrix = 0.5 * (matrix + matrix.T)
    factor = jnp.linalg.cholesky(matrix)
    return jax.scipy.linalg.cho_solve((factor, True), rhs_block)


def times_small(left, small):
    return jnp.dot(left, small, precision=lax.Precision.HIGHEST)


def squares(residual):
    return lax.psum(local_gram(residual, residual), ("row", "col"))


def local(sketches, targets):
    units = unit_rows(sketches)
    row_block = lax.all_gather(units, "col", axis=0, tiled=True)
    tile = kernel_block(row_block, lax.all_gather(units, "row", axis=0, tiled=True))
    weights = jnp.zeros_like(targets)
    residual = targets
    direction = targets
    norm_now = squares(residual)
    for step in range(ITERS):
        whole = lax.all_gather(direction, "row", axis=0, tiled=True)
        partial_rows = jnp.dot(tile, whole, precision=lax.Precision.HIGHEST)
        image_rows = (
            lax.psum_scatter(partial_rows, "col", scatter_dimension=0, tiled=True)
            + ridge * direction
        )
        curve = lax.psum(local_gram(direction, image_rows), ("row", "col"))
        alpha = solve_small(curve, norm_now)
        weights = weights + times_small(direction, alpha)
        residual = residual - times_small(image_rows, alpha)
        norm_next = squares(residual)
        beta = solve_small(norm_now, norm_next)
        direction = residual + times_small(direction, beta)
        norm_now = norm_next
    return (weights, residual)


def solution(mesh):
    in_specs = (P(("row", "col"), None), P(("row", "col"), None))
    out_specs = (P(("row", "col"), None), P(("row", "col"), None))
    return jax.shard_map(local, mesh=mesh, in_specs=in_specs, out_specs=out_specs, check_vma=False)
```

profile of v0, /device:TPU:1, one launch (start us, length us, event | category | flops | bytes accessed | tf_op | source)
XLA Modules:
  0.0 531.8 jit_solution(11749445179916008779)
XLA Ops:
  7.2 0.0 copy-start
  7.2 0.0 all-gather.5.cloned.1.call-start
  7.2 1.2 multiply_reduce_fusion
  8.5 2.0 divide_convert_fusion
  10.4 0.0 copy-start.1
  10.4 0.0 all-gather.5.cloned.1.call-update
  10.5 0.0 all-gather.7.cloned.1.call-start
  10.5 0.7 all-gather.7.cloned.1.call-update
  11.2 0.0 copy-done
  11.2 40.0 %all-gather = f32[32,40,32]{1,2,0:T(8,128)S(1)} all-gather(f32[1,40,32]{1,2,0:T(8,128)S(1)} %bitcast.90), channel_id=1, replica_groups=mesh['row'=32,'col'=8] {'row'}, dimensions={0}, use_global_device_ids=true | all-gather | bytes 168960 | tf_op jit(solution)/shard_map/all_gather | solution.py:50
  51.2 0.3 copy.20
  51.5 0.3 reshape.21
  51.8 0.0 copy-done.1
  51.8 0.6 dynamic-slice
  53.1 0.1 fusion.30
  53.2 25.0 %all-gather.5.cloned.1.call-done = bf16[320,4096]{1,0:T(8,128)(2,1)} async-done(((bf16[40,4096]{1,0:T(8,128)(2,1)}), bf16[320,4096]{1,0:T(8,128)(2,1)}) %all-gather.5.cloned.1.call-update) | async-done | bytes 2621456 | tf_op jit(solution)/shard_map/all_gather | solution.py:43
  78.2 76.7 %all-gather.7.cloned.1.call-done = bf16[1280,4096]{1,0:T(8,128)(2,1)} async-done(((bf16[40,4096]{1,0:T(8,128)(2,1)}), bf16[1280,4096]{1,0:T(8,128)(2,1)}) %all-gather.7.cloned.1.call-update) | async-done | bytes 10485776 | tf_op jit(solution)/shard_map/all_gather | solution.py:44
  154.9 7.9 %fusion.1 = f32[320,1280]{1,0:T(8,128)S(1)} fusion(bf16[320,4096]{1,0:T(8,128)(2,1)} %all-gather.5.cloned.1.call-done, bf16[1280,4096]{1,0:T(8,128)(2,1)} %all-gather.7.cloned.1.call-done), kind=kOutput, calls=%fused_computation.2 | convolution fusion | flops 3356262400 | bytes 14745600 | tf_op jit(solution)/shard_map/dot_general | solution.py:19
  162.8 1.4 fusion.29
  164.2 34.5 %all-reduce = f32[320,32]{0,1:T(8,128)S(1)} all-reduce(f32[320,32]{0,1:T(8,128)S(1)} %fusion.29), channel_id=2, replica_groups=mesh['row'=32,'col'=8] {'col'}, use_global_device_ids=true, to_apply=%region_1.0.clone | all-reduce | flops 10240 | bytes 81920
  198.7 0.2 convolution_bitcast_fusion.2
  199.0 79.4 %all-reduce.2 = (f32[32,32]{1,0:T(8,128)S(1)}, f32[32,32]{1,0:T(8,128)S(1)}) all-reduce(f32[32,32]{1,0:T(8,128)S(1)} %fusion.30, f32[32,32]{1,0:T(8,128)S(1)} %convolution_bitcast_fusion.2), channel_id=1, replica_groups=mesh['row'=32,'col'=8] {'row','col'}, use_global_device_ids=true, to_apply=%region_5.7 | all-reduce | flops 2048 | bytes 16384 | tf_op jit(solution)/shard_map/psum | solution.py:38
  278.4 0.1 copy.24
  278.4 0.1 copy.22
  278.5 0.1 copy.23
  278.6 2.9 cholesky.59
  281.6 0.6 compare_reduce_fusion.2
  282.2 0.7 fusion.3
  282.9 2.4 custom-call.9
  285.3 0.2 fusion.20
  285.5 0.1 fusion.18
  285.7 0.3 convolution_subtract_fusion.1
  285.9 0.2 convolution_bitcast_fusion.1
  286.2 0.1 copy.25
  286.2 2.9 cholesky.70
  289.2 0.6 compare_reduce_fusion.1
  289.8 0.7 fusion.4
  290.5 2.4 custom-call.10
  292.9 0.2 fusion.31
  293.1 73.9 %psum.30 = f32[32,32]{1,0:T(8,128)S(1)} all-reduce(f32[32,32]{1,0:T(8,128)S(1)} %fusion.31), channel_id=1, replica_groups=mesh['row'=32,'col'=8] {'row','col'}, use_global_device_ids=true, to_apply=%region_6.0 | all-reduce | flops 1024 | bytes 8192 | tf_op jit(solution)/shard_map/psum | solution.py:38
  367.0 0.2 fusion.14
  367.2 0.1 fusion.12
  367.3 0.2 fusion.2
  367.5 34.7 %all-gather.1 = f32[32,40,32]{1,2,0:T(8,128)S(1)} all-gather(f32[1,40,32]{1,2,0:T(8,128)S(1)} %bitcast.91), channel_id=1, replica_groups=mesh['row'=32,'col'=8] {'row'}, dimensions={0}, use_global_device_ids=true | all-gather | bytes 168960 | tf_op jit(solution)/shard_map/all_gather | solution.py:50
  402.3 0.3 copy.26
  402.6 0.3 reshape.23
  402.9 1.4 fusion.32
  404.3 31.7 %all-reduce.1 = f32[320,32]{0,1:T(8,128)S(1)} all-reduce(f32[320,32]{0,1:T(8,128)S(1)} %fusion.32), channel_id=3, replica_groups=mesh['row'=32,'col'=8] {'col'}, use_global_device_ids=true, to_apply=%region_7.10.clone | all-reduce | flops 10240 | bytes 81920
  436.0 0.2 fusion.24
  436.2 79.9 %psum.31 = f32[32,32]{1,0:T(8,128)S(1)} all-reduce(f32[32,32]{1,0:T(8,128)S(1)} %fusion.24), channel_id=1, replica_groups=mesh['row'=32,'col'=8] {'row','col'}, use_global_device_ids=true, to_apply=%region_8.11 | all-reduce | flops 1024 | bytes 8192 | tf_op jit(solution)/shard_map/psum | solution.py:56
  516.1 0.1 copy.27
  516.2 0.1 copy.28
  516.2 2.9 cholesky.81
  519.2 0.6 compare_reduce_fusion
  519.8 0.7 fusion.5
  520.5 2.4 custom-call.11
  522.9 0.2 fusion.8
  523.2 0.1 fusion.6
  523.3 0.9 convolution_subtract_fusion
  524.2 0.8 convolution_add_fusion.1
  (9 shorter events, 0.1 us)
Async XLA Ops:
  7.2 4.1 copy-start
  7.2 71.0 %all-gather.5.cloned.1.call-start = ((), (), s32[]{:S(2)}) async-start(), calls=%async_computation | async-start | bytes 2949120 | tf_op jit(solution)/shard_map/all_gather | solution.py:43
  10.4 41.4 %copy-start.1 = (u32[256]{0:T(256)S(1)}, u32[256]{0:T(256)}, u32[]{:S(2)}) copy-start(u32[256]{0:T(256)} %constant.50) | copy-start | bytes 3076
  10.5 144.5 %all-gather.7.cloned.1.call-start = ((), (), s32[]{:S(2)}) async-start(), calls=%async_computation.1 | async-start | bytes 10813440 | tf_op jit(solution)/shard_map/all_gather | solution.py:44
Sparse Core Ops, SparseCore 0:
  10.6 67.5 all-gather.4
  80.1 74.8 all-gather.6
where the time goes:
time: 533 us; the launch traced here: 532 us
  blocking collectives  374 us (70%)
  waiting for transfers between devices  102 us (19%)
  other arithmetic  23.3 us (4%)
  matrix products  14.9 us (3%)
  between operations  14.9 us (3%)
    psum x2, blocking collectives, squares(): return lax.psum(local_gram(residual, residual), ('row', 'col'))  153 us
    psum x1, blocking collectives, local(): curve = lax.psum(local_gram(direction, image_rows), ('row', 'col'))  79.9 us
    all_gather x1, waiting for transfers between devices, local(): lax.all_gather(units, 'row', axis=0, tiled=True)  76.7 us
    all_gather x2, blocking collectives, local(): whole = lax.all_gather(direction, 'row', axis=0, tiled=True)  74.7 us
    unnamed x2, blocking collectives  66.2 us
    all_gather x1, waiting for transfers between devices, local(): row_block = lax.all_gather(units, 'col', axis=0, tiled=True)  25 us
    another operation x9, other arithmetic, solve_small(): factor = jnp.linalg.cholesky(matrix)  10.8 us
  transfers between devices with their start and end apart: 2, of which 2 were waited for; matrix products, arithmetic and copies ran while one was open for 0% of the time, Pallas kernels for 0%

commit v1 on v0

v1 whole, which is shorter than its diff:
```python
import jax
import jax.numpy as jnp
from jax import lax
from jax.sharding import PartitionSpec as P

sharpness = 4.0
ridge = 1.0
AXES = ("row", "col")
NZ, NY, NX, NC = 8, 4, 4, 2
HIGH = lax.Precision.HIGHEST


def device(z, y, x, c):
    return ((z * 2 + y % 2) * 2 + c) * 8 + (y // 2) * 4 + x


LINES = [
    [device(z, y, x, c) for z in range(NZ)]
    for y in range(NY)
    for x in range(NX)
    for c in range(NC)
]
PLANES = [
    [device(z, y, x, c) for y in range(NY) for x in range(NX)]
    for z in range(NZ)
    for c in range(NC)
]
CORES = [
    (device(z, y, x, c), device(z, y, x, 1 - c))
    for z in range(NZ)
    for y in range(NY)
    for x in range(NX)
    for c in range(NC)
]


def unit_rows(sketches):
    scale = jnp.sqrt(jnp.sum(sketches * sketches, axis=1, keepdims=True) + 1e-06)
    return (sketches / scale).astype(jnp.bfloat16)


def mm(a, b):
    return jnp.dot(a, b, precision=HIGH)


def nt(a, b):
    return lax.dot_general(a, b, (((1,), (1,)), ((), ())), precision=HIGH)


def to_all(value, groups):
    size = len(groups[0])
    copies = jnp.broadcast_to(value[None], (size,) + value.shape)
    return lax.all_to_all(copies, AXES, 0, 0, axis_index_groups=groups, tiled=True)


def other_core(value):
    return lax.ppermute(value, AXES, CORES)


def solve_small(matrix, rhs_block):
    matrix = 0.5 * (matrix + matrix.T)
    factor = jnp.linalg.cholesky(matrix)
    return jax.scipy.linalg.cho_solve((factor, True), rhs_block)


def local(sketches, targets):
    units = unit_rows(sketches)
    rows, rhs = targets.shape
    line = NZ * rows
    z = lax.axis_index("row") // 4
    mine = lax.all_gather(units, AXES, axis=0, tiled=True, axis_index_groups=LINES)
    t_own = targets.T
    t_plane = to_all(t_own, PLANES)
    t_line = to_all(t_own, LINES)
    plane = to_all(units, PLANES).reshape(NY * NX * rows, -1)
    theirs = other_core(mine)

    def tile(left):
        cosines = lax.dot_general(
            plane, left, (((1,), (1,)), ((), ())), preferred_element_type=jnp.float32
        )
        return jnp.exp(sharpness * (cosines - 1.0))

    k_mine, k_theirs = tile(mine), tile(theirs)

    t_plane = t_plane.transpose(1, 0, 2).reshape(rhs, -1)
    t_line = t_line.transpose(1, 0, 2).reshape(rhs, -1)
    m0 = nt(t_plane, t_plane)

    part = jnp.concatenate([mm(t_plane, k_mine), m0], axis=1)
    away = jnp.concatenate([mm(t_plane, k_theirs), m0], axis=1)
    part = part + other_core(away)
    part = jnp.sum(to_all(part, LINES), axis=0)
    v1_line = part[:, :line] + ridge * t_line
    m0 = part[:, line:]

    m12 = jnp.concatenate([nt(t_line, v1_line), nt(v1_line, v1_line)], axis=1)
    far = other_core(jnp.concatenate([v1_line, m12], axis=1))
    v1_far = far[:, :line]
    m12 = m12 + far[:, line:]
    v1_own = lax.dynamic_slice(v1_line, (0, z * rows), (rhs, rows))
    got = to_all(jnp.concatenate([v1_own, m12], axis=1), PLANES)
    v1_plane = got[:, :, :rows].transpose(1, 0, 2).reshape(rhs, -1)
    m12 = jnp.sum(got[:, :, rows:], axis=0)
    m1, m2 = m12[:, :rhs], m12[:, rhs:]

    near2 = mm(v1_plane, k_mine)
    far2 = mm(v1_plane, k_theirs)
    m3 = nt(v1_line, near2) + nt(v1_far, far2)
    sent = other_core(jnp.concatenate([far2, m3], axis=1))
    near2 = near2 + sent[:, :line]
    m3 = m3 + sent[:, line:]
    chunks = near2.reshape(rhs, NZ, rows).transpose(1, 0, 2)
    chunks = jnp.concatenate([chunks, jnp.broadcast_to(m3[None], (NZ, rhs, rhs))], axis=2)
    chunks = jnp.sum(
        lax.all_to_all(chunks, AXES, 0, 0, axis_index_groups=LINES, tiled=True), axis=0
    )
    v2_own = chunks[:, :rows] + ridge * v1_own
    m3 = jnp.sum(to_all(chunks[:, rows:], PLANES), axis=0)
    m3 = m3 + ridge * m2

    a1 = solve_small(m1, m0)
    m1a = mm(m1, a1)
    rr1 = m0 - m1a - m1a.T + mm(a1.T, mm(m2, a1))
    e = jnp.eye(rhs, dtype=jnp.float32) + solve_small(m0, rr1)
    em2a = mm(e.T, mm(m2, a1))
    curve = mm(e.T, mm(m1, e)) - em2a - em2a.T + mm(a1.T, mm(m3, a1))
    a2 = solve_small(curve, rr1)
    direction = mm(e.T, t_own) - mm(a1.T, v1_own)
    image = mm(e.T, v1_own) - mm(a1.T, v2_own)
    weights = mm(a1.T, t_own) + mm(a2.T, direction)
    residual = t_own - mm(a1.T, v1_own) - mm(a2.T, image)
    return weights.T, residual.T


def solution(mesh):
    in_specs = (P(AXES, None), P(AXES, None))
    out_specs = (P(AXES, None), P(AXES, None))
    return jax.shard_map(local, mesh=mesh, in_specs=in_specs, out_specs=out_specs, check_vma=False)
```

time: 533 us -> 231 us (0.43)
  blocking collectives: 374 us -> 14 us
  starting transfers between devices: 0.08 us -> 40.4 us
  local copies, waits for them, and re-layouts: 2.21 us -> 10.8 us
  matrix products: 14.9 us -> 20.8 us
    psum x3 -> x0, blocking collectives: 233 us -> none  [the longest x2 153 us: squares(): return lax.psum(local_gram(residual, residual), ('row', 'col'))]
    all_gather x2 -> x1, waiting for transfers between devices: 102 us -> 19.7 us  [local(): lax.all_gather(units, AXES, axis=0, tiled=True, axis_index_groups=LINES)]
    all_to_all x0 -> x6, waiting for transfers between devices: none -> 81.9 us  [the longest x5 73.8 us: to_all(): lax.all_to_all(copies, AXES, 0, 0, axis_index_groups=groups, tiled=True)]
    all_gather x2 -> x0, blocking collectives: 74.7 us -> none  [local(): whole = lax.all_gather(direction, 'row', axis=0, tiled=True)]
    unnamed x2 -> x0, blocking collectives: 66.2 us -> none
    all_to_all x0 -> x6, starting transfers between devices: none -> 31.5 us  [the longest x5 28.1 us: to_all(): lax.all_to_all(copies, AXES, 0, 0, axis_index_groups=groups, tiled=True)]
    all_to_all x0 -> x1, blocking collectives: none -> 14 us  [to_all(): lax.all_to_all(copies, AXES, 0, 0, axis_index_groups=groups, tiled=True)]
    ppermute x0 -> x4, starting transfers between devices: none -> 8.88 us  [other_core(): return lax.ppermute(value, AXES, CORES)]
  transfers between devices with their start and end apart: 2 -> 11, of which waited for: 2 -> 9; matrix products, arithmetic and copies ran while one was open for 0% -> 12% of each run, Pallas kernels for 0% -> 0%
where the time goes in v1:
time: 231 us; the launch traced here: 230 us
  waiting for transfers between devices  102 us (44%)
  starting transfers between devices  40.4 us (17%)
  other arithmetic  27.2 us (12%)
  matrix products  20.8 us (9%)
  between operations  14.5 us (6%)
  blocking collectives  14 us (6%)
  local copies, waits for them, and re-layouts  10.8 us (5%)
    all_to_all x5, waiting for transfers between devices, to_all(): lax.all_to_all(copies, AXES, 0, 0, axis_index_groups=groups, tiled=True)  73.8 us
    all_to_all x5, starting transfers between devices, to_all(): lax.all_to_all(copies, AXES, 0, 0, axis_index_groups=groups, tiled=True)  28.1 us
    all_gather x1, waiting for transfers between devices, local(): lax.all_gather(units, AXES, axis=0, tiled=True, axis_index_groups=LINES)  19.7 us
    all_to_all x1, blocking collectives, to_all(): lax.all_to_all(copies, AXES, 0, 0, axis_index_groups=groups, tiled=True)  14 us
    dot_general x2, matrix products, tile(): lax.dot_general(plane, left, (((1,), (1,)), ((), ())), preferred_element_...  11.1 us
    another operation x9, other arithmetic, solve_small(): factor = jnp.linalg.cholesky(matrix)  10.8 us
    another operation x6, other arithmetic, solve_small(): return jax.scipy.linalg.cho_solve((factor, True), rhs_block)  9.26 us
    ppermute x4, starting transfers between devices, other_core(): return lax.ppermute(value, AXES, CORES)  8.88 us
  transfers between devices with their start and end apart: 11, of which 9 were waited for; matrix products, arithmetic and copies ran while one was open for 12% of the time, Pallas kernels for 0%

profile of v1, /device:TPU:1, one launch (start us, length us, event | category | flops | bytes accessed | tf_op | source)
XLA Modules:
  0.0 230.0 jit_solution(8117955702057685182)
XLA Ops:
  7.2 1.2 multiply_reduce_fusion
  8.5 2.0 divide_convert_fusion
  10.4 0.7 broadcast_in_dim.15
  11.2 0.2 reshape.49
  11.4 14.0 %all_to_all.35 = f32[16,1,1280]{2,1,0:T(1,128)S(1)} all-to-all(f32[16,1,1280]{2,1,0:T(1,128)S(1)} %reshape.49), channel_id=1, replica_groups={{0,1,2,3,16,17,18,19,4,5,6,7,20,21,22,23},{8,9,10,11,24,25,26,27,12,13,..., dimensions={0} | all-to-all | bytes 163840 | tf_op jit(solution)/shard_map/all_to_all | solution.py:53
  25.4 4.0 %broadcast_in_dim.14 = bf16[16,40,4096]{2,1,0:T(8,128)(2,1)} broadcast(bf16[40,4096]{1,0:T(8,128)(2,1)} %divide_convert_fusion), dimensions={1,2} | broadcast | bytes 5570560 | tf_op jit(solution)/shard_map/broadcast_in_dim | solution.py:52
  29.4 4.7 %all-to-all-start = ((bf16[16,40,4096]{2,1,0:T(8,128)(2,1)}), bf16[16,40,4096]{2,1,0:T(8,128)(2,1)}, u32[]{:S(2)}, u32[]{:S(2)}) async-start(bf16[16,40,4096]{2,1,0:T(8,128)(2,1)} %broadcast_in_dim.14), calls=%async_computation | async-start | bytes 10485760 | tf_op jit(solution)/shard_map/all_to_all | solution.py:53
  34.1 19.7 %all-gather.2.cloned.1.call-done = bf16[320,4096]{1,0:T(8,128)(2,1)} async-done(((bf16[40,4096]{1,0:T(8,128)(2,1)}), bf16[320,4096]{1,0:T(8,128)(2,1)}) %all-gather.2.cloned.1.call-update) | async-done | bytes 2621456 | tf_op jit(solution)/shard_map/all_gather | solution.py:71
  53.8 3.5 %collective-permute-start = (bf16[320,4096]{1,0:T(8,128)(2,1)}, bf16[320,4096]{1,0:T(8,128)(2,1)}, u32[]{:S(2)}, u32[]{:S(2)}) collective-permute-start(bf16[320,4096]{1,0:T(8,128)(2,1)} %all-gather.2.cloned.1.call-done), channel_id=1, source_target_pairs={{0,8},{8,0},{1,9},{9,1},{2,10},{10,2},{3,11},{11,3},{16,24},{24,16... | collective-permute-start | bytes 7864328 | tf_op jit(solution)/shard_map/ppermute | solution.py:57
  57.4 0.8 reshape.47
  58.1 0.5 broadcast.81
  58.6 0.8 reduce.5
  60.0 0.4 convolution_bitcast_fusion.4
  60.4 48.5 %all-to-all-done = bf16[16,40,4096]{2,1,0:T(8,128)(2,1)} async-done(((bf16[16,40,4096]{2,1,0:T(8,128)(2,1)}), bf16[16,40,4096]{2,1,0:T(8,128)(2,1)}, u32[]{:S(2)}, u32[]{:S(2)}) %all-to-all-start) | async-done | bytes 5242912 | tf_op jit(solution)/shard_map/all_to_all | solution.py:53
  108.8 8.0 %all-to-all-start.3 = ((f32[8,1,1280]{2,1,0:T(1,128)}), f32[8,1,1280]{2,1,0:T(1,128)S(1)}, u32[]{:S(2)}, u32[]{:S(2)}) async-start(f32[8,1,1280]{2,1,0:T(1,128)} %reshape.47), calls=%async_computation.3 | async-start | bytes 81920 | tf_op jit(solution)/shard_map/all_to_all | solution.py:53
  116.8 5.6 %fusion.3 = f32[640,320]{0,1:T(8,128)S(1)} fusion(bf16[640,4096]{1,0:T(8,128)(2,1)} %bitcast, bf16[320,4096]{1,0:T(8,128)(2,1)} %all-gather.2.cloned.1.call-done), kind=kOutput, calls=%fused_computation.5 | convolution fusion | flops 1678131200 | bytes 8683520 | tf_op jit(solution)/shard_map/dot_general | solution.py:79
  122.4 5.6 %fusion.1 = f32[640,320]{0,1:T(8,128)S(1)} fusion(bf16[640,4096]{1,0:T(8,128)(2,1)} %bitcast, bf16[320,4096]{1,0:T(8,128)(2,1)} %collective-permute-done), kind=kOutput, calls=%fused_computation.2 | convolution fusion | flops 1678131200 | bytes 8683520 | tf_op jit(solution)/shard_map/dot_general | solution.py:79
  128.0 0.8 convolution_bitcast_fusion
  128.9 3.3 %collective-permute-start.1 = (f32[32,352]{1,0:T(8,128)S(1)}, f32[32,352]{1,0:T(8,128)S(1)}, u32[]{:S(2)}, u32[]{:S(2)}) collective-permute-start(f32[32,352]{1,0:T(8,128)S(1)} %pad_maximum_fusion.1), channel_id=1, source_target_pairs={{0,8},{8,0},{1,9},{9,1},{2,10},{10,2},{3,11},{11,3},{16,24},{24,16... | collective-permute-start | bytes 135176 | tf_op jit(solution)/shard_map/ppermute | solution.py:57
  132.2 0.8 convolution_bitcast_fusion.1
  133.1 0.8 broadcast_in_dim.16
  133.9 6.9 %all-to-all-start.2 = ((f32[8,32,352]{2,1,0:T(8,128)}), f32[8,32,352]{2,1,0:T(8,128)S(1)}, u32[]{:S(2)}, u32[]{:S(2)}) async-start(f32[8,32,352]{2,1,0:T(8,128)} %broadcast_in_dim.16), calls=%async_computation.2 | async-start | bytes 786432 | tf_op jit(solution)/shard_map/all_to_all | solution.py:53
  140.8 0.7 reduce.4
  141.9 14.1 %all-to-all-done.2 = f32[8,32,352]{2,1,0:T(8,128)S(1)} async-done(((f32[8,32,352]{2,1,0:T(8,128)}), f32[8,32,352]{2,1,0:T(8,128)S(1)}, u32[]{:S(2)}, u32[]{:S(2)}) %all-to-all-start.2) | async-done | bytes 360480 | tf_op jit(solution)/shard_map/all_to_all | solution.py:53
  156.7 2.9 %cholesky.70 = f32[32,32]{1,0:T(8,128)S(1)} custom-call(f32[32,32]{1,0:T(8,128)S(1)} %fusion.21), custom_call_target="Cholesky" | custom-call | tf_op jit(solution)/shard_map/jit(cholesky)/cholesky | solution.py:62
  159.8 0.5 collective-permute-start.2
  160.3 0.6 compare_reduce_fusion.1
  161.0 0.2 collective-permute-done.2
  161.4 0.7 broadcast_in_dim.18
  162.1 5.0 %all-to-all-start.4 = ((f32[16,32,104]{2,1,0:T(8,128)}), f32[16,32,104]{2,1,0:T(8,128)S(1)}, u32[]{:S(2)}, u32[]{:S(2)}) async-start(f32[16,32,104]{2,1,0:T(8,128)} %broadcast_in_dim.18), calls=%async_computation.4 | async-start | bytes 524288 | tf_op jit(solution)/shard_map/all_to_all | solution.py:53
  167.1 0.7 fusion.7
  167.7 2.4 %custom-call.10 = f32[1,32,32]{1,2,0:T(8,128)S(1)} custom-call(f32[1,32,32]{2,1,0:T(8,128)S(1)} %fusion.7), custom_call_target="InvertDiagBlocksLowerTriangular" | custom-call | tf_op jit(solution)/shard_map/jit(_cho_solve)/triangular_solve | solution.py:63
  170.2 5.0 %all-to-all-done.4 = f32[16,32,104]{2,1,0:T(8,128)S(1)} async-done(((f32[16,32,104]{2,1,0:T(8,128)}), f32[16,32,104]{2,1,0:T(8,128)S(1)}, u32[]{:S(2)}, u32[]{:S(2)}) %all-to-all-start.4) | async-done | bytes 213024 | tf_op jit(solution)/shard_map/all_to_all | solution.py:53
  175.5 2.9 %cholesky.59 = f32[32,32]{1,0:T(8,128)S(1)} custom-call(f32[32,32]{1,0:T(8,128)S(1)} %fusion.27), custom_call_target="Cholesky" | custom-call | tf_op jit(solution)/shard_map/jit(cholesky)/cholesky | solution.py:62
  178.5 0.6 compare_reduce_fusion.2
  179.1 0.7 fusion.6
  179.8 2.4 %custom-call.9 = f32[1,32,32]{1,2,0:T(8,128)S(1)} custom-call(f32[1,32,32]{2,1,0:T(8,128)S(1)} %fusion.6), custom_call_target="InvertDiagBlocksLowerTriangular" | custom-call | tf_op jit(solution)/shard_map/jit(_cho_solve)/triangular_solve | solution.py:63
  182.2 0.3 fusion.25
  182.8 0.2 fusion.33
  183.3 0.8 fusion.46
  184.2 0.8 fusion.45
  185.0 0.2 convolution_add_fusion.5
  185.3 0.2 fusion.19
  185.6 0.2 fusion.49
  186.0 0.2 fusion.44
  186.9 1.5 collective-permute-start.3
  188.4 0.2 convolution_subtract_fusion.2
  189.0 0.3 collective-permute-done.3
  189.5 0.7 pad_maximum_fusion
  190.3 3.4 %all-to-all-start.5 = ((f32[8,32,72]{2,1,0:T(8,128)}), f32[8,32,72]{2,1,0:T(8,128)S(1)}, u32[]{:S(2)}, u32[]{:S(2)}) async-start(f32[8,32,72]{2,1,0:T(8,128)} %pad_maximum_fusion), calls=%async_computation.5 | async-start | bytes 262144 | tf_op jit(solution)/shard_map/all_to_all | solution.py:116
  193.9 8.1 %all-to-all-done.5 = f32[8,32,72]{2,1,0:T(8,128)S(1)} async-done(((f32[8,32,72]{2,1,0:T(8,128)}), f32[8,32,72]{2,1,0:T(8,128)S(1)}, u32[]{:S(2)}, u32[]{:S(2)}) %all-to-all-start.5) | async-done | bytes 73760 | tf_op jit(solution)/shard_map/all_to_all | solution.py:116
  202.1 0.8 reshape.51
  202.9 3.5 %all-to-all-start.6 = ((f32[16,1,1024]{2,1,0:T(1,128)}), f32[16,1,1024]{2,1,0:T(1,128)S(1)}, u32[]{:S(2)}, u32[]{:S(2)}) async-start(f32[16,1,1024]{2,1,0:T(1,128)} %reshape.51), calls=%async_computation.6 | async-start | bytes 131072 | tf_op jit(solution)/shard_map/all_to_all | solution.py:53
  206.4 0.2 convolution_subtract_fusion.1
  206.6 6.2 %all-to-all-done.6 = f32[16,1,1024]{2,1,0:T(1,128)S(1)} async-done(((f32[16,1,1024]{2,1,0:T(1,128)}), f32[16,1,1024]{2,1,0:T(1,128)S(1)}, u32[]{:S(2)}, u32[]{:S(2)}) %all-to-all-start.6) | async-done | bytes 65568 | tf_op jit(solution)/shard_map/all_to_all | solution.py:53
  212.9 0.8 reduce.6
  214.0 0.2 fusion.48
  214.4 2.9 %cholesky.81 = f32[32,32]{1,0:T(8,128)S(1)} custom-call(f32[32,32]{1,0:T(8,128)S(1)} %fusion.13), custom_call_target="Cholesky" | custom-call | tf_op jit(solution)/shard_map/jit(cholesky)/cholesky | solution.py:62
  217.4 0.6 compare_reduce_fusion
  218.0 0.7 fusion.8
  218.7 2.4 %custom-call.11 = f32[1,32,32]{1,2,0:T(8,128)S(1)} custom-call(f32[1,32,32]{2,1,0:T(8,128)S(1)} %fusion.8), custom_call_target="InvertDiagBlocksLowerTriangular" | custom-call | tf_op jit(solution)/shard_map/jit(_cho_solve)/triangular_solve | solution.py:63
  221.1 0.2 fusion.11
  221.5 0.8 convolution_subtract_fusion
  222.3 0.8 convolution_add_fusion.2
  (70 shorter events, 5.6 us)
Async XLA Ops:
  7.2 46.7 %all-gather.2.cloned.1.call-start = ((), (), s32[]{:S(2)}) async-start(), calls=%async_computation.7 | async-start | bytes 2949120 | tf_op jit(solution)/shard_map/all_gather | solution.py:71
  29.4 27.9 %copy-start = (f32[40,32]{0,1:T(8,128)S(1)}, f32[40,32]{0,1:T(8,128)}, u32[]{:S(2)}) copy-start(f32[40,32]{0,1:T(8,128)} %param.6) | copy-start | bytes 15364
  29.4 79.4 %all-to-all-start = ((bf16[16,40,4096]{2,1,0:T(8,128)(2,1)}), bf16[16,40,4096]{2,1,0:T(8,128)(2,1)}, u32[]{:S(2)}, u32[]{:S(2)}) async-start(bf16[16,40,4096]{2,1,0:T(8,128)(2,1)} %broadcast_in_dim.14), calls=%async_computation | async-start | bytes 10485760 | tf_op jit(solution)/shard_map/all_to_all | solution.py:53
  53.8 68.6 %collective-permute-start = (bf16[320,4096]{1,0:T(8,128)(2,1)}, bf16[320,4096]{1,0:T(8,128)(2,1)}, u32[]{:S(2)}, u32[]{:S(2)}) collective-permute-start(bf16[320,4096]{1,0:T(8,128)(2,1)} %all-gather.2.cloned.1.call-done), channel_id=1, source_target_pairs={{0,8},{8,0},{1,9},{9,1},{2,10},{10,2},{3,11},{11,3},{16,24},{24,16... | collective-permute-start | bytes 7864328 | tf_op jit(solution)/shard_map/ppermute | solution.py:57
  108.8 24.3 %all-to-all-start.3 = ((f32[8,1,1280]{2,1,0:T(1,128)}), f32[8,1,1280]{2,1,0:T(1,128)S(1)}, u32[]{:S(2)}, u32[]{:S(2)}) async-start(f32[8,1,1280]{2,1,0:T(1,128)} %reshape.47), calls=%async_computation.3 | async-start | bytes 81920 | tf_op jit(solution)/shard_map/all_to_all | solution.py:53
  128.9 4.2 %collective-permute-start.1 = (f32[32,352]{1,0:T(8,128)S(1)}, f32[32,352]{1,0:T(8,128)S(1)}, u32[]{:S(2)}, u32[]{:S(2)}) collective-permute-start(f32[32,352]{1,0:T(8,128)S(1)} %pad_maximum_fusion.1), channel_id=1, source_target_pairs={{0,8},{8,0},{1,9},{9,1},{2,10},{10,2},{3,11},{11,3},{16,24},{24,16... | collective-permute-start | bytes 135176 | tf_op jit(solution)/shard_map/ppermute | solution.py:57
  133.9 22.1 %all-to-all-start.2 = ((f32[8,32,352]{2,1,0:T(8,128)}), f32[8,32,352]{2,1,0:T(8,128)S(1)}, u32[]{:S(2)}, u32[]{:S(2)}) async-start(f32[8,32,352]{2,1,0:T(8,128)} %broadcast_in_dim.16), calls=%async_computation.2 | async-start | bytes 786432 | tf_op jit(solution)/shard_map/all_to_all | solution.py:53
  159.8 1.4 collective-permute-start.2
  162.1 13.1 %all-to-all-start.4 = ((f32[16,32,104]{2,1,0:T(8,128)}), f32[16,32,104]{2,1,0:T(8,128)S(1)}, u32[]{:S(2)}, u32[]{:S(2)}) async-start(f32[16,32,104]{2,1,0:T(8,128)} %broadcast_in_dim.18), calls=%async_computation.4 | async-start | bytes 524288 | tf_op jit(solution)/shard_map/all_to_all | solution.py:53
  186.9 2.4 %collective-permute-start.3 = (f32[32,352]{1,0:T(8,128)S(1)}, f32[32,352]{1,0:T(8,128)S(1)}, u32[]{:S(2)}, u32[]{:S(2)}) collective-permute-start(f32[32,352]{1,0:T(8,128)S(1)} %pad_maximum_fusion.4), channel_id=1, source_target_pairs={{0,8},{8,0},{1,9},{9,1},{2,10},{10,2},{3,11},{11,3},{16,24},{24,16... | collective-permute-start | bytes 135176 | tf_op jit(solution)/shard_map/ppermute | solution.py:57
  190.3 11.7 %all-to-all-start.5 = ((f32[8,32,72]{2,1,0:T(8,128)}), f32[8,32,72]{2,1,0:T(8,128)S(1)}, u32[]{:S(2)}, u32[]{:S(2)}) async-start(f32[8,32,72]{2,1,0:T(8,128)} %pad_maximum_fusion), calls=%async_computation.5 | async-start | bytes 262144 | tf_op jit(solution)/shard_map/all_to_all | solution.py:116
  202.9 10.0 %all-to-all-start.6 = ((f32[16,1,1024]{2,1,0:T(1,128)}), f32[16,1,1024]{2,1,0:T(1,128)S(1)}, u32[]{:S(2)}, u32[]{:S(2)}) async-start(f32[16,1,1024]{2,1,0:T(1,128)} %reshape.51), calls=%async_computation.6 | async-start | bytes 131072 | tf_op jit(solution)/shard_map/all_to_all | solution.py:53
Sparse Core Ops, SparseCore 0:
  10.6 43.1 all-gather.1

commit v2 on v1

v2 whole, which is shorter than its diff:
```python
import functools

import jax
import jax.numpy as jnp
from jax import lax
from jax.experimental import pallas as pl
from jax.experimental.pallas import tpu as pltpu
from jax.sharding import PartitionSpec as P

sharpness = 4.0
AXES = ("row", "col")
NZ, NY, NX, NC = 8, 4, 4, 2
HIGH = lax.Precision.HIGHEST
PAD = 128


def device(z, y, x, c):
    z, y, x = z % NZ, y % NY, x % NX
    return ((z * 2 + y % 2) * 2 + c) * 8 + (y // 2) * 4 + x


PLACES = [
    (z, y, x, c) for z in range(NZ) for y in range(NY) for x in range(NX) for c in range(NC)
]
LINES = [
    [device(z, y, x, c) for z in range(NZ)]
    for y in range(NY)
    for x in range(NX)
    for c in range(NC)
]
PLANES = [
    [device(z, y, x, c) for y in range(NY) for x in range(NX)]
    for z in range(NZ)
    for c in range(NC)
]


def from_x(value, k):
    return lax.ppermute(
        value, AXES, [(device(z, y, x + k, c), device(z, y, x, c)) for z, y, x, c in PLACES]
    )


def from_y(value, k):
    return lax.ppermute(
        value, AXES, [(device(z, y + k, x, c), device(z, y, x, c)) for z, y, x, c in PLACES]
    )


def other_core(value):
    return lax.ppermute(
        value, AXES, [(device(z, y, x, 1 - c), device(z, y, x, c)) for z, y, x, c in PLACES]
    )


def mm(a, b):
    return jnp.dot(a, b, precision=HIGH, preferred_element_type=jnp.float32)


def nt(a, b):
    return lax.dot_general(
        a, b, (((1,), (1,)), ((), ())), precision=HIGH, preferred_element_type=jnp.float32
    )


def to_all(value, groups):
    size = len(groups[0])
    copies = jnp.broadcast_to(value[None], (size,) + value.shape)
    return lax.all_to_all(copies, AXES, 0, 0, axis_index_groups=groups, tiled=True)


def tile_kernel(rows, rhs, half, *refs):
    x_hbm, a_hbm, b_hbm = refs[0], refs[1:5], refs[5:9]
    k_ref, p_ref, tx_ref, ty_ref = refs[9:13]
    x_ref, a_ref, b_ref, cos_ref, sems = refs[13:]
    side = 4 * rows
    copies = []
    for i in range(4):
        at = pl.ds(i * side, side)
        copies.append(pltpu.make_async_copy(a_hbm[i], a_ref.at[at], sems.at[i]))
    x_copy = pltpu.make_async_copy(x_hbm, x_ref, sems.at[8])
    for i in range(4):
        at = pl.ds(i * side, side)
        copies.append(pltpu.make_async_copy(b_hbm[i], b_ref.at[at], sems.at[4 + i]))
    x_copy.start()
    for copy in copies:
        copy.start()
    x_copy.wait()
    for copy in copies[:4]:
        copy.wait()
    dims = (((1,), (1,)), ((), ()))
    k_ref[...] = lax.dot_general(
        a_ref[:, :half], x_ref[:, :half], dims, preferred_element_type=jnp.float32
    )
    for copy in copies[4:]:
        copy.wait()
    cos_ref[...] = lax.dot_general(
        b_ref[...], x_ref[:, half : 2 * half], dims, preferred_element_type=jnp.float32
    )
    for y in range(4):
        for x in range(4):
            at, other = pl.ds((4 * y + x) * rows, rows), pl.ds((4 * x + y) * rows, rows)
            k_ref[at, :] = jnp.exp(sharpness * (k_ref[at, :] + cos_ref[other, :] - 1.0))

    def targets(terms):
        terms = terms.astype(jnp.float32).T
        return terms[:rhs] + terms[rhs : 2 * rhs] + terms[2 * rhs : 3 * rhs]

    tx_ref[...] = targets(x_ref[:, 2 * half :])
    ty = targets(a_ref[:, half:])
    ty_ref[...] = ty
    p_ref[...] = mm(ty, k_ref[...])


def tile(rows, rhs, half, x, a, b):
    f32 = jnp.float32
    line, plane = x.shape[0], 16 * rows
    any_spec = pl.BlockSpec(memory_space=pl.ANY)
    vmem = pl.BlockSpec(memory_space=pltpu.VMEM)
    return pl.pallas_call(
        functools.partial(tile_kernel, rows, rhs, half),
        out_shape=(
            jax.ShapeDtypeStruct((plane, line), f32),
            jax.ShapeDtypeStruct((rhs, line), f32),
            jax.ShapeDtypeStruct((rhs, line), f32),
            jax.ShapeDtypeStruct((rhs, plane), f32),
        ),
        in_specs=[any_spec] * 9,
        out_specs=[vmem] * 4,
        scratch_shapes=[
            pltpu.VMEM((line, 2 * half + PAD), jnp.bfloat16),
            pltpu.VMEM((plane, half + PAD), jnp.bfloat16),
            pltpu.VMEM((plane, half), jnp.bfloat16),
            pltpu.VMEM((plane, line), f32),
            pltpu.SemaphoreType.DMA((9,)),
        ],
        compiler_params=pltpu.CompilerParams(vmem_limit_bytes=32 * 1024 * 1024),
        cost_estimate=pl.CostEstimate(
            flops=2 * plane * line * 2 * half,
            bytes_accessed=2 * (plane + line) * 2 * half,
            transcendentals=plane * line,
        ),
        name="tile",
    )(x, *a, *b)


def solve_small(matrix, rhs_block):
    matrix = 0.5 * (matrix + matrix.T)
    factor = jnp.linalg.cholesky(matrix)
    return jax.scipy.linalg.cho_solve((factor, True), rhs_block)


def local(sketches, targets):
    rows, rhs = targets.shape
    depth = sketches.shape[1]
    half = depth // 2
    line = NZ * rows
    z = lax.axis_index("row") // 4
    y = lax.axis_index("row") // 2 % 2 + 2 * (lax.axis_index("col") // NX)
    x = lax.axis_index("col") % NX
    bf16 = jnp.bfloat16

    scale = jnp.sqrt(jnp.sum(sketches * sketches, axis=1, keepdims=True) + 1e-06)
    units = (sketches / scale).astype(bf16)
    hi = targets.astype(bf16)
    rest = targets - hi.astype(jnp.float32)
    mid = rest.astype(bf16)
    low = (rest - mid.astype(jnp.float32)).astype(bf16)
    zero = jnp.zeros((rows, PAD - 3 * rhs), bf16)
    terms = jnp.concatenate([hi, mid, low, zero], axis=1)
    first = jnp.concatenate([units[:, :half], terms], axis=1)
    second = units[:, half:]

    mine = lax.all_gather(
        jnp.concatenate([units, terms], axis=1),
        AXES,
        axis=0,
        tiled=True,
        axis_index_groups=LINES,
    )
    a = jnp.concatenate([first] + [from_x(first, k) for k in range(1, NX)], axis=0)
    b = jnp.concatenate([second] + [from_y(second, k) for k in range(1, NY)], axis=0)
    a = [a] + [from_y(a, k) for k in range(1, NY)]
    b = [b] + [from_x(b, k) for k in range(1, NX)]
    theirs = other_core(mine)
    k_mine, p_mine, t_line, t_plane = tile(rows, rhs, half, mine, a, b)
    k_theirs, p_theirs, t_far, _ = tile(rows, rhs, half, theirs, a, b)

    n0 = nt(t_plane, t_plane)
    part = jnp.concatenate([p_mine, n0], axis=1)
    part = part + other_core(jnp.concatenate([p_theirs, n0], axis=1))
    part = jnp.sum(to_all(part, LINES), axis=0)
    w_line = part[:, :line] - t_line
    n0 = part[:, line:]

    n12 = jnp.concatenate([nt(t_line, w_line), nt(w_line, w_line)], axis=1)
    far = other_core(jnp.concatenate([w_line, n12], axis=1))
    w_far = far[:, :line]
    n12 = n12 + far[:, line:]
    w_own = lax.dynamic_slice(w_line, (0, z * rows), (rhs, rows))
    t_own = targets.T
    got = to_all(jnp.concatenate([w_own, n12], axis=1), PLANES)
    w_plane = got[:, :, :rows].reshape(NY, NX, rhs, rows)
    w_plane = lax.dynamic_slice_in_dim(jnp.concatenate([w_plane] * 2, axis=0), y, NY, 0)
    w_plane = lax.dynamic_slice_in_dim(jnp.concatenate([w_plane] * 2, axis=1), x, NX, 1)
    w_plane = w_plane.transpose(2, 0, 1, 3).reshape(rhs, -1)
    n12 = jnp.sum(got[:, :, rows:], axis=0)
    n1, n2 = n12[:, :rhs], n12[:, rhs:]

    eye = jnp.eye(rhs, dtype=jnp.float32)
    a1 = solve_small(n1 + 2.0 * n0, n0)
    q = eye - 2.0 * a1
    cross = mm(q.T, mm(n1, a1))
    rr1 = mm(q.T, mm(n0, q)) - cross - cross.T + mm(a1.T, mm(n2, a1))
    mix = (q + solve_small(n0, rr1)).T

    def direction(t, w):
        return mm(mix, t) - mm(a1.T, w)

    d_plane = direction(t_plane, w_plane)
    d_own = direction(t_own, w_own)
    near2 = mm(d_plane, k_mine)
    far2 = mm(d_plane, k_theirs)
    curve = nt(direction(t_line, w_line), near2) + nt(direction(t_far, w_far), far2)
    curve = curve + nt(d_own, d_own)
    sent = other_core(jnp.concatenate([far2, curve], axis=1))
    near2 = near2 + sent[:, :line]
    curve = curve + sent[:, line:]
    chunks = near2.reshape(rhs, NZ, rows).transpose(1, 0, 2)
    chunks = jnp.concatenate(
        [chunks, jnp.broadcast_to(curve[None], (NZ, rhs, rhs))], axis=2
    )
    chunks = jnp.sum(
        lax.all_to_all(chunks, AXES, 0, 0, axis_index_groups=LINES, tiled=True), axis=0
    )
    image = chunks[:, :rows] + d_own
    curve = jnp.sum(to_all(chunks[:, rows:], PLANES), axis=0)
    a2 = solve_small(curve, rr1)
    weights = mm(a1.T, t_own) + mm(a2.T, d_own)
    residual = mm(q.T, t_own) - mm(a1.T, w_own) - mm(a2.T, image)
    return weights.T, residual.T


def solution(mesh):
    in_specs = (P(AXES, None), P(AXES, None))
    out_specs = (P(AXES, None), P(AXES, None))
    return jax.shard_map(local, mesh=mesh, in_specs=in_specs, out_specs=out_specs, check_vma=False)
```

time: 231 us -> 263 us (1.14)
  waiting for transfers between devices: 102 us -> 158 us
  blocking collectives: 14 us -> 0 us
  Pallas kernels: 0 us -> 12.1 us
  matrix products: 20.8 us -> 8.75 us
  starting transfers between devices: 40.4 us -> 33.6 us
  local copies, waits for them, and re-layouts: 10.8 us -> 7.93 us
    ppermute x4 -> x16, waiting for transfers between devices: 0.63 us -> 75.5 us  [the longest x6 48.7 us: from_x(): lax.ppermute(value, AXES, [(device(z, y, x + k, c), device(z, y, x, c)) f...]
    all_to_all x5 -> x3, waiting for transfers between devices: 73.8 us -> 29.7 us  [to_all(): lax.all_to_all(copies, AXES, 0, 0, axis_index_groups=groups, tiled=True)]
    all_gather x1, waiting for transfers between devices: 19.7 us -> 44.3 us  [local(): lax.all_gather(jnp.concatenate([units, terms], axis=1), AXES, axis=0, til...]
    all_to_all x5 -> x3, starting transfers between devices: 28.1 us -> 10.9 us  [to_all(): lax.all_to_all(copies, AXES, 0, 0, axis_index_groups=groups, tiled=True)]
    all_to_all x1 -> x0, blocking collectives: 14 us -> none  [to_all(): lax.all_to_all(copies, AXES, 0, 0, axis_index_groups=groups, tiled=True)]
    pallas_call x0 -> x2, Pallas kernels: none -> 12.1 us  [tile(): pl.pallas_call(functools.partial(tile_kernel, rows, rhs, half), out_shape...]
    dot_general x26, matrix products: 19.7 us -> 7.65 us  [the longest x20 6.57 us: mm(): return jnp.dot(a, b, precision=HIGH, preferred_element_type=jnp.float32)]
    ppermute x4 -> x16, starting transfers between devices: 8.88 us -> 19.4 us  [the longest x6 8.52 us: from_x(): lax.ppermute(value, AXES, [(device(z, y, x + k, c), device(z, y, x, c)) f...]
  transfers between devices with their start and end apart: 11 -> 21, of which waited for: 9 -> 17; matrix products, arithmetic and copies ran while one was open for 12% -> 1% of each run, Pallas kernels for 0% -> 2%
where the time goes in v2:
time: 263 us; the launch traced here: 262 us
  waiting for transfers between devices  158 us (60%)
  starting transfers between devices  33.6 us (13%)
  other arithmetic  27.2 us (10%)
  between operations  14.6 us (6%)
  Pallas kernels  12.1 us (5%)
  matrix products  8.75 us (3%)
  local copies, waits for them, and re-layouts  7.93 us (3%)
    ppermute x6, waiting for transfers between devices, from_x(): lax.ppermute(value, AXES, [(device(z, y, x + k, c), device(z, y, x, c)) f...  48.7 us
    all_gather x1, waiting for transfers between devices, local(): lax.all_gather(jnp.concatenate([units, terms], axis=1), AXES, axis=0, til...  44.3 us
    all_to_all x3, waiting for transfers between devices, to_all(): lax.all_to_all(copies, AXES, 0, 0, axis_index_groups=groups, tiled=True)  29.7 us
    ppermute x6, waiting for transfers between devices, from_y(): lax.ppermute(value, AXES, [(device(z, y + k, x, c), device(z, y, x, c)) f...  24.2 us
    pallas_call x2, Pallas kernels, tile(): pl.pallas_call(functools.partial(tile_kernel, rows, rhs, half), out_shape...  12.1 us
    all_to_all x3, starting transfers between devices, to_all(): lax.all_to_all(copies, AXES, 0, 0, axis_index_groups=groups, tiled=True)  10.9 us
    another operation x9, other arithmetic, solve_small(): factor = jnp.linalg.cholesky(matrix)  10.8 us
    another operation x6, other arithmetic, solve_small(): return jax.scipy.linalg.cho_solve((factor, True), rhs_block)  9.26 us
  transfers between devices with their start and end apart: 21, of which 17 were waited for; matrix products, arithmetic and copies ran while one was open for 1% of the time, Pallas kernels for 2%

profile of v2, /device:TPU:1, one launch (start us, length us, event | category | flops | bytes accessed | tf_op | source)
XLA Modules:
  0.0 261.8 jit_solution(10792853283965166972)
XLA Ops:
  7.2 0.7 convert_element_type.22
  7.9 0.8 copy.55
  8.8 1.2 multiply_reduce_fusion
  10.1 1.2 divide_convert_fusion
  11.3 0.8 concatenate.43
  12.2 44.3 %all-gather.2.cloned.1.call-done.refs_0_ = bf16[320,4224]{1,0:T(8,128)(2,1)} async-done(((bf16[40,4224]{1,0:T(8,128)(2,1)}), bf16[320,4224]{1,0:T(8,128)(2,1)}) %all-gather.2.cloned.1.call-update) | async-done | bytes 2703376 | tf_op jit(solution)/shard_map/all_gather | solution.py:174
  56.5 3.1 %collective-permute-start.12 = (bf16[320,4224]{1,0:T(8,128)(2,1)}, bf16[320,4224]{1,0:T(8,128)(2,1)}, u32[]{:S(2)}, u32[]{:S(2)}) collective-permute-start(bf16[320,4224]{1,0:T(8,128)(2,1)} %all-gather.2.cloned.1.call-done.refs_0_), channel_id=1, source_target_pairs={{8,0},{0,8},{9,1},{1,9},{10,2},{2,10},{11,3},{3,11},{24,16},{16,24... | collective-permute-start | bytes 8110088 | tf_op jit(solution)/shard_map/ppermute | solution.py:51
  59.6 2.5 collective-permute-start.6
  62.2 0.5 collective-permute-start.7
  62.7 0.6 collective-permute-start.8
  63.3 1.0 concatenate.44
  64.3 2.5 collective-permute-start
  66.8 2.4 collective-permute-done.6
  69.2 4.2 %collective-permute-done.8 = bf16[40,2048]{1,0:T(8,128)(2,1)} collective-permute-done((bf16[40,2048]{1,0:T(8,128)(2,1)S(1)}, bf16[40,2048]{1,0:T(8,128)(2,1)}, u32[]{:S(2)}, u32[]{:S(2)}) %collective-permute-start.8) | collective-permute-done | bytes 163872 | tf_op jit(solution)/shard_map/ppermute | solution.py:45
  73.4 1.0 pad_maximum_fusion.1.refs_5_
  74.4 2.8 %collective-permute-start.10 = (bf16[160,2048]{1,0:T(8,128)(2,1)S(1)}, bf16[160,2048]{1,0:T(8,128)(2,1)S(1)}, u32[]{:S(2)}, u32[]{:S(2)}) collective-permute-start(bf16[160,2048]{1,0:T(8,128)(2,1)S(1)} %pad_maximum_fusion.1.refs_5_), channel_id=1, source_target_pairs={{2,0},{10,8},{3,1},{11,9},{0,2},{8,10},{1,3},{9,11},{18,16},{26,24... | collective-permute-start | bytes 1966088 | tf_op jit(solution)/shard_map/ppermute | solution.py:39
  77.4 1.8 collective-permute-start.1
  79.2 1.2 collective-permute-start.2
  80.4 29.2 %collective-permute-done.1 = bf16[40,2176]{1,0:T(8,128)(2,1)S(1)} collective-permute-done((bf16[40,2176]{1,0:T(8,128)(2,1)S(1)}, bf16[40,2176]{1,0:T(8,128)(2,1)S(1)}, u32[]{:S(2)}, u32[]{:S(2)}) %collective-permute-start.1) | collective-permute-done | bytes 174112 | tf_op jit(solution)/shard_map/ppermute | solution.py:39
  109.6 4.5 %collective-permute-done.2 = bf16[40,2176]{1,0:T(8,128)(2,1)S(1)} collective-permute-done((bf16[40,2176]{1,0:T(8,128)(2,1)S(1)}, bf16[40,2176]{1,0:T(8,128)(2,1)S(1)}, u32[]{:S(2)}, u32[]{:S(2)}) %collective-permute-start.2) | collective-permute-done | bytes 174112 | tf_op jit(solution)/shard_map/ppermute | solution.py:39
  114.3 0.6 collective-permute-start.4
  114.9 0.8 collective-permute-start.5
  115.7 15.0 %collective-permute-done.9.refs_6_ = bf16[160,2048]{1,0:T(8,128)(2,1)S(1)} collective-permute-done((bf16[160,2048]{1,0:T(8,128)(2,1)S(1)}, bf16[160,2048]{1,0:T(8,128)(2,1)S(1)}, u32[]{:S(2)}, u32[]{:S(2)}) %collective-permute-start.9) | collective-permute-done | bytes 655392 | tf_op jit(solution)/shard_map/ppermute | solution.py:39
  130.9 1.6 collective-permute-done.4.refs_3_
  132.6 15.7 %collective-permute-done.5.refs_4_ = bf16[160,2176]{1,0:T(8,128)(2,1)S(1)} collective-permute-done((bf16[160,2176]{1,0:T(8,128)(2,1)S(1)}, bf16[160,2176]{1,0:T(8,128)(2,1)S(1)}, u32[]{:S(2)}, u32[]{:S(2)}) %collective-permute-start.5) | collective-permute-done | bytes 696352 | tf_op jit(solution)/shard_map/ppermute | solution.py:45
  148.3 6.1 %tile.2 = (f32[640,320]{1,0:T(8,128)S(1)}, f32[32,320]{1,0:T(8,128)S(1)}, f32[32,320]{1,0:T(8,128)S(1)}, f32[32,640]{1,0:T(8,128)S(1)}) custom-call(bf16[320,4224]{1,0:T(8,128)(2,1)S(1)} %copy-done, bf16[160,2176]{1,0:T(8,128)(2,1)S(1)} %pad_maximum_fusion.refs_1_, bf16[160,2176]{1,0:T(8,128)(2,1)S(1)} %collective-permute-done.3.refs_2_, ...), custom_call_target="tpu_custom_call" | custom-call | flops 1677721600 | bytes 7864320 | tf_op jit(solution)/shard_map/tile/pallas_call | solution.py:120
  154.4 1.0 copy-done.1
  155.6 6.0 %tile.3 = (f32[640,320]{1,0:T(8,128)S(1)}, f32[32,320]{1,0:T(8,128)S(1)}, f32[32,320]{1,0:T(8,128)S(1)}, f32[32,640]{1,0:T(8,128)}) custom-call(bf16[320,4224]{1,0:T(8,128)(2,1)} %collective-permute-done.12.refs_0_, bf16[160,2176]{1,0:T(8,128)(2,1)S(1)} %pad_maximum_fusion.refs_1_, bf16[160,2176]{1,0:T(8,128)(2,1)S(1)} %collective-permute-done.3.refs_2_, ...), custom_call_target="tpu_custom_call" | custom-call | flops 1677721600 | bytes 7864320 | tf_op jit(solution)/shard_map/tile/pallas_call | solution.py:120
  161.7 0.5 collective-permute-start.13
  162.2 0.9 collective-permute-done.13
  163.2 0.8 broadcast_in_dim.12
  164.0 3.8 %all-to-all-start = ((f32[8,32,352]{2,1,0:T(8,128)}), f32[8,32,352]{2,1,0:T(8,128)S(1)}, u32[]{:S(2)}, u32[]{:S(2)}) async-start(f32[8,32,352]{2,1,0:T(8,128)} %broadcast_in_dim.12), calls=%async_computation | async-start | bytes 786432 | tf_op jit(solution)/shard_map/all_to_all | solution.py:69
  167.8 15.1 %all-to-all-done = f32[8,32,352]{2,1,0:T(8,128)S(1)} async-done(((f32[8,32,352]{2,1,0:T(8,128)}), f32[8,32,352]{2,1,0:T(8,128)S(1)}, u32[]{:S(2)}, u32[]{:S(2)}) %all-to-all-start) | async-done | bytes 360480 | tf_op jit(solution)/shard_map/all_to_all | solution.py:69
  183.5 0.5 collective-permute-start.14
  184.1 0.8 collective-permute-done.14
  185.0 0.7 broadcast_in_dim.13
  185.7 3.5 %all-to-all-start.1 = ((f32[16,32,104]{2,1,0:T(8,128)}), f32[16,32,104]{2,1,0:T(8,128)S(1)}, u32[]{:S(2)}, u32[]{:S(2)}) async-start(f32[16,32,104]{2,1,0:T(8,128)} %broadcast_in_dim.13), calls=%async_computation.1 | async-start | bytes 524288 | tf_op jit(solution)/shard_map/all_to_all | solution.py:69
  189.3 8.4 %all-to-all-done.1 = f32[16,32,104]{2,1,0:T(8,128)S(1)} async-done(((f32[16,32,104]{2,1,0:T(8,128)}), f32[16,32,104]{2,1,0:T(8,128)S(1)}, u32[]{:S(2)}, u32[]{:S(2)}) %all-to-all-start.1) | async-done | bytes 213024 | tf_op jit(solution)/shard_map/all_to_all | solution.py:69
  198.2 2.9 %cholesky.59 = f32[32,32]{1,0:T(8,128)S(1)} custom-call(f32[32,32]{1,0:T(8,128)S(1)} %copy.61), custom_call_target="Cholesky" | custom-call | tf_op jit(solution)/shard_map/jit(cholesky)/cholesky | solution.py:149
  201.1 0.6 compare_reduce_fusion.2
  201.8 0.7 fusion.8
  202.4 2.4 custom-call.9
  207.7 2.9 %cholesky.70 = f32[32,32]{1,0:T(8,128)S(1)} custom-call(f32[32,32]{1,0:T(8,128)S(1)} %fusion.22), custom_call_target="Cholesky" | custom-call | tf_op jit(solution)/shard_map/jit(cholesky)/cholesky | solution.py:149
  210.6 0.6 compare_reduce_fusion.1
  211.3 0.7 fusion.9
  211.9 2.4 custom-call.10
  215.8 0.6 fusion.55
  216.4 0.6 fusion.54
  218.7 1.4 collective-permute-start.15
  220.1 0.9 collective-permute-done.15
  221.2 0.7 pad_maximum_fusion.2
  222.0 3.4 %all-to-all-start.2 = ((f32[8,32,72]{2,1,0:T(8,128)}), f32[8,32,72]{2,1,0:T(8,128)S(1)}, u32[]{:S(2)}, u32[]{:S(2)}) async-start(f32[8,32,72]{2,1,0:T(8,128)} %pad_maximum_fusion.2), calls=%async_computation.2 | async-start | bytes 262144 | tf_op jit(solution)/shard_map/all_to_all | solution.py:234
  225.6 8.1 %all-to-all-done.2 = f32[8,32,72]{2,1,0:T(8,128)S(1)} async-done(((f32[8,32,72]{2,1,0:T(8,128)}), f32[8,32,72]{2,1,0:T(8,128)S(1)}, u32[]{:S(2)}, u32[]{:S(2)}) %all-to-all-start.2) | async-done | bytes 73760 | tf_op jit(solution)/shard_map/all_to_all | solution.py:234
  233.8 0.8 reshape.36
  234.6 3.5 %all-to-all-start.3 = ((f32[16,1,1024]{2,1,0:T(1,128)}), f32[16,1,1024]{2,1,0:T(1,128)S(1)}, u32[]{:S(2)}, u32[]{:S(2)}) async-start(f32[16,1,1024]{2,1,0:T(1,128)} %reshape.36), calls=%async_computation.3 | async-start | bytes 131072 | tf_op jit(solution)/shard_map/all_to_all | solution.py:69
  238.3 6.2 %all-to-all-done.3 = f32[16,1,1024]{2,1,0:T(1,128)S(1)} async-done(((f32[16,1,1024]{2,1,0:T(1,128)}), f32[16,1,1024]{2,1,0:T(1,128)S(1)}, u32[]{:S(2)}, u32[]{:S(2)}) %all-to-all-start.3) | async-done | bytes 65568 | tf_op jit(solution)/shard_map/all_to_all | solution.py:69
  244.5 0.5 broadcast.81
  245.1 0.8 reduce.4
  246.2 2.9 %cholesky.81 = f32[32,32]{1,0:T(8,128)S(1)} custom-call(f32[32,32]{1,0:T(8,128)S(1)} %fusion.17), custom_call_target="Cholesky" | custom-call | tf_op jit(solution)/shard_map/jit(cholesky)/cholesky | solution.py:149
  249.1 0.6 compare_reduce_fusion
  249.8 0.7 fusion.10
  250.4 2.4 custom-call.11
  253.2 0.8 convolution_subtract_fusion.3
  254.1 0.8 convolution_add_fusion
  (100 shorter events, 9.6 us)
Async XLA Ops:
  7.2 49.3 %all-gather.2.cloned.1.call-start = ((), (), s32[]{:S(2)}) async-start(), calls=%async_computation.4 | async-start | bytes 3041280 | tf_op jit(solution)/shard_map/all_gather | solution.py:174
  11.3 52.0 %copy-start.5 = (bf16[40,32]{1,0:T(8,128)(2,1)}, bf16[40,32]{1,0:T(8,128)(2,1)S(1)}, u32[]{:S(2)}) copy-start(bf16[40,32]{1,0:T(8,128)(2,1)S(1)} %get-tuple-element.22) | copy-start | bytes 7684
  11.3 52.0 %copy-start.6 = (bf16[40,32]{1,0:T(8,128)(2,1)}, bf16[40,32]{1,0:T(8,128)(2,1)S(1)}, u32[]{:S(2)}) copy-start(bf16[40,32]{1,0:T(8,128)(2,1)S(1)} %get-tuple-element.23) | copy-start | bytes 7684
  11.3 52.0 %copy-start.4 = (bf16[40,32]{1,0:T(8,128)(2,1)}, bf16[40,32]{1,0:T(8,128)(2,1)S(1)}, u32[]{:S(2)}) copy-start(bf16[40,32]{1,0:T(8,128)(2,1)S(1)} %broadcast_in_dim.10) | copy-start | bytes 7684
  56.5 99.2 %collective-permute-start.12 = (bf16[320,4224]{1,0:T(8,128)(2,1)}, bf16[320,4224]{1,0:T(8,128)(2,1)}, u32[]{:S(2)}, u32[]{:S(2)}) collective-permute-start(bf16[320,4224]{1,0:T(8,128)(2,1)} %all-gather.2.cloned.1.call-done.refs_0_), channel_id=1, source_target_pairs={{8,0},{0,8},{9,1},{1,9},{10,2},{2,10},{11,3},{3,11},{24,16},{16,24... | collective-permute-start | bytes 8110088 | tf_op jit(solution)/shard_map/ppermute | solution.py:51
  59.6 9.5 %collective-permute-start.6 = (bf16[40,2048]{1,0:T(8,128)(2,1)S(1)}, bf16[40,2048]{1,0:T(8,128)(2,1)S(1)}, u32[]{:S(2)}, u32[]{:S(2)}) collective-permute-start(bf16[40,2048]{1,0:T(8,128)(2,1)S(1)} %get-tuple-element.18), channel_id=1, source_target_pairs={{16,0},{24,8},{17,1},{25,9},{18,2},{26,10},{19,3},{27,11},{4,16},{... | collective-permute-start | bytes 491528 | tf_op jit(solution)/shard_map/ppermute | solution.py:45
  62.2 7.1 %collective-permute-start.7 = (bf16[40,2048]{1,0:T(8,128)(2,1)S(1)}, bf16[40,2048]{1,0:T(8,128)(2,1)S(1)}, u32[]{:S(2)}, u32[]{:S(2)}) collective-permute-start(bf16[40,2048]{1,0:T(8,128)(2,1)S(1)} %get-tuple-element.18), channel_id=1, source_target_pairs={{4,0},{12,8},{5,1},{13,9},{6,2},{14,10},{7,3},{15,11},{20,16},{28,... | collective-permute-start | bytes 491528 | tf_op jit(solution)/shard_map/ppermute | solution.py:45
  62.7 10.7 %collective-permute-start.8 = (bf16[40,2048]{1,0:T(8,128)(2,1)S(1)}, bf16[40,2048]{1,0:T(8,128)(2,1)}, u32[]{:S(2)}, u32[]{:S(2)}) collective-permute-start(bf16[40,2048]{1,0:T(8,128)(2,1)S(1)} %get-tuple-element.18), channel_id=1, source_target_pairs={{20,0},{28,8},{21,1},{29,9},{22,2},{30,10},{23,3},{31,11},{0,16},{... | collective-permute-start | bytes 491528 | tf_op jit(solution)/shard_map/ppermute | solution.py:45
  63.3 85.0 %copy-start = (bf16[320,4224]{1,0:T(8,128)(2,1)S(1)}, bf16[320,4224]{1,0:T(8,128)(2,1)}, u32[]{:S(2)}) copy-start(bf16[320,4224]{1,0:T(8,128)(2,1)} %all-gather.2.cloned.1.call-done.refs_0_) | copy-start | bytes 8110084
  64.3 14.9 %collective-permute-start = (bf16[40,2176]{1,0:T(8,128)(2,1)S(1)}, bf16[40,2176]{1,0:T(8,128)(2,1)S(1)}, u32[]{:S(2)}, u32[]{:S(2)}) collective-permute-start(bf16[40,2176]{1,0:T(8,128)(2,1)S(1)} %concatenate.44), channel_id=1, source_target_pairs={{1,0},{9,8},{2,1},{10,9},{3,2},{11,10},{0,3},{8,11},{17,16},{25,24... | collective-permute-start | bytes 522248 | tf_op jit(solution)/shard_map/ppermute | solution.py:39
  74.4 40.5 %collective-permute-start.10 = (bf16[160,2048]{1,0:T(8,128)(2,1)S(1)}, bf16[160,2048]{1,0:T(8,128)(2,1)S(1)}, u32[]{:S(2)}, u32[]{:S(2)}) collective-permute-start(bf16[160,2048]{1,0:T(8,128)(2,1)S(1)} %pad_maximum_fusion.1.refs_5_), channel_id=1, source_target_pairs={{2,0},{10,8},{3,1},{11,9},{0,2},{8,10},{1,3},{9,11},{18,16},{26,24... | collective-permute-start | bytes 1966088 | tf_op jit(solution)/shard_map/ppermute | solution.py:39
  77.2 38.6 %collective-permute-start.11 = (bf16[160,2048]{1,0:T(8,128)(2,1)S(1)}, bf16[160,2048]{1,0:T(8,128)(2,1)S(1)}, u32[]{:S(2)}, u32[]{:S(2)}) collective-permute-start(bf16[160,2048]{1,0:T(8,128)(2,1)S(1)} %pad_maximum_fusion.1.refs_5_), channel_id=1, source_target_pairs={{3,0},{11,8},{0,1},{8,9},{1,2},{9,10},{2,3},{10,11},{19,16},{27,24... | collective-permute-start | bytes 1966088 | tf_op jit(solution)/shard_map/ppermute | solution.py:39
  77.4 32.2 %collective-permute-start.1 = (bf16[40,2176]{1,0:T(8,128)(2,1)S(1)}, bf16[40,2176]{1,0:T(8,128)(2,1)S(1)}, u32[]{:S(2)}, u32[]{:S(2)}) collective-permute-start(bf16[40,2176]{1,0:T(8,128)(2,1)S(1)} %concatenate.44), channel_id=1, source_target_pairs={{2,0},{10,8},{3,1},{11,9},{0,2},{8,10},{1,3},{9,11},{18,16},{26,24... | collective-permute-start | bytes 522248 | tf_op jit(solution)/shard_map/ppermute | solution.py:39
  79.2 34.9 %collective-permute-start.2 = (bf16[40,2176]{1,0:T(8,128)(2,1)S(1)}, bf16[40,2176]{1,0:T(8,128)(2,1)S(1)}, u32[]{:S(2)}, u32[]{:S(2)}) collective-permute-start(bf16[40,2176]{1,0:T(8,128)(2,1)S(1)} %concatenate.44), channel_id=1, source_target_pairs={{3,0},{11,8},{0,1},{8,9},{1,2},{9,10},{2,3},{10,11},{19,16},{27,24... | collective-permute-start | bytes 522248 | tf_op jit(solution)/shard_map/ppermute | solution.py:39
  114.2 16.8 %collective-permute-start.3 = (bf16[160,2176]{1,0:T(8,128)(2,1)S(1)}, bf16[160,2176]{1,0:T(8,128)(2,1)S(1)}, u32[]{:S(2)}, u32[]{:S(2)}) collective-permute-start(bf16[160,2176]{1,0:T(8,128)(2,1)S(1)} %pad_maximum_fusion.refs_1_), channel_id=1, source_target_pairs={{16,0},{24,8},{17,1},{25,9},{18,2},{26,10},{19,3},{27,11},{4,16},{... | collective-permute-start | bytes 2088968 | tf_op jit(solution)/shard_map/ppermute | solution.py:45
  114.3 18.3 %collective-permute-start.4 = (bf16[160,2176]{1,0:T(8,128)(2,1)S(1)}, bf16[160,2176]{1,0:T(8,128)(2,1)S(1)}, u32[]{:S(2)}, u32[]{:S(2)}) collective-permute-start(bf16[160,2176]{1,0:T(8,128)(2,1)S(1)} %pad_maximum_fusion.refs_1_), channel_id=1, source_target_pairs={{4,0},{12,8},{5,1},{13,9},{6,2},{14,10},{7,3},{15,11},{20,16},{28,... | collective-permute-start | bytes 2088968 | tf_op jit(solution)/shard_map/ppermute | solution.py:45
  114.9 33.4 %collective-permute-start.5 = (bf16[160,2176]{1,0:T(8,128)(2,1)S(1)}, bf16[160,2176]{1,0:T(8,128)(2,1)S(1)}, u32[]{:S(2)}, u32[]{:S(2)}) collective-permute-start(bf16[160,2176]{1,0:T(8,128)(2,1)S(1)} %pad_maximum_fusion.refs_1_), channel_id=1, source_target_pairs={{20,0},{28,8},{21,1},{29,9},{22,2},{30,10},{23,3},{31,11},{0,16},{... | collective-permute-start | bytes 2088968 | tf_op jit(solution)/shard_map/ppermute | solution.py:45
  115.7 15.0 %collective-permute-start.9 = (bf16[160,2048]{1,0:T(8,128)(2,1)S(1)}, bf16[160,2048]{1,0:T(8,128)(2,1)S(1)}, u32[]{:S(2)}, u32[]{:S(2)}) collective-permute-start(bf16[160,2048]{1,0:T(8,128)(2,1)S(1)} %pad_maximum_fusion.1.refs_5_), channel_id=1, source_target_pairs={{1,0},{9,8},{2,1},{10,9},{3,2},{11,10},{0,3},{8,11},{17,16},{25,24... | collective-permute-start | bytes 1966088 | tf_op jit(solution)/shard_map/ppermute | solution.py:39
  154.4 1.0 copy-start.1
  161.7 1.4 collective-permute-start.13
  164.0 19.0 %all-to-all-start = ((f32[8,32,352]{2,1,0:T(8,128)}), f32[8,32,352]{2,1,0:T(8,128)S(1)}, u32[]{:S(2)}, u32[]{:S(2)}) async-start(f32[8,32,352]{2,1,0:T(8,128)} %broadcast_in_dim.12), calls=%async_computation | async-start | bytes 786432 | tf_op jit(solution)/shard_map/all_to_all | solution.py:69
  183.5 1.4 collective-permute-start.14
  185.7 12.0 %all-to-all-start.1 = ((f32[16,32,104]{2,1,0:T(8,128)}), f32[16,32,104]{2,1,0:T(8,128)S(1)}, u32[]{:S(2)}, u32[]{:S(2)}) async-start(f32[16,32,104]{2,1,0:T(8,128)} %broadcast_in_dim.13), calls=%async_computation.1 | async-start | bytes 524288 | tf_op jit(solution)/shard_map/all_to_all | solution.py:69
  206.6 9.8 %copy-start.2 = (f32[640,320]{1,0:T(8,128)S(1)}, f32[640,320]{1,0:T(8,128)}, u32[]{:S(2)}) copy-start(f32[640,320]{1,0:T(8,128)} %copy-done.1) | copy-start | bytes 2457604
  215.1 2.2 copy-start.3
  218.7 2.3 collective-permute-start.15
  222.0 11.7 %all-to-all-start.2 = ((f32[8,32,72]{2,1,0:T(8,128)}), f32[8,32,72]{2,1,0:T(8,128)S(1)}, u32[]{:S(2)}, u32[]{:S(2)}) async-start(f32[8,32,72]{2,1,0:T(8,128)} %pad_maximum_fusion.2), calls=%async_computation.2 | async-start | bytes 262144 | tf_op jit(solution)/shard_map/all_to_all | solution.py:234
  234.6 9.9 %all-to-all-start.3 = ((f32[16,1,1024]{2,1,0:T(1,128)}), f32[16,1,1024]{2,1,0:T(1,128)S(1)}, u32[]{:S(2)}, u32[]{:S(2)}) async-start(f32[16,1,1024]{2,1,0:T(1,128)} %reshape.36), calls=%async_computation.3 | async-start | bytes 131072 | tf_op jit(solution)/shard_map/all_to_all | solution.py:69
Sparse Core Ops, SparseCore 0:
  12.3 44.0 all-gather.1

commit v3 on v2

v3 whole, which is shorter than its diff:
```python
import functools

import jax
import jax.numpy as jnp
from jax import lax
from jax.experimental import pallas as pl
from jax.experimental.pallas import tpu as pltpu
from jax.sharding import PartitionSpec as P

sharpness = 4.0
AXES = ("row", "col")
NZ, NY, NX, NC = 8, 4, 4, 2
HIGH = lax.Precision.HIGHEST
PAD = 128
VMEM = 48 * 1024 * 1024


def device(z, y, x, c):
    z, y, x = z % NZ, y % NY, x % NX
    return ((z * 2 + y % 2) * 2 + c) * 8 + (y // 2) * 4 + x


PLACES = [
    (z, y, x, c) for z in range(NZ) for y in range(NY) for x in range(NX) for c in range(NC)
]
LINES = [
    [device(z, y, x, c) for z in range(NZ)]
    for y in range(NY)
    for x in range(NX)
    for c in range(NC)
]
PLANES = [
    [device(z, y, x, c) for y in range(NY) for x in range(NX)]
    for z in range(NZ)
    for c in range(NC)
]


def from_x(value, k):
    return lax.ppermute(
        value, AXES, [(device(z, y, x + k, c), device(z, y, x, c)) for z, y, x, c in PLACES]
    )


def from_y(value, k):
    return lax.ppermute(
        value, AXES, [(device(z, y + k, x, c), device(z, y, x, c)) for z, y, x, c in PLACES]
    )


def other_core(value):
    return lax.ppermute(
        value, AXES, [(device(z, y, x, 1 - c), device(z, y, x, c)) for z, y, x, c in PLACES]
    )


def mm(a, b):
    return jnp.dot(a, b, precision=HIGH, preferred_element_type=jnp.float32)


def nt(a, b):
    return lax.dot_general(
        a, b, (((1,), (1,)), ((), ())), precision=HIGH, preferred_element_type=jnp.float32
    )


def to_all(value, groups):
    size = len(groups[0])
    copies = jnp.broadcast_to(value[None], (size,) + value.shape)
    return lax.all_to_all(copies, AXES, 0, 0, axis_index_groups=groups, tiled=True)


def tile_kernel(rows, rhs, half, *refs):
    x_hbm, a_hbm, b_hbm = refs[0:2], refs[2:6], refs[6:10]
    k_refs, p_refs, t_refs, ty_ref = refs[10:12], refs[12:14], refs[14:16], refs[16]
    x_ref, a_ref, b_ref, cos_ref, sems = refs[17:]
    side, line = 4 * rows, 8 * rows
    x_copies = [
        pltpu.make_async_copy(x_hbm[i], x_ref.at[pl.ds(i * line, line)], sems.at[i])
        for i in range(2)
    ]
    a_copies = [
        pltpu.make_async_copy(a_hbm[i], a_ref.at[pl.ds(i * side, side)], sems.at[2 + i])
        for i in range(4)
    ]
    b_copies = [
        pltpu.make_async_copy(b_hbm[i], b_ref.at[pl.ds(i * side, side)], sems.at[6 + i])
        for i in range(4)
    ]
    for copy in [x_copies[0]] + a_copies + b_copies + [x_copies[1]]:
        copy.start()

    def targets(terms):
        terms = terms.astype(jnp.float32).T
        return terms[:rhs] + terms[rhs : 2 * rhs] + terms[2 * rhs : 3 * rhs]

    dims = (((1,), (1,)), ((), ()))
    for i in range(2):
        at = pl.ds(i * line, line)
        k_ref = k_refs[i]
        x_copies[i].wait()
        if i == 0:
            for copy in a_copies:
                copy.wait()
            ty_ref[...] = targets(a_ref[:, half:])
        k_ref[...] = lax.dot_general(
            a_ref[:, :half], x_ref[at, :half], dims, preferred_element_type=jnp.float32
        )
        if i == 0:
            for copy in b_copies:
                copy.wait()
        cos_ref[...] = lax.dot_general(
            b_ref[...], x_ref[at, half : 2 * half], dims, preferred_element_type=jnp.float32
        )
        for y in range(4):
            for x in range(4):
                to, of = pl.ds((4 * y + x) * rows, rows), pl.ds((4 * x + y) * rows, rows)
                k_ref[to, :] = jnp.exp(sharpness * (k_ref[to, :] + cos_ref[of, :] - 1.0))
        t_refs[i][...] = targets(x_ref[at, 2 * half :])
        p_refs[i][...] = mm(ty_ref[...], k_ref[...])


def tile(rows, rhs, half, xs, a, b):
    f32 = jnp.float32
    line, plane = xs[0].shape[0], 16 * rows
    hbm = pl.BlockSpec(memory_space=pltpu.HBM)
    vmem = pl.BlockSpec(memory_space=pltpu.VMEM)
    return pl.pallas_call(
        functools.partial(tile_kernel, rows, rhs, half),
        out_shape=(jax.ShapeDtypeStruct((plane, line), f32),) * 2
        + (jax.ShapeDtypeStruct((rhs, line), f32),) * 4
        + (jax.ShapeDtypeStruct((rhs, plane), f32),),
        in_specs=[hbm] * 10,
        out_specs=[vmem] * 7,
        scratch_shapes=[
            pltpu.VMEM((2 * line, 2 * half + PAD), jnp.bfloat16),
            pltpu.VMEM((plane, half + PAD), jnp.bfloat16),
            pltpu.VMEM((plane, half), jnp.bfloat16),
            pltpu.VMEM((plane, line), f32),
            pltpu.SemaphoreType.DMA((10,)),
        ],
        compiler_params=pltpu.CompilerParams(vmem_limit_bytes=VMEM),
        cost_estimate=pl.CostEstimate(
            flops=4 * plane * line * 2 * half,
            bytes_accessed=2 * (plane + 2 * line) * 2 * half,
            transcendentals=2 * plane * line,
        ),
        name="tile",
    )(*xs, *a, *b)


def eliminate(pairs):
    size = pairs[0][0].shape[0]
    row = lax.broadcasted_iota(jnp.int32, (size, 1), 0)
    col = lax.broadcasted_iota(jnp.int32, (size, size), 1)
    pairs = list(pairs)
    for k in range(size):
        for n, (m, c) in enumerate(pairs):
            column = m[:, k : k + 1]
            factor = jnp.where(row == k, 0.0, column / m[k : k + 1, k : k + 1])
            pairs[n] = m - factor * m[k : k + 1, :], c - factor * c[k : k + 1, :]
    diagonal = lax.broadcasted_iota(jnp.int32, (size, size), 0) == col
    return [
        c / jnp.sum(jnp.where(diagonal, m, 0.0), axis=1, keepdims=True) for m, c in pairs
    ]


def symmetric(matrix):
    return 0.5 * (matrix + matrix.T)


def step_kernel(rows, rhs, *refs):
    at_ref, got_ref, n0_ref = refs[0:3]
    (w_line, w_far, w_own, t_line, t_far, t_own, k_mine, k_far, p_near, p_far) = refs[3:13]
    near_ref, far_ref, d_ref, weights_ref, residual_ref, rr_ref, w_ref = refs[13:]
    got = jnp.sum(got_ref[...], axis=0)
    n0 = symmetric(n0_ref[...])
    n1, n2 = got[:, rows : rows + rhs], got[:, rows + rhs : rows + 2 * rhs]
    y, x = at_ref[0], at_ref[1]
    for dy in range(4):
        for dx in range(4):
            s = 4 * dy + dx
            of = lax.rem(y + dy, 4) * 4 + lax.rem(x + dx, 4)
            w_ref[:, s * rows : (s + 1) * rows] = got_ref[of][:, :rows]
    kw_near, kw_far = mm(w_ref[...], k_mine[...]), mm(w_ref[...], k_far[...])
    eye = (
        lax.broadcasted_iota(jnp.int32, (rhs, rhs), 0)
        == lax.broadcasted_iota(jnp.int32, (rhs, rhs), 1)
    ).astype(jnp.float32)
    a1, n0_inverse = eliminate([(symmetric(n1) + 2.0 * n0, n0), (n0, eye)])
    a1t = a1.T
    q = eye - 2.0 * a1
    qt = eye - 2.0 * a1t
    cross = mm(qt, mm(n1, a1))
    rr1 = mm(qt, mm(n0, q)) - cross - cross.T + mm(a1t, mm(n2, a1))
    mix = qt + mm(n0_inverse, rr1).T
    d_own = mm(mix, t_own[...]) - mm(a1t, w_own[...])
    near = mm(mix, p_near[...]) - mm(a1t, kw_near)
    far = mm(mix, p_far[...]) - mm(a1t, kw_far)
    d_line = mm(mix, t_line[...]) - mm(a1t, w_line[...])
    d_far = mm(mix, t_far[...]) - mm(a1t, w_far[...])
    curve = nt(d_line, near) + nt(d_far, far) + nt(d_own, d_own)
    near_ref[...] = near
    line = near.shape[1]
    far_ref[:, :line] = far
    far_ref[:, line : line + rhs] = curve
    d_ref[...] = d_own
    weights_ref[...] = mm(a1t, t_own[...])
    residual_ref[...] = mm(qt, t_own[...]) - mm(a1t, w_own[...])
    rr_ref[...] = rr1


def step(rows, rhs, at, *values):
    f32 = jnp.float32
    line = values[2].shape[1]
    vmem = pl.BlockSpec(memory_space=pltpu.VMEM)
    own = jax.ShapeDtypeStruct((rhs, rows), f32)
    return pl.pallas_call(
        functools.partial(step_kernel, rows, rhs),
        out_shape=(
            jax.ShapeDtypeStruct((rhs, line), f32),
            jax.ShapeDtypeStruct((rhs, line + rhs), f32),
            own,
            own,
            own,
            jax.ShapeDtypeStruct((rhs, rhs), f32),
        ),
        in_specs=[pl.BlockSpec(memory_space=pltpu.SMEM)] + [vmem] * len(values),
        out_specs=[vmem] * 6,
        scratch_shapes=[pltpu.VMEM((rhs, 16 * rows), f32)],
        compiler_params=pltpu.CompilerParams(vmem_limit_bytes=VMEM),
        name="step",
    )(at, *values)


def last_kernel(rhs, got, rr, d_own, image, weights, residual, out_weights, out_residual):
    (a2,) = eliminate([(symmetric(jnp.sum(got[...], axis=0)), rr[...])])
    a2t = a2.T
    out_weights[...] = (weights[...] + mm(a2t, d_own[...])).T
    out_residual[...] = (residual[...] - mm(a2t, image[...])).T


def last(rows, rhs, *values):
    vmem = pl.BlockSpec(memory_space=pltpu.VMEM)
    return pl.pallas_call(
        functools.partial(last_kernel, rhs),
        out_shape=(jax.ShapeDtypeStruct((rows, rhs), jnp.float32),) * 2,
        in_specs=[vmem] * len(values),
        out_specs=[vmem] * 2,
        name="last",
    )(*values)


def local(sketches, targets):
    rows, rhs = targets.shape
    depth = sketches.shape[1]
    half = depth // 2
    line = NZ * rows
    z = lax.axis_index("row") // 4
    y = lax.axis_index("row") // 2 % 2 + 2 * (lax.axis_index("col") // NX)
    x = lax.axis_index("col") % NX
    bf16 = jnp.bfloat16

    scale = jnp.sqrt(jnp.sum(sketches * sketches, axis=1, keepdims=True) + 1e-06)
    units = (sketches / scale).astype(bf16)
    hi = targets.astype(bf16)
    rest = targets - hi.astype(jnp.float32)
    mid = rest.astype(bf16)
    low = (rest - mid.astype(jnp.float32)).astype(bf16)
    zero = jnp.zeros((rows, PAD - 3 * rhs), bf16)
    terms = jnp.concatenate([hi, mid, low, zero], axis=1)
    first = jnp.concatenate([units[:, :half], terms], axis=1)
    second = units[:, half:]

    mine = lax.all_gather(
        jnp.concatenate([units, terms], axis=1),
        AXES,
        axis=0,
        tiled=True,
        axis_index_groups=LINES,
    )
    a = jnp.concatenate([first] + [from_x(first, k) for k in range(1, NX)], axis=0)
    b = jnp.concatenate([second] + [from_y(second, k) for k in range(1, NY)], axis=0)
    a, b = lax.optimization_barrier((a, b))
    a = [a] + [from_y(a, k) for k in range(1, NY)]
    b = [b] + [from_x(b, k) for k in range(1, NX)]
    mine, a, b = lax.optimization_barrier((mine, a, b))
    theirs = other_core(mine)
    k_mine, k_far, p_mine, p_far, t_line, t_far, t_plane = tile(
        rows, rhs, half, (mine, theirs), a, b
    )

    n0 = nt(t_plane, t_plane)
    part = jnp.concatenate([p_mine, n0], axis=1)
    part = part + other_core(jnp.concatenate([p_far, n0], axis=1))
    part = jnp.sum(to_all(part, LINES), axis=0)
    w_line = part[:, :line] - t_line
    n0 = part[:, line:]

    n12 = jnp.concatenate([nt(t_line, w_line), nt(w_line, w_line)], axis=1)
    far = other_core(jnp.concatenate([w_line, n12], axis=1))
    w_far = far[:, :line]
    n12 = n12 + far[:, line:]
    w_own = lax.dynamic_slice(w_line, (0, z * rows), (rhs, rows))
    t_own = targets.T
    got = to_all(jnp.concatenate([w_own, n12], axis=1), PLANES)
    at = jnp.stack([y, x]).astype(jnp.int32)
    near2, away, d_own, weights, residual, rr1 = step(
        rows, rhs, at, got, n0, w_line, w_far, w_own, t_line, t_far, t_own, k_mine, k_far, p_mine, p_far
    )

    sent = other_core(away)
    near2 = near2 + sent[:, :line]
    chunks = near2.reshape(rhs, NZ, rows).transpose(1, 0, 2)
    curve = jnp.broadcast_to((away[:, line:] + sent[:, line:])[None], (NZ, rhs, rhs))
    chunks = jnp.concatenate([chunks, curve], axis=2)
    chunks = jnp.sum(
        lax.all_to_all(chunks, AXES, 0, 0, axis_index_groups=LINES, tiled=True), axis=0
    )
    image = chunks[:, :rows] + d_own
    got = to_all(chunks[:, rows:], PLANES)
    return last(rows, rhs, got, rr1, d_own, image, weights, residual)


def solution(mesh):
    in_specs = (P(AXES, None), P(AXES, None))
    out_specs = (P(AXES, None), P(AXES, None))
    return jax.shard_map(local, mesh=mesh, in_specs=in_specs, out_specs=out_specs, check_vma=False)
```

time: 263 us -> 180 us (0.68)
  waiting for transfers between devices: 158 us -> 74.5 us
  other arithmetic: 27.2 us -> 5.43 us
  local copies, waits for them, and re-layouts: 7.93 us -> 19.9 us
  blocking collectives: 0 us -> 10.8 us
  matrix products: 8.75 us -> 0.57 us
  Pallas kernels: 12.1 us -> 19.8 us
    all_gather x1, waiting for transfers between devices: 44.3 us -> 0.01 us  [local(): lax.all_gather(jnp.concatenate([units, terms], axis=1), AXES, axis=0, til...]
    another operation x15 -> x1, other arithmetic: 20.1 us -> 0.08 us  [local(): at = jnp.stack([y, x]).astype(jnp.int32)]
    ppermute x6, waiting for transfers between devices: 24.2 us -> 6.07 us  [from_y(): lax.ppermute(value, AXES, [(device(z, y + k, x, c), device(z, y, x, c)) f...]
    ppermute x6, waiting for transfers between devices: 48.7 us -> 32 us  [from_x(): lax.ppermute(value, AXES, [(device(z, y, x + k, c), device(z, y, x, c)) f...]
    unnamed x17 -> x35, local copies, waits for them, and re-layouts: 2.68 us -> 13.6 us
    all_to_all x0 -> x1, blocking collectives: none -> 10.8 us  [local(): lax.all_to_all(chunks, AXES, 0, 0, axis_index_groups=LINES, tiled=True)]
    pallas_call x0 -> x2, Pallas kernels: none -> 10.2 us  [the longest x1 5.5 us: step(): pl.pallas_call(functools.partial(step_kernel, rows, rhs), out_shape=(jax....]
    all_to_all x1 -> x0, waiting for transfers between devices: 8.12 us -> none  [local(): lax.all_to_all(chunks, AXES, 0, 0, axis_index_groups=LINES, tiled=True)]
  transfers between devices with their start and end apart: 21 -> 20, of which waited for: 17 -> 13; matrix products, arithmetic and copies ran while one was open for 1% -> 1% of each run, Pallas kernels for 2% -> 0%
where the time goes in v3:
time: 180 us; the launch traced here: 179 us
  waiting for transfers between devices  74.5 us (41%)
  starting transfers between devices  33.2 us (18%)
  local copies, waits for them, and re-layouts  19.9 us (11%)
  Pallas kernels  19.8 us (11%)
  between operations  14.3 us (8%)
  blocking collectives  10.8 us (6%)
  other arithmetic  5.43 us (3%)
    ppermute x6, waiting for transfers between devices, from_x(): lax.ppermute(value, AXES, [(device(z, y, x + k, c), device(z, y, x, c)) f...  32 us
    all_to_all x3, waiting for transfers between devices, to_all(): lax.all_to_all(copies, AXES, 0, 0, axis_index_groups=groups, tiled=True)  28.9 us
    all_to_all x3, starting transfers between devices, to_all(): lax.all_to_all(copies, AXES, 0, 0, axis_index_groups=groups, tiled=True)  16.4 us
    unnamed x35, local copies, waits for them, and re-layouts  13.6 us
    all_to_all x1, blocking collectives, local(): lax.all_to_all(chunks, AXES, 0, 0, axis_index_groups=LINES, tiled=True)  10.8 us
    pallas_call x1, Pallas kernels, tile(): pl.pallas_call(functools.partial(tile_kernel, rows, rhs, half), out_shape...  9.62 us
    ppermute x6, starting transfers between devices, from_y(): lax.ppermute(value, AXES, [(device(z, y + k, x, c), device(z, y, x, c)) f...  7.8 us
    ppermute x4, waiting for transfers between devices, other_core(): lax.ppermute(value, AXES, [(device(z, y, x, 1 - c), device(z, y, x, c)) f...  7.43 us
  transfers between devices with their start and end apart: 20, of which 13 were waited for; matrix products, arithmetic and copies ran while one was open for 1% of the time, Pallas kernels for 0%

profile of v3, /device:TPU:1, one launch (start us, length us, event | category | flops | bytes accessed | tf_op | source)
XLA Modules:
  0.0 178.5 jit_solution(8880802965644401323)
XLA Ops:
  7.2 0.7 convert_element_type.19
  7.9 0.8 copy.19
  8.8 1.2 multiply_reduce_fusion
  10.1 1.2 divide_convert_fusion
  11.3 0.8 concatenate.34
  12.2 3.6 %collective-permute-start.3 = (bf16[40,2048]{1,0:T(8,128)(2,1)S(1)}, bf16[40,2048]{1,0:T(8,128)(2,1)S(1)}, u32[]{:S(2)}, u32[]{:S(2)}) collective-permute-start(bf16[40,2048]{1,0:T(8,128)(2,1)S(1)} %get-tuple-element.58), channel_id=1, source_target_pairs={{16,0},{24,8},{17,1},{25,9},{18,2},{26,10},{19,3},{27,11},{4,16},{... | collective-permute-start | bytes 491528 | tf_op jit(solution)/shard_map/ppermute | solution.py:46
  15.8 0.3 collective-permute-start.4
  16.2 0.7 collective-permute-start.5
  16.9 0.1 concatenate.35
  17.0 2.6 %collective-permute-start = (bf16[40,2176]{1,0:T(8,128)(2,1)S(1)}, bf16[40,2176]{1,0:T(8,128)(2,1)S(1)}, u32[]{:S(2)}, u32[]{:S(2)}) collective-permute-start(bf16[40,2176]{1,0:T(8,128)(2,1)S(1)} %concatenate.35), channel_id=1, source_target_pairs={{1,0},{9,8},{2,1},{10,9},{3,2},{11,10},{0,3},{8,11},{17,16},{25,24... | collective-permute-start | bytes 522248 | tf_op jit(solution)/shard_map/ppermute | solution.py:40
  19.5 0.5 collective-permute-start.1
  20.0 0.5 collective-permute-done.3
  20.6 2.9 %collective-permute-start.2 = (bf16[40,2176]{1,0:T(8,128)(2,1)S(1)}, bf16[40,2176]{1,0:T(8,128)(2,1)S(1)}, u32[]{:S(2)}, u32[]{:S(2)}) collective-permute-start(bf16[40,2176]{1,0:T(8,128)(2,1)S(1)} %concatenate.35), channel_id=1, source_target_pairs={{3,0},{11,8},{0,1},{8,9},{1,2},{9,10},{2,3},{10,11},{19,16},{27,24... | collective-permute-start | bytes 522248 | tf_op jit(solution)/shard_map/ppermute | solution.py:40
  23.4 3.5 %collective-permute-done.5 = bf16[40,2048]{1,0:T(8,128)(2,1)S(1)} collective-permute-done((bf16[40,2048]{1,0:T(8,128)(2,1)S(1)}, bf16[40,2048]{1,0:T(8,128)(2,1)S(1)}, u32[]{:S(2)}, u32[]{:S(2)}) %collective-permute-start.5) | collective-permute-done | bytes 163872 | tf_op jit(solution)/shard_map/ppermute | solution.py:46
  27.0 3.8 %collective-permute-done.2 = bf16[40,2176]{1,0:T(8,128)(2,1)S(1)} collective-permute-done((bf16[40,2176]{1,0:T(8,128)(2,1)S(1)}, bf16[40,2176]{1,0:T(8,128)(2,1)S(1)}, u32[]{:S(2)}, u32[]{:S(2)}) %collective-permute-start.2) | collective-permute-done | bytes 174112 | tf_op jit(solution)/shard_map/ppermute | solution.py:40
  31.0 1.9 %collective-permute-start.6 = (bf16[160,2176]{1,0:T(8,128)(2,1)S(1)}, bf16[160,2176]{1,0:T(8,128)(2,1)S(1)}, u32[]{:S(2)}, u32[]{:S(2)}) collective-permute-start(bf16[160,2176]{1,0:T(8,128)(2,1)S(1)} %pad_maximum_fusion.refs_2_), channel_id=1, source_target_pairs={{16,0},{24,8},{17,1},{25,9},{18,2},{26,10},{19,3},{27,11},{4,16},{... | collective-permute-start | bytes 2088968 | tf_op jit(solution)/shard_map/ppermute | solution.py:46
  32.9 1.2 collective-permute-start.7
  34.2 13.6 %collective-permute-done.10.refs_8_ = bf16[160,2048]{1,0:T(8,128)(2,1)S(1)} collective-permute-done((bf16[160,2048]{1,0:T(8,128)(2,1)S(1)}, bf16[160,2048]{1,0:T(8,128)(2,1)S(1)}, u32[]{:S(2)}, u32[]{:S(2)}) %collective-permute-start.10) | collective-permute-done | bytes 655392 | tf_op jit(solution)/shard_map/ppermute | solution.py:40
  47.7 0.9 copy-done.9
  48.6 14.6 %collective-permute-done.11.refs_9_ = bf16[160,2048]{1,0:T(8,128)(2,1)S(1)} collective-permute-done((bf16[160,2048]{1,0:T(8,128)(2,1)S(1)}, bf16[160,2048]{1,0:T(8,128)(2,1)S(1)}, u32[]{:S(2)}, u32[]{:S(2)}) %collective-permute-start.11) | collective-permute-done | bytes 655392 | tf_op jit(solution)/shard_map/ppermute | solution.py:40
  63.2 0.8 copy-done.11
  64.1 0.9 copy-done.13
  64.9 2.0 %collective-permute-done.8.refs_5_ = bf16[160,2176]{1,0:T(8,128)(2,1)S(1)} collective-permute-done((bf16[160,2176]{1,0:T(8,128)(2,1)S(1)}, bf16[160,2176]{1,0:T(8,128)(2,1)S(1)}, u32[]{:S(2)}, u32[]{:S(2)}) %collective-permute-start.8) | collective-permute-done | bytes 696352 | tf_op jit(solution)/shard_map/ppermute | solution.py:46
  66.9 0.9 copy-done.7
  67.8 0.5 collective-permute-start.12
  68.3 4.9 %collective-permute-done.12.refs_1_ = bf16[320,4224]{1,0:T(8,128)(2,1)S(1)} collective-permute-done((bf16[320,4224]{1,0:T(8,128)(2,1)}, bf16[320,4224]{1,0:T(8,128)(2,1)S(1)}, u32[]{:S(2)}, u32[]{:S(2)}) %collective-permute-start.12) | collective-permute-done | bytes 2703392 | tf_op jit(solution)/shard_map/ppermute | solution.py:52
  73.2 1.5 copy-done.15
  74.7 1.1 copy-done.8
  75.8 1.1 copy-done.10
  76.9 1.1 copy-done.12
  78.0 1.1 copy-done.14
  79.1 9.6 %tile.1 = (f32[640,320]{1,0:T(8,128)}, f32[640,320]{1,0:T(8,128)}, f32[32,320]{1,0:T(8,128)S(1)}, f32[32,320]{1,0:T(8,128)S(1)}, f32[32,320]{1,0:T(8,128)S(1)}, ...) custom-call(bf16[320,4224]{1,0:T(8,128)(2,1)} %all-gather.2.cloned.1.call-done.refs_0_, bf16[320,4224]{1,0:T(8,128)(2,1)} %copy-done.15, ...), custom_call_target="tpu_custom_call" | custom-call | flops 3355443200 | bytes 10485760 | tf_op jit(solution)/shard_map/tile/pallas_call | solution.py:128
  88.7 0.2 fusion.3
  89.0 0.4 collective-permute-start.13
  89.4 0.9 collective-permute-done.13
  90.4 0.8 broadcast_in_dim.11
  91.1 8.7 %all-to-all-start = ((f32[8,32,352]{2,1,0:T(8,128)}), f32[8,32,352]{2,1,0:T(8,128)S(1)}, u32[]{:S(2)}, u32[]{:S(2)}) async-start(f32[8,32,352]{2,1,0:T(8,128)} %broadcast_in_dim.11), calls=%async_computation | async-start | bytes 786432 | tf_op jit(solution)/shard_map/all_to_all | solution.py:70
  99.8 15.1 %all-to-all-done = f32[8,32,352]{2,1,0:T(8,128)S(1)} async-done(((f32[8,32,352]{2,1,0:T(8,128)}), f32[8,32,352]{2,1,0:T(8,128)S(1)}, u32[]{:S(2)}, u32[]{:S(2)}) %all-to-all-start) | async-done | bytes 360480 | tf_op jit(solution)/shard_map/all_to_all | solution.py:70
  115.0 0.2 fusion.4
  115.2 0.2 fusion.5
  115.5 0.5 collective-permute-start.14
  116.1 0.8 collective-permute-done.14
  117.1 0.7 broadcast_in_dim.12
  117.8 4.2 %all-to-all-start.1 = ((f32[16,32,104]{2,1,0:T(8,128)}), f32[16,32,104]{2,1,0:T(8,128)S(1)}, u32[]{:S(2)}, u32[]{:S(2)}) async-start(f32[16,32,104]{2,1,0:T(8,128)} %broadcast_in_dim.12), calls=%async_computation.1 | async-start | bytes 524288 | tf_op jit(solution)/shard_map/all_to_all | solution.py:70
  122.2 7.9 %all-to-all-done.1.refs_1_ = f32[16,32,104]{2,1,0:T(8,128)S(1)} async-done(((f32[16,32,104]{2,1,0:T(8,128)}), f32[16,32,104]{2,1,0:T(8,128)S(1)}, u32[]{:S(2)}, u32[]{:S(2)}) %all-to-all-start.1) | async-done | bytes 213024 | tf_op jit(solution)/shard_map/all_to_all | solution.py:70
  130.2 5.5 %step.1 = (f32[32,320]{1,0:T(8,128)S(1)}, f32[32,352]{1,0:T(8,128)S(1)}, f32[32,40]{1,0:T(8,128)S(1)}, f32[32,40]{1,0:T(8,128)S(1)}, f32[32,40]{1,0:T(8,128)S(1)}, /*index=5*/f32[32,32]{1,0:T(8,128)S(1)}) custom-call(s32[2]{0:T(128)S(1)} %pad_add_fusion.refs_0_, f32[16,32,104]{2,1,0:T(8,128)S(1)} %all-to-all-done.1.refs_1_, f32[32,32]{1,0:T(8,128)S(1)} %slice.48.refs_2_, ...), custom_call_target="tpu_custom_call" | custom-call | tf_op jit(solution)/shard_map/step/pallas_call | solution.py:218
  135.7 0.6 copy-done.4
  136.3 0.6 copy-done.5
  136.9 0.6 copy-done.6
  137.5 1.5 collective-permute-start.15
  139.0 0.9 collective-permute-done.15
  139.9 0.1 reshape.17
  140.2 0.1 pad_maximum_fusion.2
  140.3 10.8 %all_to_all.20 = f32[8,32,72]{2,1,0:T(8,128)S(1)} all-to-all(f32[8,32,72]{2,1,0:T(8,128)S(1)} %pad_maximum_fusion.2), channel_id=1, replica_groups={{0,32,64,96,128,160,192,224},{8,40,72,104,136,168,200,232},{1,33,65,97,..., dimensions={0} | all-to-all | bytes 147456 | tf_op jit(solution)/shard_map/all_to_all | solution.py:318
  151.2 0.8 reshape.18
  152.0 3.5 %all-to-all-start.3 = ((f32[16,1,1024]{2,1,0:T(1,128)}), f32[16,1,1024]{2,1,0:T(1,128)S(1)}, u32[]{:S(2)}, u32[]{:S(2)}) async-start(f32[16,1,1024]{2,1,0:T(1,128)} %reshape.18), calls=%async_computation.3 | async-start | bytes 131072 | tf_op jit(solution)/shard_map/all_to_all | solution.py:70
  155.5 0.6 slice_add_fusion.1.image
  156.1 5.8 %all-to-all-done.3 = f32[16,1,1024]{2,1,0:T(1,128)S(1)} async-done(((f32[16,1,1024]{2,1,0:T(1,128)}), f32[16,1,1024]{2,1,0:T(1,128)S(1)}, u32[]{:S(2)}, u32[]{:S(2)}) %all-to-all-start.3) | async-done | bytes 65568 | tf_op jit(solution)/shard_map/all_to_all | solution.py:70
  161.9 0.6 broadcast.14
  162.5 0.8 reduce
  163.3 0.8 reshape.19.got
  164.1 4.7 %last.1 = (f32[40,32]{1,0:T(8,128)}, f32[40,32]{1,0:T(8,128)}) custom-call(f32[16,32,32]{2,1,0:T(8,128)} %reshape.19.got, f32[32,32]{1,0:T(8,128)} %copy-done.6, f32[32,40]{1,0:T(8,128)} %copy-done.3, f32[32,40]{1,0:T(8,128)} %slice_add_fusion.1.image, f32[32,40]{1,0:T(8,128)} %copy-done.4, f32[32,40]{1,0:T(8,128)} %copy-done.5), custom_call_target="tpu_custom_call" | custom-call | tf_op jit(solution)/shard_map/last/pallas_call | solution.py:245
  168.9 1.4 copy.23
  170.3 1.4 copy.24
  (57 shorter events, 1.3 us)
Async XLA Ops:
  7.2 60.6 %all-gather.2.cloned.1.call-start = ((), (), s32[]{:S(2)}) async-start(), calls=%async_computation.4 | async-start | bytes 3041280 | tf_op jit(solution)/shard_map/all_gather | solution.py:275
  12.2 8.4 %collective-permute-start.3 = (bf16[40,2048]{1,0:T(8,128)(2,1)S(1)}, bf16[40,2048]{1,0:T(8,128)(2,1)S(1)}, u32[]{:S(2)}, u32[]{:S(2)}) collective-permute-start(bf16[40,2048]{1,0:T(8,128)(2,1)S(1)} %get-tuple-element.58), channel_id=1, source_target_pairs={{16,0},{24,8},{17,1},{25,9},{18,2},{26,10},{19,3},{27,11},{4,16},{... | collective-permute-start | bytes 491528 | tf_op jit(solution)/shard_map/ppermute | solution.py:46
  15.8 7.6 %collective-permute-start.4 = (bf16[40,2048]{1,0:T(8,128)(2,1)S(1)}, bf16[40,2048]{1,0:T(8,128)(2,1)S(1)}, u32[]{:S(2)}, u32[]{:S(2)}) collective-permute-start(bf16[40,2048]{1,0:T(8,128)(2,1)S(1)} %get-tuple-element.58), channel_id=1, source_target_pairs={{4,0},{12,8},{5,1},{13,9},{6,2},{14,10},{7,3},{15,11},{20,16},{28,... | collective-permute-start | bytes 491528 | tf_op jit(solution)/shard_map/ppermute | solution.py:46
  16.2 10.8 %collective-permute-start.5 = (bf16[40,2048]{1,0:T(8,128)(2,1)S(1)}, bf16[40,2048]{1,0:T(8,128)(2,1)S(1)}, u32[]{:S(2)}, u32[]{:S(2)}) collective-permute-start(bf16[40,2048]{1,0:T(8,128)(2,1)S(1)} %get-tuple-element.58), channel_id=1, source_target_pairs={{20,0},{28,8},{21,1},{29,9},{22,2},{30,10},{23,3},{31,11},{0,16},{... | collective-permute-start | bytes 491528 | tf_op jit(solution)/shard_map/ppermute | solution.py:46
  17.0 10.1 %collective-permute-start = (bf16[40,2176]{1,0:T(8,128)(2,1)S(1)}, bf16[40,2176]{1,0:T(8,128)(2,1)S(1)}, u32[]{:S(2)}, u32[]{:S(2)}) collective-permute-start(bf16[40,2176]{1,0:T(8,128)(2,1)S(1)} %concatenate.35), channel_id=1, source_target_pairs={{1,0},{9,8},{2,1},{10,9},{3,2},{11,10},{0,3},{8,11},{17,16},{25,24... | collective-permute-start | bytes 522248 | tf_op jit(solution)/shard_map/ppermute | solution.py:40
  19.5 7.5 %collective-permute-start.1 = (bf16[40,2176]{1,0:T(8,128)(2,1)S(1)}, bf16[40,2176]{1,0:T(8,128)(2,1)S(1)}, u32[]{:S(2)}, u32[]{:S(2)}) collective-permute-start(bf16[40,2176]{1,0:T(8,128)(2,1)S(1)} %concatenate.35), channel_id=1, source_target_pairs={{2,0},{10,8},{3,1},{11,9},{0,2},{8,10},{1,3},{9,11},{18,16},{26,24... | collective-permute-start | bytes 522248 | tf_op jit(solution)/shard_map/ppermute | solution.py:40
  20.6 10.3 %collective-permute-start.2 = (bf16[40,2176]{1,0:T(8,128)(2,1)S(1)}, bf16[40,2176]{1,0:T(8,128)(2,1)S(1)}, u32[]{:S(2)}, u32[]{:S(2)}) collective-permute-start(bf16[40,2176]{1,0:T(8,128)(2,1)S(1)} %concatenate.35), channel_id=1, source_target_pairs={{3,0},{11,8},{0,1},{8,9},{1,2},{9,10},{2,3},{10,11},{19,16},{27,24... | collective-permute-start | bytes 522248 | tf_op jit(solution)/shard_map/ppermute | solution.py:40
  30.9 16.8 %collective-permute-start.10 = (bf16[160,2048]{1,0:T(8,128)(2,1)S(1)}, bf16[160,2048]{1,0:T(8,128)(2,1)S(1)}, u32[]{:S(2)}, u32[]{:S(2)}) collective-permute-start(bf16[160,2048]{1,0:T(8,128)(2,1)S(1)} %pad_maximum_fusion.1.refs_6_), channel_id=1, source_target_pairs={{2,0},{10,8},{3,1},{11,9},{0,2},{8,10},{1,3},{9,11},{18,16},{26,24... | collective-permute-start | bytes 1966088 | tf_op jit(solution)/shard_map/ppermute | solution.py:40
  31.0 33.9 %collective-permute-start.6 = (bf16[160,2176]{1,0:T(8,128)(2,1)S(1)}, bf16[160,2176]{1,0:T(8,128)(2,1)S(1)}, u32[]{:S(2)}, u32[]{:S(2)}) collective-permute-start(bf16[160,2176]{1,0:T(8,128)(2,1)S(1)} %pad_maximum_fusion.refs_2_), channel_id=1, source_target_pairs={{16,0},{24,8},{17,1},{25,9},{18,2},{26,10},{19,3},{27,11},{4,16},{... | collective-permute-start | bytes 2088968 | tf_op jit(solution)/shard_map/ppermute | solution.py:46
  32.9 32.0 %collective-permute-start.7 = (bf16[160,2176]{1,0:T(8,128)(2,1)S(1)}, bf16[160,2176]{1,0:T(8,128)(2,1)S(1)}, u32[]{:S(2)}, u32[]{:S(2)}) collective-permute-start(bf16[160,2176]{1,0:T(8,128)(2,1)S(1)} %pad_maximum_fusion.refs_2_), channel_id=1, source_target_pairs={{4,0},{12,8},{5,1},{13,9},{6,2},{14,10},{7,3},{15,11},{20,16},{28,... | collective-permute-start | bytes 2088968 | tf_op jit(solution)/shard_map/ppermute | solution.py:46
  34.1 32.8 %collective-permute-start.8 = (bf16[160,2176]{1,0:T(8,128)(2,1)S(1)}, bf16[160,2176]{1,0:T(8,128)(2,1)S(1)}, u32[]{:S(2)}, u32[]{:S(2)}) collective-permute-start(bf16[160,2176]{1,0:T(8,128)(2,1)S(1)} %pad_maximum_fusion.refs_2_), channel_id=1, source_target_pairs={{20,0},{28,8},{21,1},{29,9},{22,2},{30,10},{23,3},{31,11},{0,16},{... | collective-permute-start | bytes 2088968 | tf_op jit(solution)/shard_map/ppermute | solution.py:46
  34.2 29.1 %collective-permute-start.11 = (bf16[160,2048]{1,0:T(8,128)(2,1)S(1)}, bf16[160,2048]{1,0:T(8,128)(2,1)S(1)}, u32[]{:S(2)}, u32[]{:S(2)}) collective-permute-start(bf16[160,2048]{1,0:T(8,128)(2,1)S(1)} %pad_maximum_fusion.1.refs_6_), channel_id=1, source_target_pairs={{3,0},{11,8},{0,1},{8,9},{1,2},{9,10},{2,3},{10,11},{19,16},{27,24... | collective-permute-start | bytes 1966088 | tf_op jit(solution)/shard_map/ppermute | solution.py:40
  47.7 0.9 copy-start.9
  48.6 15.5 %collective-permute-start.9 = (bf16[160,2048]{1,0:T(8,128)(2,1)S(1)}, bf16[160,2048]{1,0:T(8,128)(2,1)S(1)}, u32[]{:S(2)}, u32[]{:S(2)}) collective-permute-start(bf16[160,2048]{1,0:T(8,128)(2,1)S(1)} %pad_maximum_fusion.1.refs_6_), channel_id=1, source_target_pairs={{1,0},{9,8},{2,1},{10,9},{3,2},{11,10},{0,3},{8,11},{17,16},{25,24... | collective-permute-start | bytes 1966088 | tf_op jit(solution)/shard_map/ppermute | solution.py:40
  63.2 0.8 copy-start.11
  64.0 0.9 copy-start.13
  66.9 0.9 copy-start.7
  67.8 5.4 %collective-permute-start.12 = (bf16[320,4224]{1,0:T(8,128)(2,1)}, bf16[320,4224]{1,0:T(8,128)(2,1)S(1)}, u32[]{:S(2)}, u32[]{:S(2)}) collective-permute-start(bf16[320,4224]{1,0:T(8,128)(2,1)} %all-gather.2.cloned.1.call-done.refs_0_), channel_id=1, source_target_pairs={{8,0},{0,8},{9,1},{1,9},{10,2},{2,10},{11,3},{3,11},{24,16},{16,24... | collective-permute-start | bytes 8110088 | tf_op jit(solution)/shard_map/ppermute | solution.py:52
  73.2 1.5 copy-start.15
  74.7 1.1 copy-start.8
  75.8 1.1 copy-start.10
  76.9 1.1 copy-start.12
  78.0 1.1 copy-start.14
  89.0 1.3 collective-permute-start.13
  91.1 39.0 %copy-start = (f32[640,320]{1,0:T(8,128)S(1)}, f32[640,320]{1,0:T(8,128)}, u32[]{:S(2)}) copy-start(f32[640,320]{1,0:T(8,128)} %get-tuple-element.42.refs_9_) | copy-start | bytes 2457604
  91.1 39.1 %copy-start.1 = (f32[640,320]{1,0:T(8,128)S(1)}, f32[640,320]{1,0:T(8,128)}, u32[]{:S(2)}) copy-start(f32[640,320]{1,0:T(8,128)} %get-tuple-element.43.refs_10_) | copy-start | bytes 2457604
  91.1 39.1 %copy-start.2 = (f32[40,32]{0,1:T(8,128)S(1)}, f32[40,32]{0,1:T(8,128)}, u32[]{:S(2)}) copy-start(f32[40,32]{0,1:T(8,128)} %param.3) | copy-start | bytes 15364
  91.1 23.9 %all-to-all-start = ((f32[8,32,352]{2,1,0:T(8,128)}), f32[8,32,352]{2,1,0:T(8,128)S(1)}, u32[]{:S(2)}, u32[]{:S(2)}) async-start(f32[8,32,352]{2,1,0:T(8,128)} %broadcast_in_dim.11), calls=%async_computation | async-start | bytes 786432 | tf_op jit(solution)/shard_map/all_to_all | solution.py:70
  115.5 1.4 collective-permute-start.14
  117.8 12.4 %all-to-all-start.1 = ((f32[16,32,104]{2,1,0:T(8,128)}), f32[16,32,104]{2,1,0:T(8,128)S(1)}, u32[]{:S(2)}, u32[]{:S(2)}) async-start(f32[16,32,104]{2,1,0:T(8,128)} %broadcast_in_dim.12), calls=%async_computation.1 | async-start | bytes 524288 | tf_op jit(solution)/shard_map/all_to_all | solution.py:70
  135.7 0.6 copy-start.4
  136.3 0.6 copy-start.5
  136.9 0.6 copy-start.6
  137.5 26.6 %copy-start.3 = (f32[32,40]{1,0:T(8,128)}, f32[32,40]{1,0:T(8,128)S(1)}, u32[]{:S(2)}) copy-start(f32[32,40]{1,0:T(8,128)S(1)} %get-tuple-element.47.d_own) | copy-start | bytes 15364
  137.5 2.4 %collective-permute-start.15 = (f32[32,352]{1,0:T(8,128)S(1)}, f32[32,352]{1,0:T(8,128)S(1)}, u32[]{:S(2)}, u32[]{:S(2)}) collective-permute-start(f32[32,352]{1,0:T(8,128)S(1)} %get-tuple-element.45), channel_id=1, source_target_pairs={{8,0},{0,8},{9,1},{1,9},{10,2},{2,10},{11,3},{3,11},{24,16},{16,24... | collective-permute-start | bytes 135176 | tf_op jit(solution)/shard_map/ppermute | solution.py:52
  152.0 9.9 %all-to-all-start.3 = ((f32[16,1,1024]{2,1,0:T(1,128)}), f32[16,1,1024]{2,1,0:T(1,128)S(1)}, u32[]{:S(2)}, u32[]{:S(2)}) async-start(f32[16,1,1024]{2,1,0:T(1,128)} %reshape.18), calls=%async_computation.3 | async-start | bytes 131072 | tf_op jit(solution)/shard_map/all_to_all | solution.py:70
Sparse Core Ops, SparseCore 0:
  12.3 44.0 all-gather.1

commit v4 on v0

v4 whole, which is shorter than its diff:
```python
import functools

import jax
import jax.numpy as jnp
from jax import lax
from jax.experimental import pallas as pl
from jax.experimental.pallas import tpu as pltpu
from jax.sharding import PartitionSpec as P

sharpness = 4.0
AXES = ("row", "col")
NZ, NY, NX, NC = 8, 4, 4, 2
HIGH = lax.Precision.HIGHEST
PAD = 128
MIB = 1024 * 1024
F32 = jnp.float32
BF16 = jnp.bfloat16
VM = pl.BlockSpec(memory_space=pltpu.VMEM)
SM = pl.BlockSpec(memory_space=pltpu.SMEM)
ANY = pl.BlockSpec(memory_space=pl.ANY)


def device(z, y, x, c):
    z, y, x = z % NZ, y % NY, x % NX
    return ((z * 2 + y % 2) * 2 + c) * 8 + (y // 2) * 4 + x


PLACES = [
    (z, y, x, c) for z in range(NZ) for y in range(NY) for x in range(NX) for c in range(NC)
]
LINES = [
    [device(z, y, x, c) for z in range(NZ)]
    for y in range(NY)
    for x in range(NX)
    for c in range(NC)
]
PLANES = [
    [device(z, y, x, c) for y in range(NY) for x in range(NX)]
    for z in range(NZ)
    for c in range(NC)
]


def from_x(value, k):
    return lax.ppermute(
        value, AXES, [(device(z, y, x + k, c), device(z, y, x, c)) for z, y, x, c in PLACES]
    )


def from_y(value, k):
    return lax.ppermute(
        value, AXES, [(device(z, y + k, x, c), device(z, y, x, c)) for z, y, x, c in PLACES]
    )


def other_core(value):
    return lax.ppermute(
        value, AXES, [(device(z, y, x, 1 - c), device(z, y, x, c)) for z, y, x, c in PLACES]
    )


def exchange(chunks, groups):
    return lax.all_to_all(chunks, AXES, 0, 0, axis_index_groups=groups, tiled=True)


def shape(*dims, dtype=F32):
    return jax.ShapeDtypeStruct(dims, dtype)


def mm(a, b):
    return jnp.dot(a, b, precision=HIGH, preferred_element_type=F32)


def nt(a, b):
    return lax.dot_general(
        a, b, (((1,), (1,)), ((), ())), precision=HIGH, preferred_element_type=F32
    )


def small_kernel(body, out, args, specs=None, limit=8, scratch=(), name=None):
    return pl.pallas_call(
        body,
        out_shape=out,
        in_specs=specs or [VM] * len(args),
        out_specs=jax.tree.map(lambda _: VM, out),
        scratch_shapes=list(scratch),
        compiler_params=pltpu.CompilerParams(vmem_limit_bytes=limit * MIB),
        name=name,
    )(*args)


def prepare_kernel(half, s_ref, t_ref, all_ref, first_ref, second_ref):
    sketches = s_ref[...]
    scale = jnp.sqrt(jnp.sum(sketches * sketches, axis=1, keepdims=True) + 1e-06)
    units = (sketches / scale).astype(BF16)
    targets = t_ref[...].T
    hi = targets.astype(BF16).astype(F32)
    mid = (targets - hi).astype(BF16).astype(F32)
    low = targets - hi - mid
    terms = jnp.concatenate([hi, mid, low, jnp.zeros_like(low)], axis=1).astype(BF16)
    all_ref[:, : 2 * half] = units
    all_ref[:, 2 * half :] = terms
    first_ref[:, :half] = units[:, :half]
    first_ref[:, half:] = terms
    second_ref[...] = units[:, half:]


def tile_body(rows, rhs, half, x_ref, a_ref, b_ref, cos_ref, k_ref):
    dims = (((1,), (1,)), ((), ()))
    k_ref[...] = lax.dot_general(
        a_ref[:, :half], x_ref[:, :half], dims, preferred_element_type=F32
    )
    cos_ref[...] = lax.dot_general(
        b_ref[...], x_ref[:, half : 2 * half], dims, preferred_element_type=F32
    )
    for y in range(4):
        for x in range(4):
            to, of = pl.ds((4 * y + x) * rows, rows), pl.ds((4 * x + y) * rows, rows)
            k_ref[to, :] = jnp.exp(sharpness * (k_ref[to, :] + cos_ref[of, :] - 1.0))


def targets_of(terms, rhs):
    terms = terms.astype(F32).T
    return terms[:rhs] + terms[rhs : 2 * rhs] + terms[2 * rhs : 3 * rhs]


def mine_kernel(rows, rhs, half, *refs):
    x_hbm, a_hbm, b_hbm = refs[0], refs[1:6], refs[6:11]
    k_ref, p_ref, tx_ref, ty_ref, n0_ref, a_ref, b_ref = refs[11:18]
    x_ref, cos_ref, sems = refs[18:]
    side, line = 4 * rows, 8 * rows
    places = [(0, side), (side, side), (2 * side, side // 2)]
    places += [(5 * side // 2, side // 2), (3 * side, side)]
    copies = [pltpu.make_async_copy(x_hbm, x_ref, sems.at[0])]
    for i, (at, size) in enumerate(places):
        to = pl.ds(at, size)
        copies.append(pltpu.make_async_copy(a_hbm[i], a_ref.at[to], sems.at[1 + 2 * i]))
        copies.append(pltpu.make_async_copy(b_hbm[i], b_ref.at[to], sems.at[2 + 2 * i]))
    for copy in copies:
        copy.start()
    for copy in copies:
        copy.wait()
    tile_body(rows, rhs, half, x_ref, a_ref, b_ref, cos_ref, k_ref)
    tx_ref[...] = targets_of(x_ref[:, 2 * half :], rhs)
    ty = targets_of(a_ref[:, half:], rhs)
    ty_ref[...] = ty
    n0 = nt(ty, ty)
    n0_ref[...] = n0
    p_ref[:, :line] = mm(ty, k_ref[...])
    p_ref[:, line:] = n0


def theirs_kernel(rows, rhs, half, *refs):
    x_hbm, a_ref, b_ref, ty_ref, n0_ref, k_ref, p_ref, tx_ref, x_ref, cos_ref, sem = refs
    line = 8 * rows
    copy = pltpu.make_async_copy(x_hbm, x_ref, sem)
    copy.start()
    copy.wait()
    tile_body(rows, rhs, half, x_ref, a_ref, b_ref, cos_ref, k_ref)
    tx_ref[...] = targets_of(x_ref[:, 2 * half :], rhs)
    p_ref[:, :line] = mm(ty_ref[...], k_ref[...])
    p_ref[:, line:] = n0_ref[...]


def share_kernel(count, a_ref, b_ref, out_ref):
    value = a_ref[...] + b_ref[...]
    for i in range(count):
        out_ref[i] = value


def line_kernel(line, part_ref, t_ref, send_ref, n0_ref):
    part = jnp.sum(part_ref[...], axis=0)
    rhs = part.shape[0]
    t = t_ref[...]
    w = part[:, :line] - t
    n0_ref[...] = part[:, line:]
    send_ref[:, :line] = w
    send_ref[:, line : line + rhs] = nt(t, w)
    send_ref[:, line + rhs :] = nt(w, w)


def spread_kernel(rows, line, at_ref, near_ref, far_ref, out_ref):
    grams = near_ref[:, line:] + far_ref[:, line:]
    own = jnp.zeros((near_ref.shape[0], rows), F32)
    for z in range(NZ):
        own = jnp.where(at_ref[0] == z, near_ref[:, z * rows : (z + 1) * rows], own)
    for i in range(NY * NX):
        out_ref[i, :, :rows] = own
        out_ref[i, :, rows:] = grams


def eliminate(pairs):
    size = pairs[0][0].shape[0]
    row = lax.broadcasted_iota(jnp.int32, (size, size), 0)
    col = lax.broadcasted_iota(jnp.int32, (size, size), 1)
    pairs = list(pairs)
    for k in range(size):
        for n, (m, c) in enumerate(pairs):
            column = jnp.broadcast_to(m[:, k : k + 1], (size, size))
            inverse = 1.0 / column[k : k + 1, :]
            column = jnp.where(row == k, 0.0, column)
            m_row, c_row = m[k : k + 1, :] * inverse, c[k : k + 1, :] * inverse
            pairs[n] = m - column * m_row, c - column * c_row
    return [
        c / jnp.sum(jnp.where(row == col, m, 0.0), axis=1, keepdims=True) for m, c in pairs
    ]


def symmetric(matrix):
    return 0.5 * (matrix + matrix.T)


def step_kernel(rows, rhs, line, at_ref, *refs):
    got_ref, n0_ref, w_line, w_far, t_line, t_far, t_plane, k_mine, k_far = refs[:9]
    near_ref, far_ref, d_ref, weights_ref, residual_ref, rr_ref, w_ref = refs[9:]
    got = jnp.sum(got_ref[...], axis=0)
    n0 = symmetric(n0_ref[...])
    n1, n2 = got[:, rows : rows + rhs], got[:, rows + rhs : rows + 2 * rhs]
    y, x = at_ref[1], at_ref[2]
    for dy in range(NY):
        for dx in range(NX):
            s = NX * dy + dx
            of = lax.rem(y + dy, NY) * NX + lax.rem(x + dx, NX)
            w_ref[:, s * rows : (s + 1) * rows] = got_ref[of][:, :rows]
    eye = (
        lax.broadcasted_iota(jnp.int32, (rhs, rhs), 0)
        == lax.broadcasted_iota(jnp.int32, (rhs, rhs), 1)
    ).astype(F32)
    a1, n0_inverse = eliminate([(symmetric(n1) + 2.0 * n0, n0), (n0, eye)])
    a1t = a1.T
    q = eye - 2.0 * a1
    qt = eye - 2.0 * a1t
    cross = mm(qt, mm(n1, a1))
    rr1 = mm(qt, mm(n0, q)) - cross - cross.T + mm(a1t, mm(n2, a1))
    mix = qt + mm(n0_inverse, rr1).T
    d_plane = mm(mix, t_plane[...]) - mm(a1t, w_ref[...])
    near = mm(d_plane, k_mine[...])
    far = mm(d_plane, k_far[...])
    d_line = mm(mix, t_line[...]) - mm(a1t, w_line[:, :line])
    d_far = mm(mix, t_far[...]) - mm(a1t, w_far[:, :line])
    d_own, t_own = d_plane[:, :rows], t_plane[:, :rows]
    near_ref[...] = near
    far_ref[:, :line] = far
    far_ref[:, line:] = nt(d_line, near) + nt(d_far, far) + nt(d_own, d_own)
    d_ref[...] = d_own
    weights_ref[...] = mm(a1t, t_own)
    residual_ref[...] = mm(qt, t_own) - mm(a1t, w_ref[:, :rows])
    rr_ref[...] = rr1


def chunk_kernel(rows, line, near_ref, far_ref, here_ref, out_ref):
    gram = far_ref[:, line:] + here_ref[:, line:]
    total = near_ref[...] + far_ref[:, :line]
    for z in range(NZ):
        out_ref[z, :, :rows] = total[:, z * rows : (z + 1) * rows]
        out_ref[z, :, rows:] = gram


def image_kernel(rows, got_ref, d_ref, image_ref, out_ref):
    got = jnp.sum(got_ref[...], axis=0)
    image_ref[...] = got[:, :rows] + d_ref[...]
    gram = got[:, rows:]
    dense = jnp.concatenate([gram[8 * i : 8 * i + 8] for i in range(4)], axis=1)
    for i in range(NY * NX):
        out_ref[i] = dense


def last_kernel(rhs, got_ref, rr, d_own, image, weights, residual, out_weights, out_residual):
    dense = jnp.sum(got_ref[...], axis=0)
    gram = jnp.concatenate([dense[:, rhs * i : rhs * (i + 1)] for i in range(4)], axis=0)
    (a2,) = eliminate([(symmetric(gram), rr[...])])
    a2t = a2.T
    out_weights[...] = weights[...] + mm(a2t, d_own[...])
    out_residual[...] = residual[...] - mm(a2t, image[...])


def local(sketches, targets):
    rows, rhs = targets.shape
    half = sketches.shape[1] // 2
    line, plane = NZ * rows, NY * NX * rows
    z = lax.axis_index("row") // 4
    y = lax.axis_index("row") // 2 % 2 + 2 * (lax.axis_index("col") // NX)
    x = lax.axis_index("col") % NX
    at = jnp.stack([z, y, x]).astype(jnp.int32)
    sizes = (rows, rhs, half)

    units, first, second = small_kernel(
        functools.partial(prepare_kernel, half),
        (
            shape(rows, 2 * half + PAD, dtype=BF16),
            shape(rows, half + PAD, dtype=BF16),
            shape(rows, half, dtype=BF16),
        ),
        (sketches, targets.T),
        name="prepare",
    )
    mine = lax.all_gather(units, AXES, axis=0, tiled=True, axis_index_groups=LINES)
    a = jnp.concatenate([first] + [from_x(first, k) for k in range(1, NX)], axis=0)
    b = jnp.concatenate([second] + [from_y(second, k) for k in range(1, NY)], axis=0)
    a, b = lax.optimization_barrier((a, b))
    a1, b1, a3, b3 = from_y(a, 1), from_x(b, 1), from_y(a, 3), from_x(b, 3)
    top = 2 * rows
    a2, b2 = from_y(a1[:top], 1), from_x(b1[:top], 1)
    a2_low, b2_low = from_y(a3[top:], 3), from_x(b3[top:], 3)
    mine, a, b = lax.optimization_barrier(
        (mine, (a, a1, a2, a2_low, a3), (b, b1, b2, b2_low, b3))
    )
    theirs = other_core(mine)
    cost = pl.CostEstimate(
        flops=4 * plane * line * half,
        bytes_accessed=2 * (plane + line) * 2 * half,
        transcendentals=plane * line,
    )
    k_mine, near, t_line, t_plane, n0, y_first, y_second = pl.pallas_call(
        functools.partial(mine_kernel, *sizes),
        out_shape=(
            shape(plane, line),
            shape(rhs, line + rhs),
            shape(rhs, line),
            shape(rhs, plane),
            shape(rhs, rhs),
            shape(plane, half + PAD, dtype=BF16),
            shape(plane, half, dtype=BF16),
        ),
        in_specs=[ANY] * 11,
        out_specs=[VM] * 7,
        scratch_shapes=[
            pltpu.VMEM((line, 2 * half + PAD), BF16),
            pltpu.VMEM((plane, line), F32),
            pltpu.SemaphoreType.DMA((11,)),
        ],
        compiler_params=pltpu.CompilerParams(vmem_limit_bytes=20 * MIB),
        cost_estimate=cost,
        name="tile_mine",
    )(mine, *a, *b)
    k_far, far, t_far = pl.pallas_call(
        functools.partial(theirs_kernel, *sizes),
        out_shape=(shape(plane, line), shape(rhs, line + rhs), shape(rhs, line)),
        in_specs=[ANY] + [VM] * 4,
        out_specs=[VM] * 3,
        scratch_shapes=[
            pltpu.VMEM((line, 2 * half + PAD), BF16),
            pltpu.VMEM((plane, line), F32),
            pltpu.SemaphoreType.DMA,
        ],
        compiler_params=pltpu.CompilerParams(vmem_limit_bytes=20 * MIB),
        cost_estimate=cost,
        name="tile_theirs",
    )(theirs, y_first, y_second, t_plane, n0)

    copies = small_kernel(
        functools.partial(share_kernel, NZ),
        shape(NZ, rhs, line + rhs),
        (near, other_core(far)),
        name="share",
    )
    sent, n0 = small_kernel(
        functools.partial(line_kernel, line),
        (shape(rhs, line + 2 * rhs), shape(rhs, rhs)),
        (exchange(copies, LINES), t_line),
        name="line",
    )
    received = other_core(sent)
    copies = small_kernel(
        functools.partial(spread_kernel, rows, line),
        shape(NY * NX, rhs, rows + 2 * rhs),
        (at, sent, received),
        [SM, VM, VM],
        name="spread",
    )
    got = exchange(copies, PLANES)
    own = shape(rhs, rows)
    values = (at, got, n0, sent, received, t_line, t_far, t_plane, k_mine, k_far)
    near, far, d_own, weights, residual, rr1 = small_kernel(
        functools.partial(step_kernel, rows, rhs, line),
        (shape(rhs, line), shape(rhs, line + rhs), own, own, own, shape(rhs, rhs)),
        values,
        [SM] + [VM] * 9,
        limit=16,
        scratch=[pltpu.VMEM((rhs, plane), F32)],
        name="step",
    )
    return finish(rows, rhs, line, near, far, d_own, weights, residual, rr1)


def finish(rows, rhs, line, near, far, d_own, weights, residual, rr1):
    away = other_core(far)
    chunks = small_kernel(
        functools.partial(chunk_kernel, rows, line),
        shape(NZ, rhs, rows + rhs),
        (near, away, far),
        name="chunk",
    )
    own = shape(rhs, rows)
    image, copies = small_kernel(
        functools.partial(image_kernel, rows),
        (own, shape(NY * NX, rhs // 4, 4 * rhs)),
        (exchange(chunks, LINES), d_own),
        name="image",
    )
    weights, residual = small_kernel(
        functools.partial(last_kernel, rhs),
        (own, own),
        (exchange(copies, PLANES), rr1, d_own, image, weights, residual),
        name="last",
    )
    return weights.T, residual.T


def solution(mesh):
    in_specs = (P(AXES, None), P(AXES, None))
    out_specs = (P(AXES, None), P(AXES, None))
    return jax.shard_map(local, mesh=mesh, in_specs=in_specs, out_specs=out_specs, check_vma=False)
```

time: 533 us -> 161 us (0.30)
  blocking collectives: 374 us -> 32.2 us
  waiting for transfers between devices: 102 us -> 45 us
  starting transfers between devices: 0.08 us -> 31.8 us
  other arithmetic: 23.3 us -> 0.17 us
  Pallas kernels: 0 us -> 22.9 us
  matrix products: 14.9 us -> 0 us
  local copies, waits for them, and re-layouts: 2.21 us -> 13.4 us
    psum x3 -> x0, blocking collectives: 233 us -> none  [the longest x2 153 us: squares(): return lax.psum(local_gram(residual, residual), ('row', 'col'))]
    all_gather x2 -> x1, waiting for transfers between devices: 102 us -> 0.01 us  [local(): lax.all_gather(units, AXES, axis=0, tiled=True, axis_index_groups=LINES)]
    all_gather x2 -> x0, blocking collectives: 74.7 us -> none  [local(): whole = lax.all_gather(direction, 'row', axis=0, tiled=True)]
    unnamed x2 -> x0, blocking collectives: 66.2 us -> none
    all_to_all x0 -> x3, blocking collectives: none -> 32.2 us  [exchange(): lax.all_to_all(chunks, AXES, 0, 0, axis_index_groups=groups, tiled=True)]
    ppermute x0 -> x18, waiting for transfers between devices: none -> 29.8 us  [the longest x7 17.6 us: from_y(): lax.ppermute(value, AXES, [(device(z, y + k, x, c), device(z, y, x, c)) f...]
    ppermute x0 -> x18, starting transfers between devices: none -> 23.4 us  [the longest x7 8.86 us: from_x(): lax.ppermute(value, AXES, [(device(z, y, x + k, c), device(z, y, x, c)) f...]
    pallas_call x0 -> x10, Pallas kernels: none -> 22.9 us  [the longest x8 13.3 us: small_kernel(): pl.pallas_call(body, out_shape=out, in_specs=specs or [VM] * len(args), o...]
  transfers between devices with their start and end apart: 2 -> 20, of which waited for: 2 -> 10; matrix products, arithmetic and copies ran while one was open for 0% -> 0% of each run, Pallas kernels for 0% -> 4%
where the time goes in v4:
time: 161 us; the launch traced here: 160 us
  waiting for transfers between devices  45 us (28%)
  blocking collectives  32.2 us (20%)
  starting transfers between devices  31.8 us (20%)
  Pallas kernels  22.9 us (14%)
  between operations  14.2 us (9%)
  local copies, waits for them, and re-layouts  13.4 us (8%)
    all_to_all x3, blocking collectives, exchange(): lax.all_to_all(chunks, AXES, 0, 0, axis_index_groups=groups, tiled=True)  32.2 us
    ppermute x7, waiting for transfers between devices, from_y(): lax.ppermute(value, AXES, [(device(z, y + k, x, c), device(z, y, x, c)) f...  17.6 us
    all_to_all x1, waiting for transfers between devices, exchange(): lax.all_to_all(chunks, AXES, 0, 0, axis_index_groups=groups, tiled=True)  15.2 us
    pallas_call x8, Pallas kernels, small_kernel(): pl.pallas_call(body, out_shape=out, in_specs=specs or [VM] * len(args), o...  13.3 us
    unnamed x30, local copies, waits for them, and re-layouts  13.3 us
    ppermute x7, waiting for transfers between devices, from_x(): lax.ppermute(value, AXES, [(device(z, y, x + k, c), device(z, y, x, c)) f...  9.36 us
    ppermute x7, starting transfers between devices, from_x(): lax.ppermute(value, AXES, [(device(z, y, x + k, c), device(z, y, x, c)) f...  8.86 us
    all_to_all x1, starting transfers between devices, exchange(): lax.all_to_all(chunks, AXES, 0, 0, axis_index_groups=groups, tiled=True)  8.41 us
  transfers between devices with their start and end apart: 20, of which 10 were waited for; matrix products, arithmetic and copies ran while one was open for 0% of the time, Pallas kernels for 4%

profile of v4, /device:TPU:1, one launch (start us, length us, event | category | flops | bytes accessed | tf_op | source)
XLA Modules:
  0.0 159.8 jit_solution(4171725952447990489)
XLA Ops:
  7.2 0.0 all-gather.2.cloned.1.call-start
  7.2 1.1 copy-done.5
  8.3 0.7 copy-done.14
  9.0 0.9 prepare.1
  9.9 0.0 all-gather.2.cloned.1.call-update
  9.9 3.6 %collective-permute-start.3 = (bf16[40,2048]{1,0:T(8,128)(2,1)S(1)}, bf16[40,2048]{1,0:T(8,128)(2,1)S(1)}, u32[]{:S(2)}, u32[]{:S(2)}) collective-permute-start(bf16[40,2048]{1,0:T(8,128)(2,1)S(1)} %get-tuple-element.42), channel_id=1, source_target_pairs={{16,0},{24,8},{17,1},{25,9},{18,2},{26,10},{19,3},{27,11},{4,16},{... | collective-permute-start | bytes 491528 | tf_op jit(solution)/shard_map/ppermute | solution.py:51
  13.6 0.3 collective-permute-start.4
  13.9 0.7 collective-permute-start.5
  14.6 2.5 %collective-permute-start = (bf16[40,2176]{1,0:T(8,128)(2,1)S(1)}, bf16[40,2176]{1,0:T(8,128)(2,1)S(1)}, u32[]{:S(2)}, u32[]{:S(2)}) collective-permute-start(bf16[40,2176]{1,0:T(8,128)(2,1)S(1)} %get-tuple-element.41), channel_id=1, source_target_pairs={{1,0},{9,8},{2,1},{10,9},{3,2},{11,10},{0,3},{8,11},{17,16},{25,24... | collective-permute-start | bytes 522248 | tf_op jit(solution)/shard_map/ppermute | solution.py:45
  17.1 0.5 collective-permute-start.1
  17.6 0.7 collective-permute-done.3
  18.3 2.9 %collective-permute-start.2 = (bf16[40,2176]{1,0:T(8,128)(2,1)S(1)}, bf16[40,2176]{1,0:T(8,128)(2,1)S(1)}, u32[]{:S(2)}, u32[]{:S(2)}) collective-permute-start(bf16[40,2176]{1,0:T(8,128)(2,1)S(1)} %get-tuple-element.41), channel_id=1, source_target_pairs={{3,0},{11,8},{0,1},{8,9},{1,2},{9,10},{2,3},{10,11},{19,16},{27,24... | collective-permute-start | bytes 522248 | tf_op jit(solution)/shard_map/ppermute | solution.py:45
  21.2 3.5 %collective-permute-done.5 = bf16[40,2048]{1,0:T(8,128)(2,1)S(1)} collective-permute-done((bf16[40,2048]{1,0:T(8,128)(2,1)S(1)}, bf16[40,2048]{1,0:T(8,128)(2,1)S(1)}, u32[]{:S(2)}, u32[]{:S(2)}) %collective-permute-start.5) | collective-permute-done | bytes 163872 | tf_op jit(solution)/shard_map/ppermute | solution.py:51
  24.8 0.0 collective-permute-done
  24.8 0.0 collective-permute-done.1
  24.8 3.8 %collective-permute-done.2 = bf16[40,2176]{1,0:T(8,128)(2,1)S(1)} collective-permute-done((bf16[40,2176]{1,0:T(8,128)(2,1)S(1)}, bf16[40,2176]{1,0:T(8,128)(2,1)S(1)}, u32[]{:S(2)}, u32[]{:S(2)}) %collective-permute-start.2) | collective-permute-done | bytes 174112 | tf_op jit(solution)/shard_map/ppermute | solution.py:45
  28.6 0.1 pad_maximum_fusion.refs_1_
  28.7 1.0 collective-permute-start.6
  29.6 0.6 collective-permute-start.8
  30.2 0.4 collective-permute-start.10
  30.6 1.1 collective-permute-start.12
  31.7 13.3 %collective-permute-done.6.refs_2_ = bf16[160,2176]{1,0:T(8,128)(2,1)S(1)} collective-permute-done((bf16[160,2176]{1,0:T(8,128)(2,1)S(1)}, bf16[160,2176]{1,0:T(8,128)(2,1)S(1)}, u32[]{:S(2)}, u32[]{:S(2)}) %collective-permute-start.6) | collective-permute-done | bytes 696352 | tf_op jit(solution)/shard_map/ppermute | solution.py:51
  45.0 0.9 collective-permute-start.7
  46.0 0.7 collective-permute-start.9
  46.7 0.0 collective-permute-done.10.refs_7_
  46.7 0.3 collective-permute-start.11
  47.0 0.0 collective-permute-done.12.refs_10_
  47.0 0.8 copy-done.1
  47.9 1.3 collective-permute-start.13
  49.1 4.3 %collective-permute-done.11.refs_8_ = bf16[80,2048]{1,0:T(8,128)(2,1)S(1)} collective-permute-done((bf16[80,2048]{1,0:T(8,128)(2,1)S(1)}, bf16[80,2048]{1,0:T(8,128)(2,1)S(1)}, u32[]{:S(2)}, u32[]{:S(2)}) %collective-permute-start.11) | collective-permute-done | bytes 327712 | tf_op jit(solution)/shard_map/ppermute | solution.py:45
  53.4 0.7 copy-done.10
  54.1 1.3 collective-permute-done.13.refs_9_
  55.4 0.7 copy-done.12
  56.1 0.7 copy-done.6
  56.9 0.7 copy-done.8
  57.6 4.5 %collective-permute-start.14 = (bf16[320,4224]{1,0:T(8,128)(2,1)}, bf16[320,4224]{1,0:T(8,128)(2,1)S(1)}, u32[]{:S(2)}, u32[]{:S(2)}) collective-permute-start(bf16[320,4224]{1,0:T(8,128)(2,1)} %all-gather.2.cloned.1.call-done.refs_0_), channel_id=1, source_target_pairs={{8,0},{0,8},{9,1},{1,9},{10,2},{2,10},{11,3},{3,11},{24,16},{16,24... | collective-permute-start | bytes 8110088 | tf_op jit(solution)/shard_map/ppermute | solution.py:57
  62.1 1.8 %copy-done = bf16[320,4224]{1,0:T(8,128)(2,1)S(1)} copy-done((bf16[320,4224]{1,0:T(8,128)(2,1)S(1)}, bf16[320,4224]{1,0:T(8,128)(2,1)}, u32[]{:S(2)}) %copy-start) | copy-done | bytes 2703384
  63.9 1.1 copy-done.2
  65.0 1.0 copy-done.7
  66.0 1.0 copy-done.9
  67.0 1.0 copy-done.11
  67.9 1.0 copy-done.13
  68.9 5.8 %tile_mine.1 = (f32[640,320]{1,0:T(8,128)S(1)}, f32[32,352]{1,0:T(8,128)S(1)}, f32[32,320]{1,0:T(8,128)S(1)}, f32[32,640]{1,0:T(8,128)S(1)}, f32[32,32]{1,0:T(8,...) custom-call(bf16[320,4224]{1,0:T(8,128)(2,1)S(1)} %copy-done, ...), custom_call_target="tpu_custom_call" | custom-call | flops 1677721600 | bytes 7864320 | tf_op jit(solution)/shard_map/tile_mine/pallas_call | solution.py:314
  74.7 1.0 copy-done.3
  75.7 3.8 %tile_theirs.1 = (f32[640,320]{1,0:T(8,128)S(1)}, f32[32,352]{1,0:T(8,128)S(1)}, f32[32,320]{1,0:T(8,128)S(1)}) custom-call(bf16[320,4224]{1,0:T(8,128)(2,1)S(1)} %collective-permute-done.14.refs_0_, bf16[640,2176]{1,0:T(8,128)(2,1)S(1)} %get-tuple-element.57.refs_1_, bf16[640,2048]{1,0:T(8,128)(2,1)S(1)} %get-tuple-element.58.refs_2_, ...), custom_call_target="tpu_custom_call" | custom-call | flops 1677721600 | bytes 7864320 | tf_op jit(solution)/shard_map/tile_theirs/pallas_call | solution.py:336
  79.5 0.1 collective-permute-start.15
  79.6 1.2 collective-permute-done.15.b_ref
  80.8 0.8 share.1
  81.6 8.4 %all-to-all-start = ((f32[8,32,352]{2,1,0:T(8,128)}), f32[8,32,352]{2,1,0:T(8,128)S(1)}, u32[]{:S(2)}, u32[]{:S(2)}) async-start(f32[8,32,352]{2,1,0:T(8,128)} %share.1), calls=%async_computation | async-start | bytes 786432 | tf_op jit(solution)/shard_map/all_to_all | solution.py:63
  90.0 15.2 %all-to-all-done.part_ref = f32[8,32,352]{2,1,0:T(8,128)S(1)} async-done(((f32[8,32,352]{2,1,0:T(8,128)}), f32[8,32,352]{2,1,0:T(8,128)S(1)}, u32[]{:S(2)}, u32[]{:S(2)}) %all-to-all-start) | async-done | bytes 360480 | tf_op jit(solution)/shard_map/all_to_all | solution.py:63
  105.2 0.3 line.1
  105.5 0.5 collective-permute-start.16
  106.0 0.1 pad_add_fusion.at_ref
  106.1 0.8 collective-permute-done.16.far_ref.refs_3_
  106.9 1.1 spread.1
  108.0 12.2 %all_to_all.20.refs_0_ = f32[16,32,104]{2,1,0:T(8,128)S(1)} all-to-all(f32[16,32,104]{2,1,0:T(8,128)S(1)} %spread.1), channel_id=1, replica_groups={{0,1,2,3,16,17,18,19,4,5,6,7,20,21,22,23},{8,9,10,11,24,25,26,27,12,13,..., dimensions={0} | all-to-all | bytes 425984 | tf_op jit(solution)/shard_map/all_to_all | solution.py:63
  120.3 6.3 %step.1 = (f32[32,320]{1,0:T(8,128)S(1)}, f32[32,352]{1,0:T(8,128)S(1)}, f32[32,40]{1,0:T(8,128)S(1)}, f32[32,40]{1,0:T(8,128)S(1)}, f32[32,40]{1,0:T(8,128)S(1)}, /*index=5*/f32[32,32]{1,0:T(8,128)S(1)}) custom-call(s32[3]{0:T(128)S(1)} %pad_add_fusion.at_ref, f32[16,32,104]{2,1,0:T(8,128)S(1)} %all_to_all.20.refs_0_, ...), custom_call_target="tpu_custom_call" | custom-call | tf_op jit(solution)/shard_map/step/pallas_call | solution.py:81
  126.6 1.6 collective-permute-start.17
  128.2 0.9 collective-permute-done.17.far_ref
  129.0 0.1 chunk.1
  129.2 10.8 %all_to_all.21.got_ref = f32[8,32,72]{2,1,0:T(8,128)S(1)} all-to-all(f32[8,32,72]{2,1,0:T(8,128)S(1)} %chunk.1), channel_id=1, replica_groups={{0,32,64,96,128,160,192,224},{8,40,72,104,136,168,200,232},{1,33,65,97,..., dimensions={0} | all-to-all | bytes 147456 | tf_op jit(solution)/shard_map/all_to_all | solution.py:63
  140.0 0.1 image.1
  140.1 9.1 %all_to_all.22.got_ref = f32[16,8,128]{2,1,0:T(8,128)S(1)} all-to-all(f32[16,8,128]{2,1,0:T(8,128)S(1)} %get-tuple-element.71), channel_id=1, replica_groups={{0,1,2,3,16,17,18,19,4,5,6,7,20,21,22,23},{8,9,10,11,24,25,26,27,12,13,..., dimensions={0} | all-to-all | bytes 131072 | tf_op jit(solution)/shard_map/all_to_all | solution.py:63
  149.2 3.7 %last.1 = (f32[32,40]{1,0:T(8,128)}, f32[32,40]{1,0:T(8,128)}) custom-call(f32[16,8,128]{2,1,0:T(8,128)S(1)} %all_to_all.22.got_ref, f32[32,32]{1,0:T(8,128)S(1)} %get-tuple-element.72.rr, f32[32,40]{1,0:T(8,128)S(1)} %get-tuple-element.70.d_ref.d_own, f32[32,40]{1,0:T(8,128)S(1)} %get-tuple-element.73.image, f32[32,40]{1,0:T(8,128)S(1)} %get-tuple-element.74.weights, ...), custom_call_target="tpu_custom_call" | custom-call | tf_op jit(solution)/shard_map/last/pallas_call | solution.py:81
  (27 shorter events, 0.2 us)
Async XLA Ops:
  7.2 50.5 %all-gather.2.cloned.1.call-start = ((), (), s32[]{:S(2)}) async-start(), calls=%async_computation.4 | async-start | bytes 3041280 | tf_op jit(solution)/shard_map/all_gather | solution.py:297
  7.2 1.1 copy-start.5
  8.3 0.7 copy-start.14
  9.9 8.4 %collective-permute-start.3 = (bf16[40,2048]{1,0:T(8,128)(2,1)S(1)}, bf16[40,2048]{1,0:T(8,128)(2,1)S(1)}, u32[]{:S(2)}, u32[]{:S(2)}) collective-permute-start(bf16[40,2048]{1,0:T(8,128)(2,1)S(1)} %get-tuple-element.42), channel_id=1, source_target_pairs={{16,0},{24,8},{17,1},{25,9},{18,2},{26,10},{19,3},{27,11},{4,16},{... | collective-permute-start | bytes 491528 | tf_op jit(solution)/shard_map/ppermute | solution.py:51
  13.6 7.6 %collective-permute-start.4 = (bf16[40,2048]{1,0:T(8,128)(2,1)S(1)}, bf16[40,2048]{1,0:T(8,128)(2,1)S(1)}, u32[]{:S(2)}, u32[]{:S(2)}) collective-permute-start(bf16[40,2048]{1,0:T(8,128)(2,1)S(1)} %get-tuple-element.42), channel_id=1, source_target_pairs={{4,0},{12,8},{5,1},{13,9},{6,2},{14,10},{7,3},{15,11},{20,16},{28,... | collective-permute-start | bytes 491528 | tf_op jit(solution)/shard_map/ppermute | solution.py:51
  13.9 10.8 %collective-permute-start.5 = (bf16[40,2048]{1,0:T(8,128)(2,1)S(1)}, bf16[40,2048]{1,0:T(8,128)(2,1)S(1)}, u32[]{:S(2)}, u32[]{:S(2)}) collective-permute-start(bf16[40,2048]{1,0:T(8,128)(2,1)S(1)} %get-tuple-element.42), channel_id=1, source_target_pairs={{20,0},{28,8},{21,1},{29,9},{22,2},{30,10},{23,3},{31,11},{0,16},{... | collective-permute-start | bytes 491528 | tf_op jit(solution)/shard_map/ppermute | solution.py:51
  14.6 10.1 %collective-permute-start = (bf16[40,2176]{1,0:T(8,128)(2,1)S(1)}, bf16[40,2176]{1,0:T(8,128)(2,1)S(1)}, u32[]{:S(2)}, u32[]{:S(2)}) collective-permute-start(bf16[40,2176]{1,0:T(8,128)(2,1)S(1)} %get-tuple-element.41), channel_id=1, source_target_pairs={{1,0},{9,8},{2,1},{10,9},{3,2},{11,10},{0,3},{8,11},{17,16},{25,24... | collective-permute-start | bytes 522248 | tf_op jit(solution)/shard_map/ppermute | solution.py:45
  17.1 7.7 %collective-permute-start.1 = (bf16[40,2176]{1,0:T(8,128)(2,1)S(1)}, bf16[40,2176]{1,0:T(8,128)(2,1)S(1)}, u32[]{:S(2)}, u32[]{:S(2)}) collective-permute-start(bf16[40,2176]{1,0:T(8,128)(2,1)S(1)} %get-tuple-element.41), channel_id=1, source_target_pairs={{2,0},{10,8},{3,1},{11,9},{0,2},{8,10},{1,3},{9,11},{18,16},{26,24... | collective-permute-start | bytes 522248 | tf_op jit(solution)/shard_map/ppermute | solution.py:45
  18.3 10.3 %collective-permute-start.2 = (bf16[40,2176]{1,0:T(8,128)(2,1)S(1)}, bf16[40,2176]{1,0:T(8,128)(2,1)S(1)}, u32[]{:S(2)}, u32[]{:S(2)}) collective-permute-start(bf16[40,2176]{1,0:T(8,128)(2,1)S(1)} %get-tuple-element.41), channel_id=1, source_target_pairs={{3,0},{11,8},{0,1},{8,9},{1,2},{9,10},{2,3},{10,11},{19,16},{27,24... | collective-permute-start | bytes 522248 | tf_op jit(solution)/shard_map/ppermute | solution.py:45
  28.7 16.3 %collective-permute-start.6 = (bf16[160,2176]{1,0:T(8,128)(2,1)S(1)}, bf16[160,2176]{1,0:T(8,128)(2,1)S(1)}, u32[]{:S(2)}, u32[]{:S(2)}) collective-permute-start(bf16[160,2176]{1,0:T(8,128)(2,1)S(1)} %pad_maximum_fusion.refs_1_), channel_id=1, source_target_pairs={{16,0},{24,8},{17,1},{25,9},{18,2},{26,10},{19,3},{27,11},{4,16},{... | collective-permute-start | bytes 2088968 | tf_op jit(solution)/shard_map/ppermute | solution.py:51
  29.6 16.3 %collective-permute-start.8 = (bf16[160,2176]{1,0:T(8,128)(2,1)S(1)}, bf16[160,2176]{1,0:T(8,128)(2,1)S(1)}, u32[]{:S(2)}, u32[]{:S(2)}) collective-permute-start(bf16[160,2176]{1,0:T(8,128)(2,1)S(1)} %pad_maximum_fusion.refs_1_), channel_id=1, source_target_pairs={{20,0},{28,8},{21,1},{29,9},{22,2},{30,10},{23,3},{31,11},{0,16},{... | collective-permute-start | bytes 2088968 | tf_op jit(solution)/shard_map/ppermute | solution.py:51
  30.2 16.5 %collective-permute-start.10 = (bf16[160,2048]{1,0:T(8,128)(2,1)S(1)}, bf16[160,2048]{1,0:T(8,128)(2,1)S(1)}, u32[]{:S(2)}, u32[]{:S(2)}) collective-permute-start(bf16[160,2048]{1,0:T(8,128)(2,1)S(1)} %pad_maximum_fusion.1.refs_6_), channel_id=1, source_target_pairs={{1,0},{9,8},{2,1},{10,9},{3,2},{11,10},{0,3},{8,11},{17,16},{25,24... | collective-permute-start | bytes 1966088 | tf_op jit(solution)/shard_map/ppermute | solution.py:45
  30.6 16.4 %collective-permute-start.12 = (bf16[160,2048]{1,0:T(8,128)(2,1)S(1)}, bf16[160,2048]{1,0:T(8,128)(2,1)S(1)}, u32[]{:S(2)}, u32[]{:S(2)}) collective-permute-start(bf16[160,2048]{1,0:T(8,128)(2,1)S(1)} %pad_maximum_fusion.1.refs_6_), channel_id=1, source_target_pairs={{3,0},{11,8},{0,1},{8,9},{1,2},{9,10},{2,3},{10,11},{19,16},{27,24... | collective-permute-start | bytes 1966088 | tf_op jit(solution)/shard_map/ppermute | solution.py:45
  45.0 11.1 %collective-permute-start.7 = (bf16[80,2176]{1,0:T(8,128)(2,1)S(1)}, bf16[80,2176]{1,0:T(8,128)(2,1)S(1)}, u32[]{:S(2)}, u32[]{:S(2)}) collective-permute-start(bf16[80,2176]{1,0:T(8,128)(2,1)S(1)} %slice.16), channel_id=1, source_target_pairs={{16,0},{24,8},{17,1},{25,9},{18,2},{26,10},{19,3},{27,11},{4,16},{... | collective-permute-start | bytes 1044488 | tf_op jit(solution)/shard_map/ppermute | solution.py:51
  46.0 10.9 %collective-permute-start.9 = (bf16[80,2176]{1,0:T(8,128)(2,1)S(1)}, bf16[80,2176]{1,0:T(8,128)(2,1)S(1)}, u32[]{:S(2)}, u32[]{:S(2)}) collective-permute-start(bf16[80,2176]{1,0:T(8,128)(2,1)S(1)} %slice.17), channel_id=1, source_target_pairs={{20,0},{28,8},{21,1},{29,9},{22,2},{30,10},{23,3},{31,11},{0,16},{... | collective-permute-start | bytes 1044488 | tf_op jit(solution)/shard_map/ppermute | solution.py:51
  46.7 6.7 %collective-permute-start.11 = (bf16[80,2048]{1,0:T(8,128)(2,1)S(1)}, bf16[80,2048]{1,0:T(8,128)(2,1)S(1)}, u32[]{:S(2)}, u32[]{:S(2)}) collective-permute-start(bf16[80,2048]{1,0:T(8,128)(2,1)S(1)} %slice.18), channel_id=1, source_target_pairs={{1,0},{9,8},{2,1},{10,9},{3,2},{11,10},{0,3},{8,11},{17,16},{25,24... | collective-permute-start | bytes 983048 | tf_op jit(solution)/shard_map/ppermute | solution.py:45
  47.0 0.8 copy-start.1
  47.9 7.5 %collective-permute-start.13 = (bf16[80,2048]{1,0:T(8,128)(2,1)S(1)}, bf16[80,2048]{1,0:T(8,128)(2,1)S(1)}, u32[]{:S(2)}, u32[]{:S(2)}) collective-permute-start(bf16[80,2048]{1,0:T(8,128)(2,1)S(1)} %slice.19), channel_id=1, source_target_pairs={{3,0},{11,8},{0,1},{8,9},{1,2},{9,10},{2,3},{10,11},{19,16},{27,24... | collective-permute-start | bytes 983048 | tf_op jit(solution)/shard_map/ppermute | solution.py:45
  53.4 0.7 copy-start.10
  55.4 0.7 copy-start.12
  56.1 0.7 copy-start.6
  56.9 0.8 copy-start.8
  57.6 18.1 %collective-permute-start.14 = (bf16[320,4224]{1,0:T(8,128)(2,1)}, bf16[320,4224]{1,0:T(8,128)(2,1)S(1)}, u32[]{:S(2)}, u32[]{:S(2)}) collective-permute-start(bf16[320,4224]{1,0:T(8,128)(2,1)} %all-gather.2.cloned.1.call-done.refs_0_), channel_id=1, source_target_pairs={{8,0},{0,8},{9,1},{1,9},{10,2},{2,10},{11,3},{3,11},{24,16},{16,24... | collective-permute-start | bytes 8110088 | tf_op jit(solution)/shard_map/ppermute | solution.py:57
  62.1 1.8 %copy-start = (bf16[320,4224]{1,0:T(8,128)(2,1)S(1)}, bf16[320,4224]{1,0:T(8,128)(2,1)}, u32[]{:S(2)}) copy-start(bf16[320,4224]{1,0:T(8,128)(2,1)} %all-gather.2.cloned.1.call-done.refs_0_) | copy-start | bytes 8110084
  63.9 1.1 copy-start.2
  65.0 1.0 copy-start.7
  66.0 1.0 copy-start.9
  66.9 1.0 copy-start.11
  67.9 1.0 copy-start.13
  74.7 1.0 copy-start.3
  79.5 40.8 %copy-start.4 = (f32[640,320]{1,0:T(8,128)S(1)}, f32[640,320]{1,0:T(8,128)}, u32[]{:S(2)}) copy-start(f32[640,320]{1,0:T(8,128)} %copy-done.3) | copy-start | bytes 2457604
  79.5 1.3 collective-permute-start.15
  81.6 23.6 %all-to-all-start = ((f32[8,32,352]{2,1,0:T(8,128)}), f32[8,32,352]{2,1,0:T(8,128)S(1)}, u32[]{:S(2)}, u32[]{:S(2)}) async-start(f32[8,32,352]{2,1,0:T(8,128)} %share.1), calls=%async_computation | async-start | bytes 786432 | tf_op jit(solution)/shard_map/all_to_all | solution.py:63
  105.5 1.4 collective-permute-start.16
  126.6 2.5 %collective-permute-start.17 = (f32[32,352]{1,0:T(8,128)S(1)}, f32[32,352]{1,0:T(8,128)S(1)}, u32[]{:S(2)}, u32[]{:S(2)}) collective-permute-start(f32[32,352]{1,0:T(8,128)S(1)} %get-tuple-element.69.here_ref), channel_id=1, source_target_pairs={{8,0},{0,8},{9,1},{1,9},{10,2},{2,10},{11,3},{3,11},{24,16},{16,24... | collective-permute-start | bytes 135176 | tf_op jit(solution)/shard_map/ppermute | solution.py:57
Sparse Core Ops, SparseCore 0:
  10.1 44.0 all-gather.1

commit v5 on v4

--- a/solution.py
+++ b/solution.py
@@ -17,7 +17,7 @@
 BF16 = jnp.bfloat16
 VM = pl.BlockSpec(memory_space=pltpu.VMEM)
 SM = pl.BlockSpec(memory_space=pltpu.SMEM)
-ANY = pl.BlockSpec(memory_space=pl.ANY)
+HBM = pl.BlockSpec(memory_space=pltpu.HBM)
 
 
 def device(z, y, x, c):
@@ -33,6 +33,11 @@
     for y in range(NY)
     for x in range(NX)
     for c in range(NC)
+]
+TUBES = [
+    [device(z, y, x, c) for c in range(NC) for z in range(NZ)]
+    for y in range(NY)
+    for x in range(NX)
 ]
 PLANES = [
     [device(z, y, x, c) for y in range(NY) for x in range(NX)]
@@ -89,7 +94,15 @@
     )(*args)
 
 
-def prepare_kernel(half, s_ref, t_ref, all_ref, first_ref, second_ref):
+def prepare_kernel(half, s_hbm, t_hbm, all_ref, first_ref, second_ref, s_ref, t_ref, sems):
+    copies = [
+        pltpu.make_async_copy(t_hbm, t_ref, sems.at[1]),
+        pltpu.make_async_copy(s_hbm, s_ref, sems.at[0]),
+    ]
+    for copy in copies:
+        copy.start()
+    for copy in copies:
+        copy.wait()
     sketches = s_ref[...]
     scale = jnp.sqrt(jnp.sum(sketches * sketches, axis=1, keepdims=True) + 1e-06)
     units = (sketches / scale).astype(BF16)
@@ -105,61 +118,85 @@
     second_ref[...] = units[:, half:]
 
 
-def tile_body(rows, rhs, half, x_ref, a_ref, b_ref, cos_ref, k_ref):
+def spans(rows):
+    side = 4 * rows
+    return [
+        pl.ds(at, size)
+        for at, size in (
+            (0, side),
+            (side, side),
+            (2 * side, side // 2),
+            (5 * side // 2, side // 2),
+            (3 * side, side),
+        )
+    ]
+
+
+def targets_of(terms, rhs):
+    terms = terms.astype(F32).T
+    return terms[:rhs] + terms[rhs : 2 * rhs] + terms[2 * rhs : 3 * rhs]
+
+
+def tile_kernel(rows, rhs, half, at_ref, *refs):
+    x_hbm, a_hbm, b_hbm = refs[0], refs[1:6], refs[6:11]
+    k_ref, near_ref, far_ref, tx_ref, ty_ref, n0_ref = refs[11:17]
+    x_ref, a_ref, b_ref, cos_ref, sems = refs[17:]
+    line, quarter = 8 * rows, half // 2
     dims = (((1,), (1,)), ((), ()))
-    k_ref[...] = lax.dot_general(
-        a_ref[:, :half], x_ref[:, :half], dims, preferred_element_type=F32
-    )
-    cos_ref[...] = lax.dot_general(
-        b_ref[...], x_ref[:, half : 2 * half], dims, preferred_element_type=F32
-    )
+    plans = (
+        (0, quarter, a_hbm, a_ref, 0, quarter),
+        (quarter, quarter, a_hbm, a_ref, quarter, quarter + PAD),
+        (half, quarter, b_hbm, b_ref, 0, quarter),
+        (half + quarter, quarter + PAD, b_hbm, b_ref, quarter, quarter),
+    )
+    groups = []
+    for i, (at_x, wide_x, pieces, ref, at_y, wide_y) in enumerate(plans):
+        group = []
+        of_x, of_y = pl.ds(at_x, wide_x), pl.ds(at_y, wide_y)
+        for core in range(NC):
+            of = pl.multiple_of(lax.rem(at_ref[3] + core, NC) * line, line)
+            copy = pltpu.make_async_copy(
+                x_hbm.at[pl.ds(of, line), of_x],
+                x_ref.at[pl.ds(core * line, line), of_x],
+                sems.at[i, core],
+            )
+            group.append(copy)
+        for n, (to, piece) in enumerate(zip(spans(rows), pieces)):
+            group.append(
+                pltpu.make_async_copy(piece.at[:, of_y], ref.at[to, of_y], sems.at[i, NC + n])
+            )
+        groups.append(group)
+        for copy in group:
+            copy.start()
+    for i, (at_x, _, _, ref, at_y, _) in enumerate(plans):
+        for copy in groups[i]:
+            copy.wait()
+        product = lax.dot_general(
+            ref[:, at_y : at_y + quarter],
+            x_ref[:, at_x : at_x + quarter],
+            dims,
+            preferred_element_type=F32,
+        )
+        to = k_ref if i < 2 else cos_ref
+        if i % 2:
+            to[...] += product
+        else:
+            to[...] = product
+        if i == 1:
+            ty = targets_of(a_ref[:, half:], rhs)
+            ty_ref[...] = ty
+            n0 = nt(ty, ty)
+            n0_ref[...] = n0
+            near_ref[:, line:] = n0
+            far_ref[:, line:] = n0
     for y in range(4):
         for x in range(4):
             to, of = pl.ds((4 * y + x) * rows, rows), pl.ds((4 * x + y) * rows, rows)
             k_ref[to, :] = jnp.exp(sharpness * (k_ref[to, :] + cos_ref[of, :] - 1.0))
-
-
-def targets_of(terms, rhs):
-    terms = terms.astype(F32).T
-    return terms[:rhs] + terms[rhs : 2 * rhs] + terms[2 * rhs : 3 * rhs]
-
-
-def mine_kernel(rows, rhs, half, *refs):
-    x_hbm, a_hbm, b_hbm = refs[0], refs[1:6], refs[6:11]
-    k_ref, p_ref, tx_ref, ty_ref, n0_ref, a_ref, b_ref = refs[11:18]
-    x_ref, cos_ref, sems = refs[18:]
-    side, line = 4 * rows, 8 * rows
-    places = [(0, side), (side, side), (2 * side, side // 2)]
-    places += [(5 * side // 2, side // 2), (3 * side, side)]
-    copies = [pltpu.make_async_copy(x_hbm, x_ref, sems.at[0])]
-    for i, (at, size) in enumerate(places):
-        to = pl.ds(at, size)
-        copies.append(pltpu.make_async_copy(a_hbm[i], a_ref.at[to], sems.at[1 + 2 * i]))
-        copies.append(pltpu.make_async_copy(b_hbm[i], b_ref.at[to], sems.at[2 + 2 * i]))
-    for copy in copies:
-        copy.start()
-    for copy in copies:
-        copy.wait()
-    tile_body(rows, rhs, half, x_ref, a_ref, b_ref, cos_ref, k_ref)
     tx_ref[...] = targets_of(x_ref[:, 2 * half :], rhs)
-    ty = targets_of(a_ref[:, half:], rhs)
-    ty_ref[...] = ty
-    n0 = nt(ty, ty)
-    n0_ref[...] = n0
-    p_ref[:, :line] = mm(ty, k_ref[...])
-    p_ref[:, line:] = n0
-
-
-def theirs_kernel(rows, rhs, half, *refs):
-    x_hbm, a_ref, b_ref, ty_ref, n0_ref, k_ref, p_ref, tx_ref, x_ref, cos_ref, sem = refs
-    line = 8 * rows
-    copy = pltpu.make_async_copy(x_hbm, x_ref, sem)
-    copy.start()
-    copy.wait()
-    tile_body(rows, rhs, half, x_ref, a_ref, b_ref, cos_ref, k_ref)
-    tx_ref[...] = targets_of(x_ref[:, 2 * half :], rhs)
-    p_ref[:, :line] = mm(ty_ref[...], k_ref[...])
-    p_ref[:, line:] = n0_ref[...]
+    product = mm(ty_ref[...], k_ref[...])
+    near_ref[:, :line] = product[:, :line]
+    far_ref[:, :line] = product[:, line:]
 
 
 def share_kernel(count, a_ref, b_ref, out_ref):
@@ -171,7 +208,7 @@
 def line_kernel(line, part_ref, t_ref, send_ref, n0_ref):
     part = jnp.sum(part_ref[...], axis=0)
     rhs = part.shape[0]
-    t = t_ref[...]
+    t = t_ref[:, :line]
     w = part[:, :line] - t
     n0_ref[...] = part[:, line:]
     send_ref[:, :line] = w
@@ -194,13 +231,25 @@
     row = lax.broadcasted_iota(jnp.int32, (size, size), 0)
     col = lax.broadcasted_iota(jnp.int32, (size, size), 1)
     pairs = list(pairs)
-    for k in range(size):
-        for n, (m, c) in enumerate(pairs):
-            column = jnp.broadcast_to(m[:, k : k + 1], (size, size))
-            inverse = 1.0 / column[k : k + 1, :]
-            column = jnp.where(row == k, 0.0, column)
-            m_row, c_row = m[k : k + 1, :] * inverse, c[k : k + 1, :] * inverse
-            pairs[n] = m - column * m_row, c - column * c_row
+    block = 8
+    for start in range(0, size, block):
+        panels = [
+            [
+                jnp.broadcast_to(m[:, start + j : start + j + 1], (size, size))
+                for j in range(block)
+            ]
+            for m, _ in pairs
+        ]
+        for j in range(block):
+            k = start + j
+            for n, (m, c) in enumerate(pairs):
+                panel = panels[n]
+                inverse = 1.0 / panel[j][k : k + 1, :]
+                column = jnp.where(row == k, 0.0, panel[j])
+                m_row, c_row = m[k : k + 1, :] * inverse, c[k : k + 1, :] * inverse
+                pairs[n] = m - column * m_row, c - column * c_row
+                for i in range(j + 1, block):
+                    panel[i] = panel[i] - column * (panel[i][k : k + 1, :] * inverse)
     return [
         c / jnp.sum(jnp.where(row == col, m, 0.0), axis=1, keepdims=True) for m, c in pairs
     ]
@@ -211,8 +260,8 @@
 
 
 def step_kernel(rows, rhs, line, at_ref, *refs):
-    got_ref, n0_ref, w_line, w_far, t_line, t_far, t_plane, k_mine, k_far = refs[:9]
-    near_ref, far_ref, d_ref, weights_ref, residual_ref, rr_ref, w_ref = refs[9:]
+    got_ref, n0_ref, w_line, w_far, t_tube, t_plane, k_ref = refs[:7]
+    near_ref, far_ref, d_ref, weights_ref, residual_ref, rr_ref, w_ref = refs[7:]
     got = jnp.sum(got_ref[...], axis=0)
     n0 = symmetric(n0_ref[...])
     n1, n2 = got[:, rows : rows + rhs], got[:, rows + rhs : rows + 2 * rhs]
@@ -234,10 +283,10 @@
     rr1 = mm(qt, mm(n0, q)) - cross - cross.T + mm(a1t, mm(n2, a1))
     mix = qt + mm(n0_inverse, rr1).T
     d_plane = mm(mix, t_plane[...]) - mm(a1t, w_ref[...])
-    near = mm(d_plane, k_mine[...])
-    far = mm(d_plane, k_far[...])
-    d_line = mm(mix, t_line[...]) - mm(a1t, w_line[:, :line])
-    d_far = mm(mix, t_far[...]) - mm(a1t, w_far[:, :line])
+    product = mm(d_plane, k_ref[...])
+    near, far = product[:, :line], product[:, line:]
+    d_line = mm(mix, t_tube[:, :line]) - mm(a1t, w_line[:, :line])
+    d_far = mm(mix, t_tube[:, line:]) - mm(a1t, w_far[:, :line])
     d_own, t_own = d_plane[:, :rows], t_plane[:, :rows]
     near_ref[...] = near
     far_ref[:, :line] = far
@@ -281,7 +330,8 @@
     z = lax.axis_index("row") // 4
     y = lax.axis_index("row") // 2 % 2 + 2 * (lax.axis_index("col") // NX)
     x = lax.axis_index("col") % NX
-    at = jnp.stack([z, y, x]).astype(jnp.int32)
+    c = lax.axis_index("row") % NC
+    at = jnp.stack([z, y, x, c]).astype(jnp.int32)
     sizes = (rows, rhs, half)
 
     units, first, second = small_kernel(
@@ -292,9 +342,15 @@
             shape(rows, half, dtype=BF16),
         ),
         (sketches, targets.T),
+        [HBM] * 2,
+        scratch=[
+            pltpu.VMEM((rows, 2 * half), F32),
+            pltpu.VMEM((rhs, rows), F32),
+            pltpu.SemaphoreType.DMA((2,)),
+        ],
         name="prepare",
     )
-    mine = lax.all_gather(units, AXES, axis=0, tiled=True, axis_index_groups=LINES)
+    tube = lax.all_gather(units, AXES, axis=0, tiled=True, axis_index_groups=TUBES)
     a = jnp.concatenate([first] + [from_x(first, k) for k in range(1, NX)], axis=0)
     b = jnp.concatenate([second] + [from_y(second, k) for k in range(1, NY)], axis=0)
     a, b = lax.optimization_barrier((a, b))
@@ -302,51 +358,34 @@
     top = 2 * rows
     a2, b2 = from_y(a1[:top], 1), from_x(b1[:top], 1)
     a2_low, b2_low = from_y(a3[top:], 3), from_x(b3[top:], 3)
-    mine, a, b = lax.optimization_barrier(
-        (mine, (a, a1, a2, a2_low, a3), (b, b1, b2, b2_low, b3))
-    )
-    theirs = other_core(mine)
-    cost = pl.CostEstimate(
-        flops=4 * plane * line * half,
-        bytes_accessed=2 * (plane + line) * 2 * half,
-        transcendentals=plane * line,
-    )
-    k_mine, near, t_line, t_plane, n0, y_first, y_second = pl.pallas_call(
-        functools.partial(mine_kernel, *sizes),
+    a, b = (a, a1, a2, a2_low, a3), (b, b1, b2, b2_low, b3)
+    k, near, far, t_tube, t_plane, n0 = pl.pallas_call(
+        functools.partial(tile_kernel, *sizes),
         out_shape=(
-            shape(plane, line),
+            shape(plane, NC * line),
             shape(rhs, line + rhs),
-            shape(rhs, line),
+            shape(rhs, line + rhs),
+            shape(rhs, NC * line),
             shape(rhs, plane),
             shape(rhs, rhs),
-            shape(plane, half + PAD, dtype=BF16),
-            shape(plane, half, dtype=BF16),
         ),
-        in_specs=[ANY] * 11,
-        out_specs=[VM] * 7,
+        in_specs=[SM] + [HBM] * 11,
+        out_specs=[VM] * 6,
         scratch_shapes=[
-            pltpu.VMEM((line, 2 * half + PAD), BF16),
-            pltpu.VMEM((plane, line), F32),
-            pltpu.SemaphoreType.DMA((11,)),
+            pltpu.VMEM((NC * line, 2 * half + PAD), BF16),
+            pltpu.VMEM((plane, half + PAD), BF16),
+            pltpu.VMEM((plane, half), BF16),
+            pltpu.VMEM((plane, NC * line), F32),
+            pltpu.SemaphoreType.DMA((4, NC + 5)),
         ],
-        compiler_params=pltpu.CompilerParams(vmem_limit_bytes=20 * MIB),
-        cost_estimate=cost,
-        name="tile_mine",
-    )(mine, *a, *b)
-    k_far, far, t_far = pl.pallas_call(
-        functools.partial(theirs_kernel, *sizes),
-        out_shape=(shape(plane, line), shape(rhs, line + rhs), shape(rhs, line)),
-        in_specs=[ANY] + [VM] * 4,
-        out_specs=[VM] * 3,
-        scratch_shapes=[
-            pltpu.VMEM((line, 2 * half + PAD), BF16),
-            pltpu.VMEM((plane, line), F32),
-            pltpu.SemaphoreType.DMA,
-        ],
-        compiler_params=pltpu.CompilerParams(vmem_limit_bytes=20 * MIB),
-        cost_estimate=cost,
-        name="tile_theirs",
-    )(theirs, y_first, y_second, t_plane, n0)
+        compiler_params=pltpu.CompilerParams(vmem_limit_bytes=60 * MIB),
+        cost_estimate=pl.CostEstimate(
+            flops=4 * plane * NC * line * 2 * half,
+            bytes_accessed=2 * (plane + NC * line) * 2 * half,
+            transcendentals=plane * NC * line,
+        ),
+        name="tile",
+    )(at, tube, *a, *b)
 
     copies = small_kernel(
         functools.partial(share_kernel, NZ),
@@ -357,7 +396,7 @@
     sent, n0 = small_kernel(
         functools.partial(line_kernel, line),
         (shape(rhs, line + 2 * rhs), shape(rhs, rhs)),
-        (exchange(copies, LINES), t_line),
+        (exchange(copies, LINES), t_tube),
         name="line",
     )
     received = other_core(sent)
@@ -370,12 +409,12 @@
     )
     got = exchange(copies, PLANES)
     own = shape(rhs, rows)
-    values = (at, got, n0, sent, received, t_line, t_far, t_plane, k_mine, k_far)
+    values = (at, got, n0, sent, received, t_tube, t_plane, k)
     near, far, d_own, weights, residual, rr1 = small_kernel(
         functools.partial(step_kernel, rows, rhs, line),
         (shape(rhs, line), shape(rhs, line + rhs), own, own, own, shape(rhs, rhs)),
         values,
-        [SM] + [VM] * 9,
+        [SM] + [VM] * 7,
         limit=16,
         scratch=[pltpu.VMEM((rhs, plane), F32)],
         name="step",

time: 161 us -> 147 us (0.913)
  blocking collectives: 32.2 us -> 53.1 us
  waiting for transfers between devices: 45 us -> 26.2 us
  local copies, waits for them, and re-layouts: 13.4 us -> 4.16 us
  Pallas kernels: 22.9 us -> 19.2 us
  starting transfers between devices: 31.8 us -> 28.4 us
    all_to_all x3 -> x4, blocking collectives: 32.2 us -> 53.1 us  [exchange(): lax.all_to_all(chunks, AXES, 0, 0, axis_index_groups=groups, tiled=True)]
    all_to_all x1 -> x0, waiting for transfers between devices: 15.2 us -> none  [exchange(): lax.all_to_all(chunks, AXES, 0, 0, axis_index_groups=groups, tiled=True)]
    unnamed x30, local copies, waits for them, and re-layouts: 13.3 us -> 4.07 us
    all_to_all x1 -> x0, starting transfers between devices: 8.41 us -> none  [exchange(): lax.all_to_all(chunks, AXES, 0, 0, axis_index_groups=groups, tiled=True)]
    ppermute x7, waiting for transfers between devices: 17.6 us -> 11.4 us  [from_y(): lax.ppermute(value, AXES, [(device(z, y + k, x, c), device(z, y, x, c)) f...]
    pallas_call x8, Pallas kernels: 13.3 us -> 9.02 us  [small_kernel(): pl.pallas_call(body, out_shape=out, in_specs=specs or [VM] * len(args), o...]
    ppermute x7, starting transfers between devices: 7.85 us -> 11.4 us  [from_y(): lax.ppermute(value, AXES, [(device(z, y + k, x, c), device(z, y, x, c)) f...]
    ppermute x7, starting transfers between devices: 8.86 us -> 12.1 us  [from_x(): lax.ppermute(value, AXES, [(device(z, y, x + k, c), device(z, y, x, c)) f...]
  transfers between devices with their start and end apart: 20 -> 18, of which waited for: 10 -> 9; matrix products, arithmetic and copies ran while one was open for 0% -> 1% of each run, Pallas kernels for 4% -> 0%
where the time goes in v5:
time: 147 us; the launch traced here: 146 us
  blocking collectives  53.1 us (36%)
  starting transfers between devices  28.4 us (19%)
  waiting for transfers between devices  26.2 us (18%)
  Pallas kernels  19.2 us (13%)
  between operations  14.2 us (10%)
  local copies, waits for them, and re-layouts  4.16 us (3%)
    all_to_all x4, blocking collectives, exchange(): lax.all_to_all(chunks, AXES, 0, 0, axis_index_groups=groups, tiled=True)  53.1 us
    ppermute x7, starting transfers between devices, from_x(): lax.ppermute(value, AXES, [(device(z, y, x + k, c), device(z, y, x, c)) f...  12.1 us
    ppermute x7, starting transfers between devices, from_y(): lax.ppermute(value, AXES, [(device(z, y + k, x, c), device(z, y, x, c)) f...  11.4 us
    ppermute x7, waiting for transfers between devices, from_y(): lax.ppermute(value, AXES, [(device(z, y + k, x, c), device(z, y, x, c)) f...  11.4 us
    pallas_call x1, Pallas kernels, local(): pl.pallas_call(functools.partial(tile_kernel, *sizes), out_shape=(shape(p...  10.2 us
    ppermute x7, waiting for transfers between devices, from_x(): lax.ppermute(value, AXES, [(device(z, y, x + k, c), device(z, y, x, c)) f...  9.13 us
    pallas_call x8, Pallas kernels, small_kernel(): pl.pallas_call(body, out_shape=out, in_specs=specs or [VM] * len(args), o...  9.02 us
    ppermute x3, starting transfers between devices, other_core(): lax.ppermute(value, AXES, [(device(z, y, x, 1 - c), device(z, y, x, c)) f...  4.79 us
  transfers between devices with their start and end apart: 18, of which 9 were waited for; matrix products, arithmetic and copies ran while one was open for 1% of the time, Pallas kernels for 0%

profile of v5, /device:TPU:1, one launch (start us, length us, event | category | flops | bytes accessed | tf_op | source)
XLA Modules:
  0.0 145.9 jit_solution(13608178900338789329)
XLA Ops:
  7.2 0.0 all-gather.2.cloned.1.call-start
  7.2 0.0 copy-start.1
  7.2 1.1 copy-done.1
  8.3 0.7 copy-done.6
  9.0 1.1 prepare.1
  10.2 0.0 all-gather.2.cloned.1.call-update
  10.2 2.2 %collective-permute-start.5 = (bf16[40,2048]{1,0:T(8,128)(2,1)S(1)}, bf16[40,2048]{1,0:T(8,128)(2,1)S(1)}, u32[]{:S(2)}, u32[]{:S(2)}) collective-permute-start(bf16[40,2048]{1,0:T(8,128)(2,1)S(1)} %get-tuple-element.26), channel_id=1, source_target_pairs={{20,0},{28,8},{21,1},{29,9},{22,2},{30,10},{23,3},{31,11},{0,16},{... | collective-permute-start | bytes 491528 | tf_op jit(solution)/shard_map/ppermute | solution.py:56
  12.4 2.6 %collective-permute-start.4 = (bf16[40,2048]{1,0:T(8,128)(2,1)S(1)}, bf16[40,2048]{1,0:T(8,128)(2,1)S(1)}, u32[]{:S(2)}, u32[]{:S(2)}) collective-permute-start(bf16[40,2048]{1,0:T(8,128)(2,1)S(1)} %get-tuple-element.26), channel_id=1, source_target_pairs={{4,0},{12,8},{5,1},{13,9},{6,2},{14,10},{7,3},{15,11},{20,16},{28,... | collective-permute-start | bytes 491528 | tf_op jit(solution)/shard_map/ppermute | solution.py:56
  15.0 1.1 collective-permute-start.3
  16.1 1.2 collective-permute-start.2
  17.3 2.5 %collective-permute-start.1 = (bf16[40,2176]{1,0:T(8,128)(2,1)S(1)}, bf16[40,2176]{1,0:T(8,128)(2,1)S(1)}, u32[]{:S(2)}, u32[]{:S(2)}) collective-permute-start(bf16[40,2176]{1,0:T(8,128)(2,1)S(1)} %get-tuple-element.25), channel_id=1, source_target_pairs={{2,0},{10,8},{3,1},{11,9},{0,2},{8,10},{1,3},{9,11},{18,16},{26,24... | collective-permute-start | bytes 522248 | tf_op jit(solution)/shard_map/ppermute | solution.py:50
  19.7 0.0 collective-permute-done.5
  19.8 1.2 collective-permute-start
  20.9 1.2 collective-permute-done.4
  22.1 0.0 collective-permute-done.3
  22.2 0.0 copy-start.9
  22.2 0.0 collective-permute-done.2
  22.2 3.9 %collective-permute-done.1 = bf16[40,2176]{1,0:T(8,128)(2,1)S(1)} collective-permute-done((bf16[40,2176]{1,0:T(8,128)(2,1)S(1)}, bf16[40,2176]{1,0:T(8,128)(2,1)S(1)}, u32[]{:S(2)}, u32[]{:S(2)}) %collective-permute-start.1) | collective-permute-done | bytes 174112 | tf_op jit(solution)/shard_map/ppermute | solution.py:50
  26.1 0.0 collective-permute-done
  26.1 0.1 pad_maximum_fusion.refs_1_
  26.2 0.0 copy-start.8
  26.2 0.5 collective-permute-start.8
  26.7 2.3 %collective-permute-start.6 = (bf16[160,2176]{1,0:T(8,128)(2,1)S(1)}, bf16[160,2176]{1,0:T(8,128)(2,1)S(1)}, u32[]{:S(2)}, u32[]{:S(2)}) collective-permute-start(bf16[160,2176]{1,0:T(8,128)(2,1)S(1)} %pad_maximum_fusion.refs_1_), channel_id=1, source_target_pairs={{16,0},{24,8},{17,1},{25,9},{18,2},{26,10},{19,3},{27,11},{4,16},{... | collective-permute-start | bytes 2088968 | tf_op jit(solution)/shard_map/ppermute | solution.py:56
  28.9 2.6 %collective-permute-start.12 = (bf16[160,2048]{1,0:T(8,128)(2,1)S(1)}, bf16[160,2048]{1,0:T(8,128)(2,1)S(1)}, u32[]{:S(2)}, u32[]{:S(2)}) collective-permute-start(bf16[160,2048]{1,0:T(8,128)(2,1)S(1)} %pad_maximum_fusion.1.refs_6_), channel_id=1, source_target_pairs={{3,0},{11,8},{0,1},{8,9},{1,2},{9,10},{2,3},{10,11},{19,16},{27,24... | collective-permute-start | bytes 1966088 | tf_op jit(solution)/shard_map/ppermute | solution.py:50
  31.5 0.3 collective-permute-start.10
  31.8 10.2 %collective-permute-done.8.refs_5_ = bf16[160,2176]{1,0:T(8,128)(2,1)S(1)} collective-permute-done((bf16[160,2176]{1,0:T(8,128)(2,1)S(1)}, bf16[160,2176]{1,0:T(8,128)(2,1)S(1)}, u32[]{:S(2)}, u32[]{:S(2)}) %collective-permute-start.8) | collective-permute-done | bytes 696352 | tf_op jit(solution)/shard_map/ppermute | solution.py:56
  42.0 0.1 collective-permute-start.9
  42.1 0.0 collective-permute-done.6.refs_2_
  42.1 0.0 copy-start.11
  42.1 2.7 %collective-permute-start.7 = (bf16[80,2176]{1,0:T(8,128)(2,1)S(1)}, bf16[80,2176]{1,0:T(8,128)(2,1)}, u32[]{:S(2)}, u32[]{:S(2)}) collective-permute-start(bf16[80,2176]{1,0:T(8,128)(2,1)S(1)} %slice.16), channel_id=1, source_target_pairs={{16,0},{24,8},{17,1},{25,9},{18,2},{26,10},{19,3},{27,11},{4,16},{... | collective-permute-start | bytes 1044488 | tf_op jit(solution)/shard_map/ppermute | solution.py:56
  44.8 0.0 collective-permute-done.12.refs_10_
  44.9 0.0 copy-done.9
  44.9 4.2 %collective-permute-start.13 = (bf16[80,2048]{1,0:T(8,128)(2,1)S(1)}, bf16[80,2048]{1,0:T(8,128)(2,1)}, u32[]{:S(2)}, u32[]{:S(2)}) collective-permute-start(bf16[80,2048]{1,0:T(8,128)(2,1)S(1)} %slice.19), channel_id=1, source_target_pairs={{3,0},{11,8},{0,1},{8,9},{1,2},{9,10},{2,3},{10,11},{19,16},{27,24... | collective-permute-start | bytes 983048 | tf_op jit(solution)/shard_map/ppermute | solution.py:50
  49.0 0.0 collective-permute-done.10.refs_7_
  49.1 0.3 collective-permute-start.11
  49.3 0.0 copy-done.11
  49.3 0.0 copy-done.12
  49.4 0.5 copy-done.13
  49.9 0.6 pad_add_fusion.at_ref
  50.5 3.0 %collective-permute-done.13.refs_9_ = bf16[80,2048]{1,0:T(8,128)(2,1)} collective-permute-done((bf16[80,2048]{1,0:T(8,128)(2,1)S(1)}, bf16[80,2048]{1,0:T(8,128)(2,1)}, u32[]{:S(2)}, u32[]{:S(2)}) %collective-permute-start.13) | collective-permute-done | bytes 327712 | tf_op jit(solution)/shard_map/ppermute | solution.py:50
  53.5 2.2 %collective-permute-done.11.refs_8_ = bf16[80,2048]{1,0:T(8,128)(2,1)S(1)} collective-permute-done((bf16[80,2048]{1,0:T(8,128)(2,1)S(1)}, bf16[80,2048]{1,0:T(8,128)(2,1)S(1)}, u32[]{:S(2)}, u32[]{:S(2)}) %collective-permute-start.11) | collective-permute-done | bytes 327712 | tf_op jit(solution)/shard_map/ppermute | solution.py:50
  55.7 0.0 collective-permute-done.9.refs_4_
  55.8 0.0 collective-permute-done.7.refs_3_
  55.8 2.8 %all-gather.2.cloned.1.call-done.refs_0_ = bf16[640,4224]{1,0:T(8,128)(2,1)} async-done(((bf16[40,4224]{1,0:T(8,128)(2,1)}), bf16[640,4224]{1,0:T(8,128)(2,1)}) %all-gather.2.cloned.1.call-update) | async-done | bytes 5406736 | tf_op jit(solution)/shard_map/all_gather | solution.py:353
  58.5 10.2 %tile.1 = (f32[640,640]{1,0:T(8,128)}, f32[32,352]{1,0:T(8,128)}, f32[32,352]{1,0:T(8,128)}, f32[32,640]{1,0:T(8,128)}, f32[32,640]{1,0:T(8,128)}, /*index=5*/f32[32,32]{1,0:T(8,128)}) custom-call(s32[4]{0:T(128)} %pad_add_fusion.at_ref, bf16[640,4224]{1,0:T(8,128)(2,1)} %all-gather.2.cloned.1.call-done.refs_0_, bf16[160,2176]{1,0:T(8,128)(2,1)} %copy-done.8, ...), custom_call_target="tpu_custom_call" | custom-call | flops 6710886400 | bytes 10485760 | tf_op jit(solution)/shard_map/tile/pallas_call | solution.py:362
  68.7 1.8 %collective-permute-start.14 = (f32[32,352]{1,0:T(8,128)}, f32[32,352]{1,0:T(8,128)S(1)}, u32[]{:S(2)}, u32[]{:S(2)}) collective-permute-start(f32[32,352]{1,0:T(8,128)} %get-tuple-element.30), channel_id=1, source_target_pairs={{8,0},{0,8},{9,1},{1,9},{10,2},{2,10},{11,3},{3,11},{24,16},{16,24... | collective-permute-start | bytes 135176 | tf_op jit(solution)/shard_map/ppermute | solution.py:62
  70.5 1.1 collective-permute-done.14.b_ref
  71.6 0.8 copy-done.5
  72.4 22.2 %all_to_all.20.part_ref = f32[8,32,352]{2,1,0:T(8,128)S(1)} all-to-all(f32[8,32,352]{2,1,0:T(8,128)S(1)} %share.1), channel_id=1, replica_groups={{0,32,64,96,128,160,192,224},{8,40,72,104,136,168,200,232},{1,33,65,97,..., dimensions={0} | all-to-all | bytes 720896 | tf_op jit(solution)/shard_map/all_to_all | solution.py:68
  94.6 0.9 copy-done.2
  95.5 0.3 line.1
  95.8 1.7 %collective-permute-start.15 = (f32[32,384]{1,0:T(8,128)S(1)}, f32[32,384]{1,0:T(8,128)S(1)}, u32[]{:S(2)}, u32[]{:S(2)}) collective-permute-start(f32[32,384]{1,0:T(8,128)S(1)} %get-tuple-element.32.near_ref.refs_2_), channel_id=1, source_target_pairs={{8,0},{0,8},{9,1},{1,9},{10,2},{2,10},{11,3},{3,11},{24,16},{16,24... | collective-permute-start | bytes 147464 | tf_op jit(solution)/shard_map/ppermute | solution.py:62
  97.5 0.9 collective-permute-done.15.far_ref.refs_3_
  98.4 1.1 spread.1
  99.5 11.0 %all_to_all.21.refs_0_ = f32[16,32,104]{2,1,0:T(8,128)S(1)} all-to-all(f32[16,32,104]{2,1,0:T(8,128)S(1)} %spread.1), channel_id=1, replica_groups={{0,1,2,3,16,17,18,19,4,5,6,7,20,21,22,23},{8,9,10,11,24,25,26,27,12,13,..., dimensions={0} | all-to-all | bytes 425984 | tf_op jit(solution)/shard_map/all_to_all | solution.py:68
  110.5 0.0 copy-done.3
  110.5 4.4 %step.1 = (f32[32,320]{1,0:T(8,128)S(1)}, f32[32,352]{1,0:T(8,128)S(1)}, f32[32,40]{1,0:T(8,128)S(1)}, f32[32,40]{1,0:T(8,128)S(1)}, f32[32,40]{1,0:T(8,128)S(1)}, /*index=5*/f32[32,32]{1,0:T(8,128)S(1)}) custom-call(s32[4]{0:T(128)S(1)} %copy-done.7, f32[16,32,104]{2,1,0:T(8,128)S(1)} %all_to_all.21.refs_0_, f32[32,32]{1,0:T(8,128)S(1)} %get-tuple-element.33.refs_1_, ...), custom_call_target="tpu_custom_call" | custom-call | tf_op jit(solution)/shard_map/step/pallas_call | solution.py:86
  114.9 1.4 collective-permute-start.16
  116.2 0.9 collective-permute-done.16.far_ref
  117.1 0.1 chunk.1
  117.2 10.8 %all_to_all.22.got_ref = f32[8,32,72]{2,1,0:T(8,128)S(1)} all-to-all(f32[8,32,72]{2,1,0:T(8,128)S(1)} %chunk.1), channel_id=1, replica_groups={{0,32,64,96,128,160,192,224},{8,40,72,104,136,168,200,232},{1,33,65,97,..., dimensions={0} | all-to-all | bytes 147456 | tf_op jit(solution)/shard_map/all_to_all | solution.py:68
  128.0 0.1 image.1
  128.1 9.1 %all_to_all.23.got_ref = f32[16,8,128]{2,1,0:T(8,128)S(1)} all-to-all(f32[16,8,128]{2,1,0:T(8,128)S(1)} %get-tuple-element.39), channel_id=1, replica_groups={{0,1,2,3,16,17,18,19,4,5,6,7,20,21,22,23},{8,9,10,11,24,25,26,27,12,13,..., dimensions={0} | all-to-all | bytes 131072 | tf_op jit(solution)/shard_map/all_to_all | solution.py:68
  137.2 1.8 %last.1 = (f32[32,40]{1,0:T(8,128)}, f32[32,40]{1,0:T(8,128)}) custom-call(f32[16,8,128]{2,1,0:T(8,128)S(1)} %all_to_all.23.got_ref, f32[32,32]{1,0:T(8,128)S(1)} %get-tuple-element.40.rr, f32[32,40]{1,0:T(8,128)S(1)} %get-tuple-element.38.d_ref.d_own, f32[32,40]{1,0:T(8,128)S(1)} %get-tuple-element.41.image, f32[32,40]{1,0:T(8,128)S(1)} %get-tuple-element.42.weights, ...), custom_call_target="tpu_custom_call" | custom-call | tf_op jit(solution)/shard_map/last/pallas_call | solution.py:86
  (23 shorter events, 0.2 us)
Async XLA Ops:
  7.2 51.4 %all-gather.2.cloned.1.call-start = ((), (), s32[]{:S(2)}) async-start(), calls=%async_computation.4 | async-start | bytes 5744640 | tf_op jit(solution)/shard_map/all_gather | solution.py:353
  7.2 1.1 copy-start.1
  8.3 0.7 copy-start.6
  10.2 9.6 %collective-permute-start.5 = (bf16[40,2048]{1,0:T(8,128)(2,1)S(1)}, bf16[40,2048]{1,0:T(8,128)(2,1)S(1)}, u32[]{:S(2)}, u32[]{:S(2)}) collective-permute-start(bf16[40,2048]{1,0:T(8,128)(2,1)S(1)} %get-tuple-element.26), channel_id=1, source_target_pairs={{20,0},{28,8},{21,1},{29,9},{22,2},{30,10},{23,3},{31,11},{0,16},{... | collective-permute-start | bytes 491528 | tf_op jit(solution)/shard_map/ppermute | solution.py:56
  12.4 9.7 %collective-permute-start.4 = (bf16[40,2048]{1,0:T(8,128)(2,1)S(1)}, bf16[40,2048]{1,0:T(8,128)(2,1)S(1)}, u32[]{:S(2)}, u32[]{:S(2)}) collective-permute-start(bf16[40,2048]{1,0:T(8,128)(2,1)S(1)} %get-tuple-element.26), channel_id=1, source_target_pairs={{4,0},{12,8},{5,1},{13,9},{6,2},{14,10},{7,3},{15,11},{20,16},{28,... | collective-permute-start | bytes 491528 | tf_op jit(solution)/shard_map/ppermute | solution.py:56
  15.0 7.1 %collective-permute-start.3 = (bf16[40,2048]{1,0:T(8,128)(2,1)S(1)}, bf16[40,2048]{1,0:T(8,128)(2,1)S(1)}, u32[]{:S(2)}, u32[]{:S(2)}) collective-permute-start(bf16[40,2048]{1,0:T(8,128)(2,1)S(1)} %get-tuple-element.26), channel_id=1, source_target_pairs={{16,0},{24,8},{17,1},{25,9},{18,2},{26,10},{19,3},{27,11},{4,16},{... | collective-permute-start | bytes 491528 | tf_op jit(solution)/shard_map/ppermute | solution.py:56
  16.1 6.1 %collective-permute-start.2 = (bf16[40,2176]{1,0:T(8,128)(2,1)S(1)}, bf16[40,2176]{1,0:T(8,128)(2,1)S(1)}, u32[]{:S(2)}, u32[]{:S(2)}) collective-permute-start(bf16[40,2176]{1,0:T(8,128)(2,1)S(1)} %get-tuple-element.25), channel_id=1, source_target_pairs={{3,0},{11,8},{0,1},{8,9},{1,2},{9,10},{2,3},{10,11},{19,16},{27,24... | collective-permute-start | bytes 522248 | tf_op jit(solution)/shard_map/ppermute | solution.py:50
  17.3 8.8 %collective-permute-start.1 = (bf16[40,2176]{1,0:T(8,128)(2,1)S(1)}, bf16[40,2176]{1,0:T(8,128)(2,1)S(1)}, u32[]{:S(2)}, u32[]{:S(2)}) collective-permute-start(bf16[40,2176]{1,0:T(8,128)(2,1)S(1)} %get-tuple-element.25), channel_id=1, source_target_pairs={{2,0},{10,8},{3,1},{11,9},{0,2},{8,10},{1,3},{9,11},{18,16},{26,24... | collective-permute-start | bytes 522248 | tf_op jit(solution)/shard_map/ppermute | solution.py:50
  19.8 6.4 %collective-permute-start = (bf16[40,2176]{1,0:T(8,128)(2,1)S(1)}, bf16[40,2176]{1,0:T(8,128)(2,1)S(1)}, u32[]{:S(2)}, u32[]{:S(2)}) collective-permute-start(bf16[40,2176]{1,0:T(8,128)(2,1)S(1)} %get-tuple-element.25), channel_id=1, source_target_pairs={{1,0},{9,8},{2,1},{10,9},{3,2},{11,10},{0,3},{8,11},{17,16},{25,24... | collective-permute-start | bytes 522248 | tf_op jit(solution)/shard_map/ppermute | solution.py:50
  22.2 22.7 %copy-start.9 = (bf16[160,2048]{1,0:T(8,128)(2,1)}, bf16[160,2048]{1,0:T(8,128)(2,1)S(1)}, u32[]{:S(2)}) copy-start(bf16[160,2048]{1,0:T(8,128)(2,1)S(1)} %pad_maximum_fusion.1.refs_6_) | copy-start | bytes 1966084
  26.2 23.7 %copy-start.8 = (bf16[160,2176]{1,0:T(8,128)(2,1)}, bf16[160,2176]{1,0:T(8,128)(2,1)S(1)}, u32[]{:S(2)}) copy-start(bf16[160,2176]{1,0:T(8,128)(2,1)S(1)} %pad_maximum_fusion.refs_1_) | copy-start | bytes 2088964
  26.2 15.8 %collective-permute-start.8 = (bf16[160,2176]{1,0:T(8,128)(2,1)S(1)}, bf16[160,2176]{1,0:T(8,128)(2,1)S(1)}, u32[]{:S(2)}, u32[]{:S(2)}) collective-permute-start(bf16[160,2176]{1,0:T(8,128)(2,1)S(1)} %pad_maximum_fusion.refs_1_), channel_id=1, source_target_pairs={{20,0},{28,8},{21,1},{29,9},{22,2},{30,10},{23,3},{31,11},{0,16},{... | collective-permute-start | bytes 2088968 | tf_op jit(solution)/shard_map/ppermute | solution.py:56
  26.7 15.4 %collective-permute-start.6 = (bf16[160,2176]{1,0:T(8,128)(2,1)S(1)}, bf16[160,2176]{1,0:T(8,128)(2,1)S(1)}, u32[]{:S(2)}, u32[]{:S(2)}) collective-permute-start(bf16[160,2176]{1,0:T(8,128)(2,1)S(1)} %pad_maximum_fusion.refs_1_), channel_id=1, source_target_pairs={{16,0},{24,8},{17,1},{25,9},{18,2},{26,10},{19,3},{27,11},{4,16},{... | collective-permute-start | bytes 2088968 | tf_op jit(solution)/shard_map/ppermute | solution.py:56
  28.9 15.9 %collective-permute-start.12 = (bf16[160,2048]{1,0:T(8,128)(2,1)S(1)}, bf16[160,2048]{1,0:T(8,128)(2,1)S(1)}, u32[]{:S(2)}, u32[]{:S(2)}) collective-permute-start(bf16[160,2048]{1,0:T(8,128)(2,1)S(1)} %pad_maximum_fusion.1.refs_6_), channel_id=1, source_target_pairs={{3,0},{11,8},{0,1},{8,9},{1,2},{9,10},{2,3},{10,11},{19,16},{27,24... | collective-permute-start | bytes 1966088 | tf_op jit(solution)/shard_map/ppermute | solution.py:50
  31.5 17.5 %collective-permute-start.10 = (bf16[160,2048]{1,0:T(8,128)(2,1)S(1)}, bf16[160,2048]{1,0:T(8,128)(2,1)S(1)}, u32[]{:S(2)}, u32[]{:S(2)}) collective-permute-start(bf16[160,2048]{1,0:T(8,128)(2,1)S(1)} %pad_maximum_fusion.1.refs_6_), channel_id=1, source_target_pairs={{1,0},{9,8},{2,1},{10,9},{3,2},{11,10},{0,3},{8,11},{17,16},{25,24... | collective-permute-start | bytes 1966088 | tf_op jit(solution)/shard_map/ppermute | solution.py:50
  41.9 8.0 %copy-start.10 = (bf16[160,2176]{1,0:T(8,128)(2,1)}, bf16[160,2176]{1,0:T(8,128)(2,1)S(1)}, u32[]{:S(2)}) copy-start(bf16[160,2176]{1,0:T(8,128)(2,1)S(1)} %collective-permute-done.8.refs_5_) | copy-start | bytes 2088964
  42.0 13.8 %collective-permute-start.9 = (bf16[80,2176]{1,0:T(8,128)(2,1)S(1)}, bf16[80,2176]{1,0:T(8,128)(2,1)}, u32[]{:S(2)}, u32[]{:S(2)}) collective-permute-start(bf16[80,2176]{1,0:T(8,128)(2,1)S(1)} %slice.17), channel_id=1, source_target_pairs={{20,0},{28,8},{21,1},{29,9},{22,2},{30,10},{23,3},{31,11},{0,16},{... | collective-permute-start | bytes 1044488 | tf_op jit(solution)/shard_map/ppermute | solution.py:56
  42.1 7.3 %copy-start.11 = (bf16[160,2176]{1,0:T(8,128)(2,1)}, bf16[160,2176]{1,0:T(8,128)(2,1)S(1)}, u32[]{:S(2)}) copy-start(bf16[160,2176]{1,0:T(8,128)(2,1)S(1)} %collective-permute-done.6.refs_2_) | copy-start | bytes 2088964
  42.1 13.6 %collective-permute-start.7 = (bf16[80,2176]{1,0:T(8,128)(2,1)S(1)}, bf16[80,2176]{1,0:T(8,128)(2,1)}, u32[]{:S(2)}, u32[]{:S(2)}) collective-permute-start(bf16[80,2176]{1,0:T(8,128)(2,1)S(1)} %slice.16), channel_id=1, source_target_pairs={{16,0},{24,8},{17,1},{25,9},{18,2},{26,10},{19,3},{27,11},{4,16},{... | collective-permute-start | bytes 1044488 | tf_op jit(solution)/shard_map/ppermute | solution.py:56
  44.8 4.5 %copy-start.12 = (bf16[160,2048]{1,0:T(8,128)(2,1)}, bf16[160,2048]{1,0:T(8,128)(2,1)S(1)}, u32[]{:S(2)}) copy-start(bf16[160,2048]{1,0:T(8,128)(2,1)S(1)} %collective-permute-done.12.refs_10_) | copy-start | bytes 1966084
  44.9 8.6 %collective-permute-start.13 = (bf16[80,2048]{1,0:T(8,128)(2,1)S(1)}, bf16[80,2048]{1,0:T(8,128)(2,1)}, u32[]{:S(2)}, u32[]{:S(2)}) collective-permute-start(bf16[80,2048]{1,0:T(8,128)(2,1)S(1)} %slice.19), channel_id=1, source_target_pairs={{3,0},{11,8},{0,1},{8,9},{1,2},{9,10},{2,3},{10,11},{19,16},{27,24... | collective-permute-start | bytes 983048 | tf_op jit(solution)/shard_map/ppermute | solution.py:50
  49.0 0.9 copy-start.13
  49.1 6.7 %collective-permute-start.11 = (bf16[80,2048]{1,0:T(8,128)(2,1)S(1)}, bf16[80,2048]{1,0:T(8,128)(2,1)S(1)}, u32[]{:S(2)}, u32[]{:S(2)}) collective-permute-start(bf16[80,2048]{1,0:T(8,128)(2,1)S(1)} %slice.18), channel_id=1, source_target_pairs={{1,0},{9,8},{2,1},{10,9},{3,2},{11,10},{0,3},{8,11},{17,16},{25,24... | collective-permute-start | bytes 983048 | tf_op jit(solution)/shard_map/ppermute | solution.py:50
  55.7 2.8 %copy-start.14 = (bf16[80,2048]{1,0:T(8,128)(2,1)}, bf16[80,2048]{1,0:T(8,128)(2,1)S(1)}, u32[]{:S(2)}) copy-start(bf16[80,2048]{1,0:T(8,128)(2,1)S(1)} %collective-permute-done.11.refs_8_) | copy-start | bytes 983044
  58.5 39.9 %copy-start.7 = (s32[4]{0:T(128)S(1)}, s32[4]{0:T(128)}, u32[]{:S(2)}) copy-start(s32[4]{0:T(128)} %pad_add_fusion.at_ref) | copy-start | bytes 52
  68.7 41.8 %copy-start = (f32[640,640]{1,0:T(8,128)S(1)}, f32[640,640]{1,0:T(8,128)}, u32[]{:S(2)}) copy-start(f32[640,640]{1,0:T(8,128)} %get-tuple-element.35.refs_6_) | copy-start | bytes 4915204
  68.7 2.8 %collective-permute-start.14 = (f32[32,352]{1,0:T(8,128)}, f32[32,352]{1,0:T(8,128)S(1)}, u32[]{:S(2)}, u32[]{:S(2)}) collective-permute-start(f32[32,352]{1,0:T(8,128)} %get-tuple-element.30), channel_id=1, source_target_pairs={{8,0},{0,8},{9,1},{1,9},{10,2},{2,10},{11,3},{3,11},{24,16},{16,24... | collective-permute-start | bytes 135176 | tf_op jit(solution)/shard_map/ppermute | solution.py:62
  71.6 0.8 copy-start.5
  94.6 0.9 copy-start.2
  95.5 15.0 %copy-start.3 = (f32[32,640]{1,0:T(8,128)S(1)}, f32[32,640]{1,0:T(8,128)}, u32[]{:S(2)}) copy-start(f32[32,640]{1,0:T(8,128)} %get-tuple-element.31.t_ref.refs_4_) | copy-start | bytes 245764
  95.5 15.0 %copy-start.4 = (f32[32,640]{1,0:T(8,128)S(1)}, f32[32,640]{1,0:T(8,128)}, u32[]{:S(2)}) copy-start(f32[32,640]{1,0:T(8,128)} %get-tuple-element.34.refs_5_) | copy-start | bytes 245764
  95.8 2.6 %collective-permute-start.15 = (f32[32,384]{1,0:T(8,128)S(1)}, f32[32,384]{1,0:T(8,128)S(1)}, u32[]{:S(2)}, u32[]{:S(2)}) collective-permute-start(f32[32,384]{1,0:T(8,128)S(1)} %get-tuple-element.32.near_ref.refs_2_), channel_id=1, source_target_pairs={{8,0},{0,8},{9,1},{1,9},{10,2},{2,10},{11,3},{3,11},{24,16},{16,24... | collective-permute-start | bytes 147464 | tf_op jit(solution)/shard_map/ppermute | solution.py:62
  114.9 2.2 %collective-permute-start.16 = (f32[32,352]{1,0:T(8,128)S(1)}, f32[32,352]{1,0:T(8,128)S(1)}, u32[]{:S(2)}, u32[]{:S(2)}) collective-permute-start(f32[32,352]{1,0:T(8,128)S(1)} %get-tuple-element.37.here_ref), channel_id=1, source_target_pairs={{8,0},{0,8},{9,1},{1,9},{10,2},{2,10},{11,3},{3,11},{24,16},{16,24... | collective-permute-start | bytes 135176 | tf_op jit(solution)/shard_map/ppermute | solution.py:62
Sparse Core Ops, SparseCore 0:
  10.3 48.1 all-gather.1

commit v6 on v5

--- a/solution.py
+++ b/solution.py
@@ -141,13 +141,13 @@
     x_hbm, a_hbm, b_hbm = refs[0], refs[1:6], refs[6:11]
     k_ref, near_ref, far_ref, tx_ref, ty_ref, n0_ref = refs[11:17]
     x_ref, a_ref, b_ref, cos_ref, sems = refs[17:]
-    line, quarter = 8 * rows, half // 2
+    line, quarter, last = 8 * rows, half // 2, half // 4
     dims = (((1,), (1,)), ((), ()))
     plans = (
         (0, quarter, a_hbm, a_ref, 0, quarter),
         (quarter, quarter, a_hbm, a_ref, quarter, quarter + PAD),
-        (half, quarter, b_hbm, b_ref, 0, quarter),
-        (half + quarter, quarter + PAD, b_hbm, b_ref, quarter, quarter),
+        (half, half - last, b_hbm, b_ref, 0, half - last),
+        (2 * half - last, last + PAD, b_hbm, b_ref, half - last, last),
     )
     groups = []
     for i, (at_x, wide_x, pieces, ref, at_y, wide_y) in enumerate(plans):
@@ -168,12 +168,13 @@
         groups.append(group)
         for copy in group:
             copy.start()
-    for i, (at_x, _, _, ref, at_y, _) in enumerate(plans):
+    for i, (at_x, wide_x, _, ref, at_y, wide_y) in enumerate(plans):
         for copy in groups[i]:
             copy.wait()
+        wide = min(wide_x, wide_y)
         product = lax.dot_general(
-            ref[:, at_y : at_y + quarter],
-            x_ref[:, at_x : at_x + quarter],
+            ref[:, at_y : at_y + wide],
+            x_ref[:, at_x : at_x + wide],
             dims,
             preferred_element_type=F32,
         )
@@ -216,14 +217,12 @@
     send_ref[:, line + rhs :] = nt(w, w)
 
 
-def spread_kernel(rows, line, at_ref, near_ref, far_ref, out_ref):
-    grams = near_ref[:, line:] + far_ref[:, line:]
-    own = jnp.zeros((near_ref.shape[0], rows), F32)
-    for z in range(NZ):
-        own = jnp.where(at_ref[0] == z, near_ref[:, z * rows : (z + 1) * rows], own)
-    for i in range(NY * NX):
-        out_ref[i, :, :rows] = own
-        out_ref[i, :, rows:] = grams
+def spread_kernel(rows, line, own_ref, near_ref, far_ref, out_ref):
+    out_ref[0, :, :rows] = own_ref[...]
+    out_ref[0, :, rows:] = near_ref[:, line:] + far_ref[:, line:]
+    payload = out_ref[0]
+    for i in range(1, NY * NX):
+        out_ref[i] = payload
 
 
 def eliminate(pairs):
@@ -261,7 +260,7 @@
 
 def step_kernel(rows, rhs, line, at_ref, *refs):
     got_ref, n0_ref, w_line, w_far, t_tube, t_plane, k_ref = refs[:7]
-    near_ref, far_ref, d_ref, weights_ref, residual_ref, rr_ref, w_ref = refs[7:]
+    out_ref, d_ref, weights_ref, residual_ref, rr_ref, w_ref, d_tube = refs[7:]
     got = jnp.sum(got_ref[...], axis=0)
     n0 = symmetric(n0_ref[...])
     n1, n2 = got[:, rows : rows + rhs], got[:, rows + rhs : rows + 2 * rhs]
@@ -283,26 +282,21 @@
     rr1 = mm(qt, mm(n0, q)) - cross - cross.T + mm(a1t, mm(n2, a1))
     mix = qt + mm(n0_inverse, rr1).T
     d_plane = mm(mix, t_plane[...]) - mm(a1t, w_ref[...])
-    product = mm(d_plane, k_ref[...])
-    near, far = product[:, :line], product[:, line:]
-    d_line = mm(mix, t_tube[:, :line]) - mm(a1t, w_line[:, :line])
-    d_far = mm(mix, t_tube[:, line:]) - mm(a1t, w_far[:, :line])
+    d_tube[:, :line] = mm(mix, t_tube[:, :line]) - mm(a1t, w_line[:, :line])
+    d_tube[:, line:] = mm(mix, t_tube[:, line:]) - mm(a1t, w_far[:, :line])
+    product = nt(d_tube[...], k_ref[...])
     d_own, t_own = d_plane[:, :rows], t_plane[:, :rows]
-    near_ref[...] = near
-    far_ref[:, :line] = far
-    far_ref[:, line:] = nt(d_line, near) + nt(d_far, far) + nt(d_own, d_own)
+    gram = nt(d_plane, product) + nt(d_own, d_own)
+    for dy in range(NY):
+        for dx in range(NX):
+            s = NX * dy + dx
+            of = lax.rem(y + dy, NY) * NX + lax.rem(x + dx, NX)
+            block = product[:, s * rows : (s + 1) * rows]
+            out_ref[of] = jnp.concatenate([block, gram], axis=1)
     d_ref[...] = d_own
     weights_ref[...] = mm(a1t, t_own)
     residual_ref[...] = mm(qt, t_own) - mm(a1t, w_ref[:, :rows])
     rr_ref[...] = rr1
-
-
-def chunk_kernel(rows, line, near_ref, far_ref, here_ref, out_ref):
-    gram = far_ref[:, line:] + here_ref[:, line:]
-    total = near_ref[...] + far_ref[:, :line]
-    for z in range(NZ):
-        out_ref[z, :, :rows] = total[:, z * rows : (z + 1) * rows]
-        out_ref[z, :, rows:] = gram
 
 
 def image_kernel(rows, got_ref, d_ref, image_ref, out_ref):
@@ -310,7 +304,7 @@
     image_ref[...] = got[:, :rows] + d_ref[...]
     gram = got[:, rows:]
     dense = jnp.concatenate([gram[8 * i : 8 * i + 8] for i in range(4)], axis=1)
-    for i in range(NY * NX):
+    for i in range(NZ * NC):
         out_ref[i] = dense
 
 
@@ -343,6 +337,7 @@
         ),
         (sketches, targets.T),
         [HBM] * 2,
+        limit=60,
         scratch=[
             pltpu.VMEM((rows, 2 * half), F32),
             pltpu.VMEM((rhs, rows), F32),
@@ -378,7 +373,7 @@
             pltpu.VMEM((plane, NC * line), F32),
             pltpu.SemaphoreType.DMA((4, NC + 5)),
         ],
-        compiler_params=pltpu.CompilerParams(vmem_limit_bytes=60 * MIB),
+        compiler_params=pltpu.CompilerParams(vmem_limit_bytes=57 * MIB),
         cost_estimate=pl.CostEstimate(
             flops=4 * plane * NC * line * 2 * half,
             bytes_accessed=2 * (plane + NC * line) * 2 * half,
@@ -399,48 +394,36 @@
         (exchange(copies, LINES), t_tube),
         name="line",
     )
+    w_own = lax.dynamic_slice(sent, (0, z * rows), (rhs, rows))
     received = other_core(sent)
     copies = small_kernel(
         functools.partial(spread_kernel, rows, line),
         shape(NY * NX, rhs, rows + 2 * rhs),
-        (at, sent, received),
-        [SM, VM, VM],
+        (w_own, sent, received),
         name="spread",
     )
     got = exchange(copies, PLANES)
     own = shape(rhs, rows)
     values = (at, got, n0, sent, received, t_tube, t_plane, k)
-    near, far, d_own, weights, residual, rr1 = small_kernel(
+    chunks, d_own, weights, residual, rr1 = small_kernel(
         functools.partial(step_kernel, rows, rhs, line),
-        (shape(rhs, line), shape(rhs, line + rhs), own, own, own, shape(rhs, rhs)),
+        (shape(NY * NX, rhs, rows + rhs), own, own, own, shape(rhs, rhs)),
         values,
         [SM] + [VM] * 7,
         limit=16,
-        scratch=[pltpu.VMEM((rhs, plane), F32)],
+        scratch=[pltpu.VMEM((rhs, plane), F32), pltpu.VMEM((rhs, NC * line), F32)],
         name="step",
     )
-    return finish(rows, rhs, line, near, far, d_own, weights, residual, rr1)
-
-
-def finish(rows, rhs, line, near, far, d_own, weights, residual, rr1):
-    away = other_core(far)
-    chunks = small_kernel(
-        functools.partial(chunk_kernel, rows, line),
-        shape(NZ, rhs, rows + rhs),
-        (near, away, far),
-        name="chunk",
-    )
-    own = shape(rhs, rows)
     image, copies = small_kernel(
         functools.partial(image_kernel, rows),
-        (own, shape(NY * NX, rhs // 4, 4 * rhs)),
-        (exchange(chunks, LINES), d_own),
+        (own, shape(NZ * NC, rhs // 4, 4 * rhs)),
+        (exchange(chunks, PLANES), d_own),
         name="image",
     )
     weights, residual = small_kernel(
         functools.partial(last_kernel, rhs),
         (own, own),
-        (exchange(copies, PLANES), rr1, d_own, image, weights, residual),
+        (exchange(copies, TUBES), rr1, d_own, image, weights, residual),
         name="last",
     )
     return weights.T, residual.T

time: 147 us -> 147 us (level)
  blocking collectives: 53.1 us -> 33.4 us
  waiting for transfers between devices: 26.2 us -> 39.7 us
  starting transfers between devices: 28.4 us -> 34.3 us
  local copies, waits for them, and re-layouts: 4.16 us -> 2.45 us
    all_to_all x4 -> x3, blocking collectives: 53.1 us -> 33.4 us  [exchange(): lax.all_to_all(chunks, AXES, 0, 0, axis_index_groups=groups, tiled=True)]
    all_to_all x0 -> x1, waiting for transfers between devices: none -> 15.1 us  [exchange(): lax.all_to_all(chunks, AXES, 0, 0, axis_index_groups=groups, tiled=True)]
    all_to_all x0 -> x1, starting transfers between devices: none -> 8.5 us  [exchange(): lax.all_to_all(chunks, AXES, 0, 0, axis_index_groups=groups, tiled=True)]
    ppermute x3 -> x2, starting transfers between devices: 4.79 us -> 2.19 us  [other_core(): lax.ppermute(value, AXES, [(device(z, y, x, 1 - c), device(z, y, x, c)) f...]
    unnamed x30, local copies, waits for them, and re-layouts: 4.07 us -> 2.28 us
    pallas_call x8 -> x7, Pallas kernels: 9.02 us -> 10.1 us  [small_kernel(): pl.pallas_call(body, out_shape=out, in_specs=specs or [VM] * len(args), o...]
where the time goes in v6:
time: 147 us; the launch traced here: 146 us
  waiting for transfers between devices  39.7 us (27%)
  starting transfers between devices  34.3 us (23%)
  blocking collectives  33.4 us (23%)
  Pallas kernels  20.5 us (14%)
  between operations  14.2 us (10%)
  local copies, waits for them, and re-layouts  2.45 us (2%)
  other arithmetic  1.67 us (1%)
    all_to_all x3, blocking collectives, exchange(): lax.all_to_all(chunks, AXES, 0, 0, axis_index_groups=groups, tiled=True)  33.4 us
    all_to_all x1, waiting for transfers between devices, exchange(): lax.all_to_all(chunks, AXES, 0, 0, axis_index_groups=groups, tiled=True)  15.1 us
    ppermute x7, starting transfers between devices, from_x(): lax.ppermute(value, AXES, [(device(z, y, x + k, c), device(z, y, x, c)) f...  12.1 us
    ppermute x7, waiting for transfers between devices, from_y(): lax.ppermute(value, AXES, [(device(z, y + k, x, c), device(z, y, x, c)) f...  11.5 us
    ppermute x7, starting transfers between devices, from_y(): lax.ppermute(value, AXES, [(device(z, y + k, x, c), device(z, y, x, c)) f...  11.4 us
    pallas_call x1, Pallas kernels, local(): pl.pallas_call(functools.partial(tile_kernel, *sizes), out_shape=(shape(p...  10.4 us
    pallas_call x7, Pallas kernels, small_kernel(): pl.pallas_call(body, out_shape=out, in_specs=specs or [VM] * len(args), o...  10.1 us
    all_to_all x1, starting transfers between devices, exchange(): lax.all_to_all(chunks, AXES, 0, 0, axis_index_groups=groups, tiled=True)  8.5 us
  transfers between devices with their start and end apart: 18, of which 9 were waited for; matrix products, arithmetic and copies ran while one was open for 1% of the time, Pallas kernels for 0%

profile of v6, /device:TPU:1, one launch (start us, length us, event | category | flops | bytes accessed | tf_op | source)
XLA Modules:
  0.0 146.2 jit_solution(12649223722123386218)
XLA Ops:
  7.2 0.0 all-gather.2.cloned.1.call-start
  7.2 2.2 %prepare.1 = (bf16[40,4224]{1,0:T(8,128)(2,1)}, bf16[40,2176]{1,0:T(8,128)(2,1)}, bf16[40,2048]{1,0:T(8,128)(2,1)}) custom-call(f32[40,4096]{1,0:T(8,128)} %s_hbm.1, f32[32,40]{1,0:T(8,128)} %bitcast.7), custom_call_target="tpu_custom_call" | custom-call | tf_op jit(solution)/shard_map/prepare/pallas_call | solution.py:86
  9.4 0.0 copy-start.10
  9.4 0.0 all-gather.2.cloned.1.call-update
  9.4 2.2 %collective-permute-start.5 = (bf16[40,2048]{1,0:T(8,128)(2,1)}, bf16[40,2048]{1,0:T(8,128)(2,1)S(1)}, u32[]{:S(2)}, u32[]{:S(2)}) collective-permute-start(bf16[40,2048]{1,0:T(8,128)(2,1)} %get-tuple-element.25), channel_id=1, source_target_pairs={{20,0},{28,8},{21,1},{29,9},{22,2},{30,10},{23,3},{31,11},{0,16},{... | collective-permute-start | bytes 491528 | tf_op jit(solution)/shard_map/ppermute | solution.py:56
  11.6 2.6 %collective-permute-start.4 = (bf16[40,2048]{1,0:T(8,128)(2,1)}, bf16[40,2048]{1,0:T(8,128)(2,1)S(1)}, u32[]{:S(2)}, u32[]{:S(2)}) collective-permute-start(bf16[40,2048]{1,0:T(8,128)(2,1)} %get-tuple-element.25), channel_id=1, source_target_pairs={{4,0},{12,8},{5,1},{13,9},{6,2},{14,10},{7,3},{15,11},{20,16},{28,... | collective-permute-start | bytes 491528 | tf_op jit(solution)/shard_map/ppermute | solution.py:56
  14.2 1.1 collective-permute-start.3
  15.3 1.2 collective-permute-start.2
  16.5 2.5 %collective-permute-start.1 = (bf16[40,2176]{1,0:T(8,128)(2,1)}, bf16[40,2176]{1,0:T(8,128)(2,1)S(1)}, u32[]{:S(2)}, u32[]{:S(2)}) collective-permute-start(bf16[40,2176]{1,0:T(8,128)(2,1)} %get-tuple-element.24), channel_id=1, source_target_pairs={{2,0},{10,8},{3,1},{11,9},{0,2},{8,10},{1,3},{9,11},{18,16},{26,24... | collective-permute-start | bytes 522248 | tf_op jit(solution)/shard_map/ppermute | solution.py:50
  19.0 0.0 collective-permute-done.5
  19.0 1.2 collective-permute-start
  20.1 1.4 collective-permute-done.4
  21.6 0.0 collective-permute-done.3
  21.6 1.0 pad_maximum_fusion.1.refs_6_
  22.5 0.0 copy-start.7
  22.6 0.0 collective-permute-done.2
  22.6 3.0 %collective-permute-done.1 = bf16[40,2176]{1,0:T(8,128)(2,1)S(1)} collective-permute-done((bf16[40,2176]{1,0:T(8,128)(2,1)}, bf16[40,2176]{1,0:T(8,128)(2,1)S(1)}, u32[]{:S(2)}, u32[]{:S(2)}) %collective-permute-start.1) | collective-permute-done | bytes 174112 | tf_op jit(solution)/shard_map/ppermute | solution.py:50
  25.5 0.0 collective-permute-done
  25.5 0.0 copy-done.10
  25.5 0.1 pad_maximum_fusion.refs_1_
  25.6 0.0 copy-start.6
  25.6 0.5 collective-permute-start.8
  26.1 2.3 %collective-permute-start.6 = (bf16[160,2176]{1,0:T(8,128)(2,1)S(1)}, bf16[160,2176]{1,0:T(8,128)(2,1)S(1)}, u32[]{:S(2)}, u32[]{:S(2)}) collective-permute-start(bf16[160,2176]{1,0:T(8,128)(2,1)S(1)} %pad_maximum_fusion.refs_1_), channel_id=1, source_target_pairs={{16,0},{24,8},{17,1},{25,9},{18,2},{26,10},{19,3},{27,11},{4,16},{... | collective-permute-start | bytes 2088968 | tf_op jit(solution)/shard_map/ppermute | solution.py:56
  28.4 2.6 %collective-permute-start.12 = (bf16[160,2048]{1,0:T(8,128)(2,1)S(1)}, bf16[160,2048]{1,0:T(8,128)(2,1)S(1)}, u32[]{:S(2)}, u32[]{:S(2)}) collective-permute-start(bf16[160,2048]{1,0:T(8,128)(2,1)S(1)} %pad_maximum_fusion.1.refs_6_), channel_id=1, source_target_pairs={{3,0},{11,8},{0,1},{8,9},{1,2},{9,10},{2,3},{10,11},{19,16},{27,24... | collective-permute-start | bytes 1966088 | tf_op jit(solution)/shard_map/ppermute | solution.py:50
  30.9 0.3 collective-permute-start.10
  31.2 10.1 %collective-permute-done.8.refs_5_ = bf16[160,2176]{1,0:T(8,128)(2,1)S(1)} collective-permute-done((bf16[160,2176]{1,0:T(8,128)(2,1)S(1)}, bf16[160,2176]{1,0:T(8,128)(2,1)S(1)}, u32[]{:S(2)}, u32[]{:S(2)}) %collective-permute-start.8) | collective-permute-done | bytes 696352 | tf_op jit(solution)/shard_map/ppermute | solution.py:56
  41.3 0.1 collective-permute-start.9
  41.4 0.0 collective-permute-done.6.refs_2_
  41.4 0.0 copy-start.9
  41.4 2.7 %collective-permute-start.7 = (bf16[80,2176]{1,0:T(8,128)(2,1)S(1)}, bf16[80,2176]{1,0:T(8,128)(2,1)}, u32[]{:S(2)}, u32[]{:S(2)}) collective-permute-start(bf16[80,2176]{1,0:T(8,128)(2,1)S(1)} %slice.16), channel_id=1, source_target_pairs={{16,0},{24,8},{17,1},{25,9},{18,2},{26,10},{19,3},{27,11},{4,16},{... | collective-permute-start | bytes 1044488 | tf_op jit(solution)/shard_map/ppermute | solution.py:56
  44.2 0.0 collective-permute-done.12.refs_10_
  44.2 0.0 copy-done.7
  44.2 4.2 %collective-permute-start.13 = (bf16[80,2048]{1,0:T(8,128)(2,1)S(1)}, bf16[80,2048]{1,0:T(8,128)(2,1)}, u32[]{:S(2)}, u32[]{:S(2)}) collective-permute-start(bf16[80,2048]{1,0:T(8,128)(2,1)S(1)} %slice.19), channel_id=1, source_target_pairs={{3,0},{11,8},{0,1},{8,9},{1,2},{9,10},{2,3},{10,11},{19,16},{27,24... | collective-permute-start | bytes 983048 | tf_op jit(solution)/shard_map/ppermute | solution.py:50
  48.4 0.0 collective-permute-done.10.refs_7_
  48.4 0.3 collective-permute-start.11
  48.7 0.0 copy-done.9
  48.7 0.0 copy-done.11
  48.7 0.5 copy-done.12
  49.2 0.7 pad_add_fusion.at_ref
  49.9 3.1 %collective-permute-done.13.refs_9_ = bf16[80,2048]{1,0:T(8,128)(2,1)} collective-permute-done((bf16[80,2048]{1,0:T(8,128)(2,1)S(1)}, bf16[80,2048]{1,0:T(8,128)(2,1)}, u32[]{:S(2)}, u32[]{:S(2)}) %collective-permute-start.13) | collective-permute-done | bytes 327712 | tf_op jit(solution)/shard_map/ppermute | solution.py:50
  53.0 2.0 %collective-permute-done.11.refs_8_ = bf16[80,2048]{1,0:T(8,128)(2,1)S(1)} collective-permute-done((bf16[80,2048]{1,0:T(8,128)(2,1)S(1)}, bf16[80,2048]{1,0:T(8,128)(2,1)S(1)}, u32[]{:S(2)}, u32[]{:S(2)}) %collective-permute-start.11) | collective-permute-done | bytes 327712 | tf_op jit(solution)/shard_map/ppermute | solution.py:50
  55.0 0.0 collective-permute-done.9.refs_4_
  55.0 0.0 collective-permute-done.7.refs_3_
  55.0 3.1 %all-gather.2.cloned.1.call-done.refs_0_ = bf16[640,4224]{1,0:T(8,128)(2,1)} async-done(((bf16[40,4224]{1,0:T(8,128)(2,1)}), bf16[640,4224]{1,0:T(8,128)(2,1)}) %all-gather.2.cloned.1.call-update) | async-done | bytes 5406736 | tf_op jit(solution)/shard_map/all_gather | solution.py:348
  58.1 10.4 %tile.1 = (f32[640,640]{1,0:T(8,128)}, f32[32,352]{1,0:T(8,128)}, f32[32,352]{1,0:T(8,128)}, f32[32,640]{1,0:T(8,128)}, f32[32,640]{1,0:T(8,128)}, /*index=5*/f32[32,32]{1,0:T(8,128)}) custom-call(s32[4]{0:T(128)} %pad_add_fusion.at_ref, bf16[640,4224]{1,0:T(8,128)(2,1)} %all-gather.2.cloned.1.call-done.refs_0_, bf16[160,2176]{1,0:T(8,128)(2,1)} %copy-done.6, ...), custom_call_target="tpu_custom_call" | custom-call | flops 6710886400 | bytes 10485760 | tf_op jit(solution)/shard_map/tile/pallas_call | solution.py:357
  68.4 1.7 %collective-permute-start.14 = (f32[32,352]{1,0:T(8,128)}, f32[32,352]{1,0:T(8,128)S(1)}, u32[]{:S(2)}, u32[]{:S(2)}) collective-permute-start(f32[32,352]{1,0:T(8,128)} %get-tuple-element.29), channel_id=1, source_target_pairs={{8,0},{0,8},{9,1},{1,9},{10,2},{2,10},{11,3},{3,11},{24,16},{16,24... | collective-permute-start | bytes 135176 | tf_op jit(solution)/shard_map/ppermute | solution.py:62
  70.1 1.1 collective-permute-done.14.b_ref
  71.2 0.8 copy-done.4
  72.0 0.8 share.1
  72.8 8.5 %all-to-all-start = ((f32[8,32,352]{2,1,0:T(8,128)}), f32[8,32,352]{2,1,0:T(8,128)S(1)}, u32[]{:S(2)}, u32[]{:S(2)}) async-start(f32[8,32,352]{2,1,0:T(8,128)} %share.1), calls=%async_computation | async-start | bytes 786432 | tf_op jit(solution)/shard_map/all_to_all | solution.py:68
  81.3 15.1 %all-to-all-done.part_ref = f32[8,32,352]{2,1,0:T(8,128)S(1)} async-done(((f32[8,32,352]{2,1,0:T(8,128)}), f32[8,32,352]{2,1,0:T(8,128)S(1)}, u32[]{:S(2)}, u32[]{:S(2)}) %all-to-all-start) | async-done | bytes 360480 | tf_op jit(solution)/shard_map/all_to_all | solution.py:68
  96.4 0.9 copy-done.1
  97.3 0.3 line.1
  97.6 0.5 collective-permute-start.15
  98.2 0.1 constant_dynamic-slice_fusion.own_ref
  98.2 0.8 collective-permute-done.15.far_ref.refs_3_
  99.0 0.1 spread.1
  99.1 11.0 %all_to_all.20.refs_0_ = f32[16,32,104]{2,1,0:T(8,128)S(1)} all-to-all(f32[16,32,104]{2,1,0:T(8,128)S(1)} %spread.1), channel_id=1, replica_groups={{0,1,2,3,16,17,18,19,4,5,6,7,20,21,22,23},{8,9,10,11,24,25,26,27,12,13,..., dimensions={0} | all-to-all | bytes 425984 | tf_op jit(solution)/shard_map/all_to_all | solution.py:68
  110.1 0.0 copy-done.5
  110.1 4.8 %step.1 = (f32[16,32,72]{2,1,0:T(8,128)S(1)}, f32[32,40]{1,0:T(8,128)S(1)}, f32[32,40]{1,0:T(8,128)S(1)}, f32[32,40]{1,0:T(8,128)S(1)}, f32[32,32]{1,0:T(8,128)S(1)}) custom-call(s32[4]{0:T(128)S(1)} %copy-done.5, f32[16,32,104]{2,1,0:T(8,128)S(1)} %all_to_all.20.refs_0_, f32[32,32]{1,0:T(8,128)S(1)} %get-tuple-element.32.refs_1_, ...), custom_call_target="tpu_custom_call" | custom-call | tf_op jit(solution)/shard_map/step/pallas_call | solution.py:86
  114.9 10.2 %all_to_all.21.got_ref = f32[16,32,72]{2,1,0:T(8,128)S(1)} all-to-all(f32[16,32,72]{2,1,0:T(8,128)S(1)} %get-tuple-element.35), channel_id=1, replica_groups={{0,1,2,3,16,17,18,19,4,5,6,7,20,21,22,23},{8,9,10,11,24,25,26,27,12,13,..., dimensions={0} | all-to-all | bytes 294912 | tf_op jit(solution)/shard_map/all_to_all | solution.py:68
  125.1 0.1 image.1
  125.2 12.3 %all_to_all.22.got_ref = f32[16,8,128]{2,1,0:T(8,128)S(1)} all-to-all(f32[16,8,128]{2,1,0:T(8,128)S(1)} %get-tuple-element.37), channel_id=1, replica_groups={{0,32,64,96,128,160,192,224,8,40,72,104,136,168,200,232},{1,33,65,97,12..., dimensions={0} | all-to-all | bytes 131072 | tf_op jit(solution)/shard_map/all_to_all | solution.py:68
  137.5 1.8 %last.1 = (f32[32,40]{1,0:T(8,128)}, f32[32,40]{1,0:T(8,128)}) custom-call(f32[16,8,128]{2,1,0:T(8,128)S(1)} %all_to_all.22.got_ref, f32[32,32]{1,0:T(8,128)S(1)} %get-tuple-element.38.rr, f32[32,40]{1,0:T(8,128)S(1)} %get-tuple-element.36.d_ref.d_own, f32[32,40]{1,0:T(8,128)S(1)} %get-tuple-element.39.image, f32[32,40]{1,0:T(8,128)S(1)} %get-tuple-element.40.weights, ...), custom_call_target="tpu_custom_call" | custom-call | tf_op jit(solution)/shard_map/last/pallas_call | solution.py:86
  (22 shorter events, 0.1 us)
Async XLA Ops:
  7.2 50.9 %all-gather.2.cloned.1.call-start = ((), (), s32[]{:S(2)}) async-start(), calls=%async_computation.4 | async-start | bytes 5744640 | tf_op jit(solution)/shard_map/all_gather | solution.py:348
  9.4 16.2 %copy-start.10 = (bf16[40,2176]{1,0:T(8,128)(2,1)S(1)}, bf16[40,2176]{1,0:T(8,128)(2,1)}, u32[]{:S(2)}) copy-start(bf16[40,2176]{1,0:T(8,128)(2,1)} %get-tuple-element.24) | copy-start | bytes 522244
  9.4 9.6 %collective-permute-start.5 = (bf16[40,2048]{1,0:T(8,128)(2,1)}, bf16[40,2048]{1,0:T(8,128)(2,1)S(1)}, u32[]{:S(2)}, u32[]{:S(2)}) collective-permute-start(bf16[40,2048]{1,0:T(8,128)(2,1)} %get-tuple-element.25), channel_id=1, source_target_pairs={{20,0},{28,8},{21,1},{29,9},{22,2},{30,10},{23,3},{31,11},{0,16},{... | collective-permute-start | bytes 491528 | tf_op jit(solution)/shard_map/ppermute | solution.py:56
  11.6 9.9 %collective-permute-start.4 = (bf16[40,2048]{1,0:T(8,128)(2,1)}, bf16[40,2048]{1,0:T(8,128)(2,1)S(1)}, u32[]{:S(2)}, u32[]{:S(2)}) collective-permute-start(bf16[40,2048]{1,0:T(8,128)(2,1)} %get-tuple-element.25), channel_id=1, source_target_pairs={{4,0},{12,8},{5,1},{13,9},{6,2},{14,10},{7,3},{15,11},{20,16},{28,... | collective-permute-start | bytes 491528 | tf_op jit(solution)/shard_map/ppermute | solution.py:56
  14.2 7.3 %collective-permute-start.3 = (bf16[40,2048]{1,0:T(8,128)(2,1)}, bf16[40,2048]{1,0:T(8,128)(2,1)S(1)}, u32[]{:S(2)}, u32[]{:S(2)}) collective-permute-start(bf16[40,2048]{1,0:T(8,128)(2,1)} %get-tuple-element.25), channel_id=1, source_target_pairs={{16,0},{24,8},{17,1},{25,9},{18,2},{26,10},{19,3},{27,11},{4,16},{... | collective-permute-start | bytes 491528 | tf_op jit(solution)/shard_map/ppermute | solution.py:56
  15.3 7.2 %collective-permute-start.2 = (bf16[40,2176]{1,0:T(8,128)(2,1)}, bf16[40,2176]{1,0:T(8,128)(2,1)S(1)}, u32[]{:S(2)}, u32[]{:S(2)}) collective-permute-start(bf16[40,2176]{1,0:T(8,128)(2,1)} %get-tuple-element.24), channel_id=1, source_target_pairs={{3,0},{11,8},{0,1},{8,9},{1,2},{9,10},{2,3},{10,11},{19,16},{27,24... | collective-permute-start | bytes 522248 | tf_op jit(solution)/shard_map/ppermute | solution.py:50
  16.5 9.0 %collective-permute-start.1 = (bf16[40,2176]{1,0:T(8,128)(2,1)}, bf16[40,2176]{1,0:T(8,128)(2,1)S(1)}, u32[]{:S(2)}, u32[]{:S(2)}) collective-permute-start(bf16[40,2176]{1,0:T(8,128)(2,1)} %get-tuple-element.24), channel_id=1, source_target_pairs={{2,0},{10,8},{3,1},{11,9},{0,2},{8,10},{1,3},{9,11},{18,16},{26,24... | collective-permute-start | bytes 522248 | tf_op jit(solution)/shard_map/ppermute | solution.py:50
  19.0 6.6 %collective-permute-start = (bf16[40,2176]{1,0:T(8,128)(2,1)}, bf16[40,2176]{1,0:T(8,128)(2,1)S(1)}, u32[]{:S(2)}, u32[]{:S(2)}) collective-permute-start(bf16[40,2176]{1,0:T(8,128)(2,1)} %get-tuple-element.24), channel_id=1, source_target_pairs={{1,0},{9,8},{2,1},{10,9},{3,2},{11,10},{0,3},{8,11},{17,16},{25,24... | collective-permute-start | bytes 522248 | tf_op jit(solution)/shard_map/ppermute | solution.py:50
  22.5 21.7 %copy-start.7 = (bf16[160,2048]{1,0:T(8,128)(2,1)}, bf16[160,2048]{1,0:T(8,128)(2,1)S(1)}, u32[]{:S(2)}) copy-start(bf16[160,2048]{1,0:T(8,128)(2,1)S(1)} %pad_maximum_fusion.1.refs_6_) | copy-start | bytes 1966084
  25.6 23.6 %copy-start.6 = (bf16[160,2176]{1,0:T(8,128)(2,1)}, bf16[160,2176]{1,0:T(8,128)(2,1)S(1)}, u32[]{:S(2)}) copy-start(bf16[160,2176]{1,0:T(8,128)(2,1)S(1)} %pad_maximum_fusion.refs_1_) | copy-start | bytes 2088964
  25.6 15.7 %collective-permute-start.8 = (bf16[160,2176]{1,0:T(8,128)(2,1)S(1)}, bf16[160,2176]{1,0:T(8,128)(2,1)S(1)}, u32[]{:S(2)}, u32[]{:S(2)}) collective-permute-start(bf16[160,2176]{1,0:T(8,128)(2,1)S(1)} %pad_maximum_fusion.refs_1_), channel_id=1, source_target_pairs={{20,0},{28,8},{21,1},{29,9},{22,2},{30,10},{23,3},{31,11},{0,16},{... | collective-permute-start | bytes 2088968 | tf_op jit(solution)/shard_map/ppermute | solution.py:56
  26.1 15.3 %collective-permute-start.6 = (bf16[160,2176]{1,0:T(8,128)(2,1)S(1)}, bf16[160,2176]{1,0:T(8,128)(2,1)S(1)}, u32[]{:S(2)}, u32[]{:S(2)}) collective-permute-start(bf16[160,2176]{1,0:T(8,128)(2,1)S(1)} %pad_maximum_fusion.refs_1_), channel_id=1, source_target_pairs={{16,0},{24,8},{17,1},{25,9},{18,2},{26,10},{19,3},{27,11},{4,16},{... | collective-permute-start | bytes 2088968 | tf_op jit(solution)/shard_map/ppermute | solution.py:56
  28.4 15.8 %collective-permute-start.12 = (bf16[160,2048]{1,0:T(8,128)(2,1)S(1)}, bf16[160,2048]{1,0:T(8,128)(2,1)S(1)}, u32[]{:S(2)}, u32[]{:S(2)}) collective-permute-start(bf16[160,2048]{1,0:T(8,128)(2,1)S(1)} %pad_maximum_fusion.1.refs_6_), channel_id=1, source_target_pairs={{3,0},{11,8},{0,1},{8,9},{1,2},{9,10},{2,3},{10,11},{19,16},{27,24... | collective-permute-start | bytes 1966088 | tf_op jit(solution)/shard_map/ppermute | solution.py:50
  30.9 17.4 %collective-permute-start.10 = (bf16[160,2048]{1,0:T(8,128)(2,1)S(1)}, bf16[160,2048]{1,0:T(8,128)(2,1)S(1)}, u32[]{:S(2)}, u32[]{:S(2)}) collective-permute-start(bf16[160,2048]{1,0:T(8,128)(2,1)S(1)} %pad_maximum_fusion.1.refs_6_), channel_id=1, source_target_pairs={{1,0},{9,8},{2,1},{10,9},{3,2},{11,10},{0,3},{8,11},{17,16},{25,24... | collective-permute-start | bytes 1966088 | tf_op jit(solution)/shard_map/ppermute | solution.py:50
  41.3 8.0 %copy-start.8 = (bf16[160,2176]{1,0:T(8,128)(2,1)}, bf16[160,2176]{1,0:T(8,128)(2,1)S(1)}, u32[]{:S(2)}) copy-start(bf16[160,2176]{1,0:T(8,128)(2,1)S(1)} %collective-permute-done.8.refs_5_) | copy-start | bytes 2088964
  41.3 13.7 %collective-permute-start.9 = (bf16[80,2176]{1,0:T(8,128)(2,1)S(1)}, bf16[80,2176]{1,0:T(8,128)(2,1)S(1)}, u32[]{:S(2)}, u32[]{:S(2)}) collective-permute-start(bf16[80,2176]{1,0:T(8,128)(2,1)S(1)} %slice.17), channel_id=1, source_target_pairs={{20,0},{28,8},{21,1},{29,9},{22,2},{30,10},{23,3},{31,11},{0,16},{... | collective-permute-start | bytes 1044488 | tf_op jit(solution)/shard_map/ppermute | solution.py:56
  41.4 7.3 %copy-start.9 = (bf16[160,2176]{1,0:T(8,128)(2,1)}, bf16[160,2176]{1,0:T(8,128)(2,1)S(1)}, u32[]{:S(2)}) copy-start(bf16[160,2176]{1,0:T(8,128)(2,1)S(1)} %collective-permute-done.6.refs_2_) | copy-start | bytes 2088964
  41.4 13.5 %collective-permute-start.7 = (bf16[80,2176]{1,0:T(8,128)(2,1)S(1)}, bf16[80,2176]{1,0:T(8,128)(2,1)}, u32[]{:S(2)}, u32[]{:S(2)}) collective-permute-start(bf16[80,2176]{1,0:T(8,128)(2,1)S(1)} %slice.16), channel_id=1, source_target_pairs={{16,0},{24,8},{17,1},{25,9},{18,2},{26,10},{19,3},{27,11},{4,16},{... | collective-permute-start | bytes 1044488 | tf_op jit(solution)/shard_map/ppermute | solution.py:56
  44.2 4.5 %copy-start.11 = (bf16[160,2048]{1,0:T(8,128)(2,1)}, bf16[160,2048]{1,0:T(8,128)(2,1)S(1)}, u32[]{:S(2)}) copy-start(bf16[160,2048]{1,0:T(8,128)(2,1)S(1)} %collective-permute-done.12.refs_10_) | copy-start | bytes 1966084
  44.2 8.8 %collective-permute-start.13 = (bf16[80,2048]{1,0:T(8,128)(2,1)S(1)}, bf16[80,2048]{1,0:T(8,128)(2,1)}, u32[]{:S(2)}, u32[]{:S(2)}) collective-permute-start(bf16[80,2048]{1,0:T(8,128)(2,1)S(1)} %slice.19), channel_id=1, source_target_pairs={{3,0},{11,8},{0,1},{8,9},{1,2},{9,10},{2,3},{10,11},{19,16},{27,24... | collective-permute-start | bytes 983048 | tf_op jit(solution)/shard_map/ppermute | solution.py:50
  48.4 0.9 copy-start.12
  48.4 6.6 %collective-permute-start.11 = (bf16[80,2048]{1,0:T(8,128)(2,1)S(1)}, bf16[80,2048]{1,0:T(8,128)(2,1)S(1)}, u32[]{:S(2)}, u32[]{:S(2)}) collective-permute-start(bf16[80,2048]{1,0:T(8,128)(2,1)S(1)} %slice.18), channel_id=1, source_target_pairs={{1,0},{9,8},{2,1},{10,9},{3,2},{11,10},{0,3},{8,11},{17,16},{25,24... | collective-permute-start | bytes 983048 | tf_op jit(solution)/shard_map/ppermute | solution.py:50
  55.0 3.1 %copy-start.14 = (bf16[80,2048]{1,0:T(8,128)(2,1)}, bf16[80,2048]{1,0:T(8,128)(2,1)S(1)}, u32[]{:S(2)}) copy-start(bf16[80,2048]{1,0:T(8,128)(2,1)S(1)} %collective-permute-done.11.refs_8_) | copy-start | bytes 983044
  55.0 3.1 %copy-start.13 = (bf16[80,2176]{1,0:T(8,128)(2,1)}, bf16[80,2176]{1,0:T(8,128)(2,1)S(1)}, u32[]{:S(2)}) copy-start(bf16[80,2176]{1,0:T(8,128)(2,1)S(1)} %collective-permute-done.9.refs_4_) | copy-start | bytes 1044484
  58.1 52.0 %copy-start.5 = (s32[4]{0:T(128)S(1)}, s32[4]{0:T(128)}, u32[]{:S(2)}) copy-start(s32[4]{0:T(128)} %pad_add_fusion.at_ref) | copy-start | bytes 52
  68.4 41.7 %copy-start = (f32[640,640]{1,0:T(8,128)S(1)}, f32[640,640]{1,0:T(8,128)}, u32[]{:S(2)}) copy-start(f32[640,640]{1,0:T(8,128)} %get-tuple-element.34.refs_6_) | copy-start | bytes 4915204
  68.4 2.8 %collective-permute-start.14 = (f32[32,352]{1,0:T(8,128)}, f32[32,352]{1,0:T(8,128)S(1)}, u32[]{:S(2)}, u32[]{:S(2)}) collective-permute-start(f32[32,352]{1,0:T(8,128)} %get-tuple-element.29), channel_id=1, source_target_pairs={{8,0},{0,8},{9,1},{1,9},{10,2},{2,10},{11,3},{3,11},{24,16},{16,24... | collective-permute-start | bytes 135176 | tf_op jit(solution)/shard_map/ppermute | solution.py:62
  71.2 0.8 copy-start.4
  72.8 23.7 %all-to-all-start = ((f32[8,32,352]{2,1,0:T(8,128)}), f32[8,32,352]{2,1,0:T(8,128)S(1)}, u32[]{:S(2)}, u32[]{:S(2)}) async-start(f32[8,32,352]{2,1,0:T(8,128)} %share.1), calls=%async_computation | async-start | bytes 786432 | tf_op jit(solution)/shard_map/all_to_all | solution.py:68
  96.4 0.9 copy-start.1
  97.3 12.8 %copy-start.2 = (f32[32,640]{1,0:T(8,128)S(1)}, f32[32,640]{1,0:T(8,128)}, u32[]{:S(2)}) copy-start(f32[32,640]{1,0:T(8,128)} %get-tuple-element.30.t_ref.refs_4_) | copy-start | bytes 245764
  97.3 12.8 %copy-start.3 = (f32[32,640]{1,0:T(8,128)S(1)}, f32[32,640]{1,0:T(8,128)}, u32[]{:S(2)}) copy-start(f32[32,640]{1,0:T(8,128)} %get-tuple-element.33.refs_5_) | copy-start | bytes 245764
  97.6 1.4 collective-permute-start.15
Sparse Core Ops, SparseCore 0:
  9.8 48.1 all-gather.1

commit v7 on v6

--- a/solution.py
+++ b/solution.py
@@ -188,30 +188,49 @@
             ty_ref[...] = ty
             n0 = nt(ty, ty)
             n0_ref[...] = n0
-            near_ref[:, line:] = n0
+            near_ref[:rhs, line:] = n0
             far_ref[:, line:] = n0
     for y in range(4):
         for x in range(4):
             to, of = pl.ds((4 * y + x) * rows, rows), pl.ds((4 * x + y) * rows, rows)
             k_ref[to, :] = jnp.exp(sharpness * (k_ref[to, :] + cos_ref[of, :] - 1.0))
-    tx_ref[...] = targets_of(x_ref[:, 2 * half :], rhs)
+    tx = targets_of(x_ref[:, 2 * half :], rhs)
+    tx_ref[...] = tx
+    near_ref[rhs:, :line] = tx[:, :line]
+    near_ref[rhs:, line:] = jnp.zeros((rhs, rhs), F32)
     product = mm(ty_ref[...], k_ref[...])
-    near_ref[:, :line] = product[:, :line]
+    near_ref[:rhs, :line] = product[:, :line]
     far_ref[:, :line] = product[:, line:]
 
 
-def share_kernel(count, a_ref, b_ref, out_ref):
-    value = a_ref[...] + b_ref[...]
-    for i in range(count):
-        out_ref[i] = value
+def share_kernel(line, near_ref, far_ref, out_ref, t_ref):
+    t_ref[...] = near_ref[far_ref.shape[0] :, :line]
+    value = near_ref[: far_ref.shape[0]] + far_ref[...]
+    rhs = value.shape[0]
+    whole, half = line // 128 * 128, rhs // 2
+    rest, gram = value[:, whole:line], value[:, line:]
+    parts = [value[:, i : i + 128] for i in range(0, whole, 128)]
+    parts.append(jnp.concatenate([rest[:half], rest[half:]], axis=1))
+    parts.append(jnp.concatenate([gram[8 * i : 8 * i + 8] for i in range(4)], axis=1))
+    at = 0
+    for part in parts:
+        out_ref[0, at : at + part.shape[0]] = part
+        at += part.shape[0]
+    dense = out_ref[0]
+    for i in range(1, NZ):
+        out_ref[i] = dense
 
 
 def line_kernel(line, part_ref, t_ref, send_ref, n0_ref):
-    part = jnp.sum(part_ref[...], axis=0)
-    rhs = part.shape[0]
-    t = t_ref[:, :line]
-    w = part[:, :line] - t
-    n0_ref[...] = part[:, line:]
+    dense = jnp.sum(part_ref[...], axis=0)
+    rhs = send_ref.shape[0]
+    whole, half = line // 128, rhs // 2
+    parts = [dense[rhs * i : rhs * (i + 1)] for i in range(whole)]
+    rest, gram = dense[rhs * whole : rhs * whole + half], dense[rhs * whole + half :]
+    parts.append(jnp.concatenate([rest[:, :64], rest[:, 64:]], axis=0))
+    t = t_ref[...]
+    w = jnp.concatenate(parts, axis=1) - t
+    n0_ref[...] = jnp.concatenate([gram[:, rhs * i : rhs * (i + 1)] for i in range(4)], axis=0)
     send_ref[:, :line] = w
     send_ref[:, line : line + rhs] = nt(t, w)
     send_ref[:, line + rhs :] = nt(w, w)
@@ -358,7 +377,7 @@
         functools.partial(tile_kernel, *sizes),
         out_shape=(
             shape(plane, NC * line),
-            shape(rhs, line + rhs),
+            shape(2 * rhs, line + rhs),
             shape(rhs, line + rhs),
             shape(rhs, NC * line),
             shape(rhs, plane),
@@ -373,7 +392,7 @@
             pltpu.VMEM((plane, NC * line), F32),
             pltpu.SemaphoreType.DMA((4, NC + 5)),
         ],
-        compiler_params=pltpu.CompilerParams(vmem_limit_bytes=57 * MIB),
+        compiler_params=pltpu.CompilerParams(vmem_limit_bytes=52 * MIB),
         cost_estimate=pl.CostEstimate(
             flops=4 * plane * NC * line * 2 * half,
             bytes_accessed=2 * (plane + NC * line) * 2 * half,
@@ -382,16 +401,16 @@
         name="tile",
     )(at, tube, *a, *b)
 
-    copies = small_kernel(
-        functools.partial(share_kernel, NZ),
-        shape(NZ, rhs, line + rhs),
+    copies, t_line = small_kernel(
+        functools.partial(share_kernel, line),
+        (shape(NZ, rhs * (line + rhs) // 128, 128), shape(rhs, line)),
         (near, other_core(far)),
         name="share",
     )
     sent, n0 = small_kernel(
         functools.partial(line_kernel, line),
         (shape(rhs, line + 2 * rhs), shape(rhs, rhs)),
-        (exchange(copies, LINES), t_tube),
+        (exchange(copies, LINES), t_line),
         name="line",
     )
     w_own = lax.dynamic_slice(sent, (0, z * rows), (rhs, rows))

time: 147 us -> 144 us (0.980)
    unnamed x30 -> x16, local copies, waits for them, and re-layouts: 2.28 us -> 0.55 us
where the time goes in v7:
time: 144 us; the launch traced here: 143 us
  waiting for transfers between devices  38.7 us (27%)
  starting transfers between devices  34.1 us (24%)
  blocking collectives  33.4 us (23%)
  Pallas kernels  20.1 us (14%)
  between operations  14.2 us (10%)
  local copies, waits for them, and re-layouts  1.55 us (1%)
    all_to_all x3, blocking collectives, exchange(): lax.all_to_all(chunks, AXES, 0, 0, axis_index_groups=groups, tiled=True)  33.4 us
    all_to_all x1, waiting for transfers between devices, exchange(): lax.all_to_all(chunks, AXES, 0, 0, axis_index_groups=groups, tiled=True)  14.4 us
    ppermute x7, starting transfers between devices, from_x(): lax.ppermute(value, AXES, [(device(z, y, x + k, c), device(z, y, x, c)) f...  12 us
    ppermute x7, waiting for transfers between devices, from_y(): lax.ppermute(value, AXES, [(device(z, y + k, x, c), device(z, y, x, c)) f...  11.5 us
    ppermute x7, starting transfers between devices, from_y(): lax.ppermute(value, AXES, [(device(z, y + k, x, c), device(z, y, x, c)) f...  11.4 us
    pallas_call x7, Pallas kernels, small_kernel(): pl.pallas_call(body, out_shape=out, in_specs=specs or [VM] * len(args), o...  10.2 us
    pallas_call x1, Pallas kernels, local(): pl.pallas_call(functools.partial(tile_kernel, *sizes), out_shape=(shape(p...  9.98 us
    ppermute x7, waiting for transfers between devices, from_x(): lax.ppermute(value, AXES, [(device(z, y, x + k, c), device(z, y, x, c)) f...  8.56 us
  transfers between devices with their start and end apart: 18, of which 9 were waited for; matrix products, arithmetic and copies ran while one was open for 1% of the time, Pallas kernels for 0%

profile of v7, /device:TPU:1, one launch (start us, length us, event | category | flops | bytes accessed | tf_op | source)
XLA Modules:
  0.0 143.2 jit_solution(16249732122698253465)
XLA Ops:
  7.2 0.0 all-gather.2.cloned.1.call-start
  7.2 2.1 %prepare.1 = (bf16[40,4224]{1,0:T(8,128)(2,1)}, bf16[40,2176]{1,0:T(8,128)(2,1)}, bf16[40,2048]{1,0:T(8,128)(2,1)}) custom-call(f32[40,4096]{1,0:T(8,128)} %s_hbm.1, f32[32,40]{1,0:T(8,128)} %bitcast.7), custom_call_target="tpu_custom_call" | custom-call | tf_op jit(solution)/shard_map/prepare/pallas_call | solution.py:86
  9.4 0.0 copy-start.5
  9.4 0.0 all-gather.2.cloned.1.call-update
  9.4 2.2 %collective-permute-start.5 = (bf16[40,2048]{1,0:T(8,128)(2,1)}, bf16[40,2048]{1,0:T(8,128)(2,1)S(1)}, u32[]{:S(2)}, u32[]{:S(2)}) collective-permute-start(bf16[40,2048]{1,0:T(8,128)(2,1)} %get-tuple-element.27), channel_id=1, source_target_pairs={{20,0},{28,8},{21,1},{29,9},{22,2},{30,10},{23,3},{31,11},{0,16},{... | collective-permute-start | bytes 491528 | tf_op jit(solution)/shard_map/ppermute | solution.py:56
  11.6 2.6 %collective-permute-start.4 = (bf16[40,2048]{1,0:T(8,128)(2,1)}, bf16[40,2048]{1,0:T(8,128)(2,1)S(1)}, u32[]{:S(2)}, u32[]{:S(2)}) collective-permute-start(bf16[40,2048]{1,0:T(8,128)(2,1)} %get-tuple-element.27), channel_id=1, source_target_pairs={{4,0},{12,8},{5,1},{13,9},{6,2},{14,10},{7,3},{15,11},{20,16},{28,... | collective-permute-start | bytes 491528 | tf_op jit(solution)/shard_map/ppermute | solution.py:56
  14.2 1.1 collective-permute-start.3
  15.3 1.2 collective-permute-start.2
  16.5 2.5 %collective-permute-start.1 = (bf16[40,2176]{1,0:T(8,128)(2,1)}, bf16[40,2176]{1,0:T(8,128)(2,1)S(1)}, u32[]{:S(2)}, u32[]{:S(2)}) collective-permute-start(bf16[40,2176]{1,0:T(8,128)(2,1)} %get-tuple-element.26), channel_id=1, source_target_pairs={{2,0},{10,8},{3,1},{11,9},{0,2},{8,10},{1,3},{9,11},{18,16},{26,24... | collective-permute-start | bytes 522248 | tf_op jit(solution)/shard_map/ppermute | solution.py:50
  18.9 0.0 collective-permute-done.5
  18.9 1.2 collective-permute-start
  20.1 1.4 %collective-permute-done.4 = bf16[40,2048]{1,0:T(8,128)(2,1)S(1)} collective-permute-done((bf16[40,2048]{1,0:T(8,128)(2,1)}, bf16[40,2048]{1,0:T(8,128)(2,1)S(1)}, u32[]{:S(2)}, u32[]{:S(2)}) %collective-permute-start.4) | collective-permute-done | bytes 163872 | tf_op jit(solution)/shard_map/ppermute | solution.py:56
  21.5 0.0 collective-permute-done.3
  21.5 1.0 pad_maximum_fusion.1.refs_6_
  22.5 0.0 copy-start.2
  22.5 0.0 collective-permute-done.2
  22.5 3.0 %collective-permute-done.1 = bf16[40,2176]{1,0:T(8,128)(2,1)S(1)} collective-permute-done((bf16[40,2176]{1,0:T(8,128)(2,1)}, bf16[40,2176]{1,0:T(8,128)(2,1)S(1)}, u32[]{:S(2)}, u32[]{:S(2)}) %collective-permute-start.1) | collective-permute-done | bytes 174112 | tf_op jit(solution)/shard_map/ppermute | solution.py:50
  25.5 0.0 collective-permute-done
  25.5 0.0 copy-done.5
  25.5 0.1 pad_maximum_fusion.refs_1_
  25.6 0.0 copy-start.1
  25.6 0.5 collective-permute-start.8
  26.1 2.3 %collective-permute-start.6 = (bf16[160,2176]{1,0:T(8,128)(2,1)S(1)}, bf16[160,2176]{1,0:T(8,128)(2,1)S(1)}, u32[]{:S(2)}, u32[]{:S(2)}) collective-permute-start(bf16[160,2176]{1,0:T(8,128)(2,1)S(1)} %pad_maximum_fusion.refs_1_), channel_id=1, source_target_pairs={{16,0},{24,8},{17,1},{25,9},{18,2},{26,10},{19,3},{27,11},{4,16},{... | collective-permute-start | bytes 2088968 | tf_op jit(solution)/shard_map/ppermute | solution.py:56
  28.3 2.6 %collective-permute-start.12 = (bf16[160,2048]{1,0:T(8,128)(2,1)S(1)}, bf16[160,2048]{1,0:T(8,128)(2,1)S(1)}, u32[]{:S(2)}, u32[]{:S(2)}) collective-permute-start(bf16[160,2048]{1,0:T(8,128)(2,1)S(1)} %pad_maximum_fusion.1.refs_6_), channel_id=1, source_target_pairs={{3,0},{11,8},{0,1},{8,9},{1,2},{9,10},{2,3},{10,11},{19,16},{27,24... | collective-permute-start | bytes 1966088 | tf_op jit(solution)/shard_map/ppermute | solution.py:50
  30.9 0.3 collective-permute-start.10
  31.2 10.1 %collective-permute-done.8.refs_5_ = bf16[160,2176]{1,0:T(8,128)(2,1)S(1)} collective-permute-done((bf16[160,2176]{1,0:T(8,128)(2,1)S(1)}, bf16[160,2176]{1,0:T(8,128)(2,1)S(1)}, u32[]{:S(2)}, u32[]{:S(2)}) %collective-permute-start.8) | collective-permute-done | bytes 696352 | tf_op jit(solution)/shard_map/ppermute | solution.py:56
  41.3 0.1 collective-permute-start.9
  41.4 0.0 collective-permute-done.6.refs_2_
  41.4 0.0 copy-start.4
  41.4 2.7 %collective-permute-start.7 = (bf16[80,2176]{1,0:T(8,128)(2,1)S(1)}, bf16[80,2176]{1,0:T(8,128)(2,1)S(1)}, u32[]{:S(2)}, u32[]{:S(2)}) collective-permute-start(bf16[80,2176]{1,0:T(8,128)(2,1)S(1)} %slice.16), channel_id=1, source_target_pairs={{16,0},{24,8},{17,1},{25,9},{18,2},{26,10},{19,3},{27,11},{4,16},{... | collective-permute-start | bytes 1044488 | tf_op jit(solution)/shard_map/ppermute | solution.py:56
  44.1 0.0 collective-permute-done.12.refs_10_
  44.2 0.8 slice.19
  45.0 0.0 copy-done.2
  45.0 4.1 %collective-permute-start.13 = (bf16[80,2048]{1,0:T(8,128)(2,1)}, bf16[80,2048]{1,0:T(8,128)(2,1)S(1)}, u32[]{:S(2)}, u32[]{:S(2)}) collective-permute-start(bf16[80,2048]{1,0:T(8,128)(2,1)} %slice.19), channel_id=1, source_target_pairs={{3,0},{11,8},{0,1},{8,9},{1,2},{9,10},{2,3},{10,11},{19,16},{27,24... | collective-permute-start | bytes 983048 | tf_op jit(solution)/shard_map/ppermute | solution.py:50
  49.1 0.0 collective-permute-done.10.refs_7_
  49.1 0.3 collective-permute-start.11
  49.4 0.0 copy-done.3
  49.4 0.0 copy-done.4
  49.4 0.0 copy-done.6
  49.4 0.5 copy-done.7
  49.9 0.0 copy-done.1
  49.9 0.1 pad_add_fusion.at_ref
  50.0 3.7 %collective-permute-done.13.refs_9_ = bf16[80,2048]{1,0:T(8,128)(2,1)S(1)} collective-permute-done((bf16[80,2048]{1,0:T(8,128)(2,1)}, bf16[80,2048]{1,0:T(8,128)(2,1)S(1)}, u32[]{:S(2)}, u32[]{:S(2)}) %collective-permute-start.13) | collective-permute-done | bytes 327712 | tf_op jit(solution)/shard_map/ppermute | solution.py:50
  53.7 1.9 %collective-permute-done.11.refs_8_ = bf16[80,2048]{1,0:T(8,128)(2,1)S(1)} collective-permute-done((bf16[80,2048]{1,0:T(8,128)(2,1)S(1)}, bf16[80,2048]{1,0:T(8,128)(2,1)S(1)}, u32[]{:S(2)}, u32[]{:S(2)}) %collective-permute-start.11) | collective-permute-done | bytes 327712 | tf_op jit(solution)/shard_map/ppermute | solution.py:50
  55.6 0.0 collective-permute-done.9.refs_4_
  55.6 0.0 collective-permute-done.7.refs_3_
  55.6 2.4 %all-gather.2.cloned.1.call-done.refs_0_ = bf16[640,4224]{1,0:T(8,128)(2,1)} async-done(((bf16[40,4224]{1,0:T(8,128)(2,1)}), bf16[640,4224]{1,0:T(8,128)(2,1)}) %all-gather.2.cloned.1.call-update) | async-done | bytes 5406736 | tf_op jit(solution)/shard_map/all_gather | solution.py:367
  58.0 10.0 %tile.1 = (f32[640,640]{1,0:T(8,128)}, f32[64,352]{1,0:T(8,128)S(1)}, f32[32,352]{1,0:T(8,128)S(1)}, f32[32,640]{1,0:T(8,128)S(1)}, f32[32,640]{1,0:T(8,128)S(1)}, /*index=5*/f32[32,32]{1,0:T(8,128)}) custom-call(s32[4]{0:T(128)S(1)} %pad_add_fusion.at_ref, bf16[640,4224]{1,0:T(8,128)(2,1)} %all-gather.2.cloned.1.call-done.refs_0_, ...), custom_call_target="tpu_custom_call" | custom-call | flops 6710886400 | bytes 10485760 | tf_op jit(solution)/shard_map/tile/pallas_call | solution.py:376
  68.0 1.6 %collective-permute-start.14 = (f32[32,352]{1,0:T(8,128)S(1)}, f32[32,352]{1,0:T(8,128)S(1)}, u32[]{:S(2)}, u32[]{:S(2)}) collective-permute-start(f32[32,352]{1,0:T(8,128)S(1)} %get-tuple-element.31), channel_id=1, source_target_pairs={{8,0},{0,8},{9,1},{1,9},{10,2},{2,10},{11,3},{3,11},{24,16},{16,24... | collective-permute-start | bytes 135176 | tf_op jit(solution)/shard_map/ppermute | solution.py:62
  69.6 0.9 collective-permute-done.14.far_ref
  70.5 0.8 share.1
  71.3 8.5 %all-to-all-start = ((f32[8,88,128]{2,1,0:T(8,128)}), f32[8,88,128]{2,1,0:T(8,128)S(1)}, u32[]{:S(2)}, u32[]{:S(2)}) async-start(f32[8,88,128]{2,1,0:T(8,128)} %get-tuple-element.32), calls=%async_computation | async-start | bytes 720896 | tf_op jit(solution)/shard_map/all_to_all | solution.py:68
  79.8 14.4 %all-to-all-done.part_ref = f32[8,88,128]{2,1,0:T(8,128)S(1)} async-done(((f32[8,88,128]{2,1,0:T(8,128)}), f32[8,88,128]{2,1,0:T(8,128)S(1)}, u32[]{:S(2)}, u32[]{:S(2)}) %all-to-all-start) | async-done | bytes 360480 | tf_op jit(solution)/shard_map/all_to_all | solution.py:68
  94.2 0.4 line.1
  94.6 0.5 collective-permute-start.15
  95.1 0.1 constant_dynamic-slice_fusion.own_ref
  95.2 0.8 collective-permute-done.15.far_ref.refs_3_
  96.0 0.1 spread.1
  96.1 11.0 %all_to_all.20.refs_0_ = f32[16,32,104]{2,1,0:T(8,128)S(1)} all-to-all(f32[16,32,104]{2,1,0:T(8,128)S(1)} %spread.1), channel_id=1, replica_groups={{0,1,2,3,16,17,18,19,4,5,6,7,20,21,22,23},{8,9,10,11,24,25,26,27,12,13,..., dimensions={0} | all-to-all | bytes 425984 | tf_op jit(solution)/shard_map/all_to_all | solution.py:68
  107.1 4.8 %step.1 = (f32[16,32,72]{2,1,0:T(8,128)S(1)}, f32[32,40]{1,0:T(8,128)S(1)}, f32[32,40]{1,0:T(8,128)S(1)}, f32[32,40]{1,0:T(8,128)S(1)}, f32[32,32]{1,0:T(8,128)S(1)}) custom-call(s32[4]{0:T(128)S(1)} %pad_add_fusion.at_ref, f32[16,32,104]{2,1,0:T(8,128)S(1)} %all_to_all.20.refs_0_, f32[32,32]{1,0:T(8,128)S(1)} %get-tuple-element.35.refs_1_, ...), custom_call_target="tpu_custom_call" | custom-call | tf_op jit(solution)/shard_map/step/pallas_call | solution.py:86
  111.9 10.2 %all_to_all.21.got_ref = f32[16,32,72]{2,1,0:T(8,128)S(1)} all-to-all(f32[16,32,72]{2,1,0:T(8,128)S(1)} %get-tuple-element.39), channel_id=1, replica_groups={{0,1,2,3,16,17,18,19,4,5,6,7,20,21,22,23},{8,9,10,11,24,25,26,27,12,13,..., dimensions={0} | all-to-all | bytes 294912 | tf_op jit(solution)/shard_map/all_to_all | solution.py:68
  122.1 0.1 image.1
  122.2 12.3 %all_to_all.22.got_ref = f32[16,8,128]{2,1,0:T(8,128)S(1)} all-to-all(f32[16,8,128]{2,1,0:T(8,128)S(1)} %get-tuple-element.41), channel_id=1, replica_groups={{0,32,64,96,128,160,192,224,8,40,72,104,136,168,200,232},{1,33,65,97,12..., dimensions={0} | all-to-all | bytes 131072 | tf_op jit(solution)/shard_map/all_to_all | solution.py:68
  134.5 1.8 %last.1 = (f32[32,40]{1,0:T(8,128)}, f32[32,40]{1,0:T(8,128)}) custom-call(f32[16,8,128]{2,1,0:T(8,128)S(1)} %all_to_all.22.got_ref, f32[32,32]{1,0:T(8,128)S(1)} %get-tuple-element.42.rr, f32[32,40]{1,0:T(8,128)S(1)} %get-tuple-element.40.d_ref.d_own, f32[32,40]{1,0:T(8,128)S(1)} %get-tuple-element.43.image, f32[32,40]{1,0:T(8,128)S(1)} %get-tuple-element.44.weights, ...), custom_call_target="tpu_custom_call" | custom-call | tf_op jit(solution)/shard_map/last/pallas_call | solution.py:86
  (8 shorter events, 0.1 us)
Async XLA Ops:
  7.2 50.9 %all-gather.2.cloned.1.call-start = ((), (), s32[]{:S(2)}) async-start(), calls=%async_computation.4 | async-start | bytes 5744640 | tf_op jit(solution)/shard_map/all_gather | solution.py:367
  9.4 16.2 %copy-start.5 = (bf16[40,2176]{1,0:T(8,128)(2,1)S(1)}, bf16[40,2176]{1,0:T(8,128)(2,1)}, u32[]{:S(2)}) copy-start(bf16[40,2176]{1,0:T(8,128)(2,1)} %get-tuple-element.26) | copy-start | bytes 522244
  9.4 9.6 %collective-permute-start.5 = (bf16[40,2048]{1,0:T(8,128)(2,1)}, bf16[40,2048]{1,0:T(8,128)(2,1)S(1)}, u32[]{:S(2)}, u32[]{:S(2)}) collective-permute-start(bf16[40,2048]{1,0:T(8,128)(2,1)} %get-tuple-element.27), channel_id=1, source_target_pairs={{20,0},{28,8},{21,1},{29,9},{22,2},{30,10},{23,3},{31,11},{0,16},{... | collective-permute-start | bytes 491528 | tf_op jit(solution)/shard_map/ppermute | solution.py:56
  11.6 9.9 %collective-permute-start.4 = (bf16[40,2048]{1,0:T(8,128)(2,1)}, bf16[40,2048]{1,0:T(8,128)(2,1)S(1)}, u32[]{:S(2)}, u32[]{:S(2)}) collective-permute-start(bf16[40,2048]{1,0:T(8,128)(2,1)} %get-tuple-element.27), channel_id=1, source_target_pairs={{4,0},{12,8},{5,1},{13,9},{6,2},{14,10},{7,3},{15,11},{20,16},{28,... | collective-permute-start | bytes 491528 | tf_op jit(solution)/shard_map/ppermute | solution.py:56
  14.2 7.3 %collective-permute-start.3 = (bf16[40,2048]{1,0:T(8,128)(2,1)}, bf16[40,2048]{1,0:T(8,128)(2,1)S(1)}, u32[]{:S(2)}, u32[]{:S(2)}) collective-permute-start(bf16[40,2048]{1,0:T(8,128)(2,1)} %get-tuple-element.27), channel_id=1, source_target_pairs={{16,0},{24,8},{17,1},{25,9},{18,2},{26,10},{19,3},{27,11},{4,16},{... | collective-permute-start | bytes 491528 | tf_op jit(solution)/shard_map/ppermute | solution.py:56
  15.3 7.2 %collective-permute-start.2 = (bf16[40,2176]{1,0:T(8,128)(2,1)}, bf16[40,2176]{1,0:T(8,128)(2,1)S(1)}, u32[]{:S(2)}, u32[]{:S(2)}) collective-permute-start(bf16[40,2176]{1,0:T(8,128)(2,1)} %get-tuple-element.26), channel_id=1, source_target_pairs={{3,0},{11,8},{0,1},{8,9},{1,2},{9,10},{2,3},{10,11},{19,16},{27,24... | collective-permute-start | bytes 522248 | tf_op jit(solution)/shard_map/ppermute | solution.py:50
  16.5 9.0 %collective-permute-start.1 = (bf16[40,2176]{1,0:T(8,128)(2,1)}, bf16[40,2176]{1,0:T(8,128)(2,1)S(1)}, u32[]{:S(2)}, u32[]{:S(2)}) collective-permute-start(bf16[40,2176]{1,0:T(8,128)(2,1)} %get-tuple-element.26), channel_id=1, source_target_pairs={{2,0},{10,8},{3,1},{11,9},{0,2},{8,10},{1,3},{9,11},{18,16},{26,24... | collective-permute-start | bytes 522248 | tf_op jit(solution)/shard_map/ppermute | solution.py:50
  18.9 6.6 %collective-permute-start = (bf16[40,2176]{1,0:T(8,128)(2,1)}, bf16[40,2176]{1,0:T(8,128)(2,1)S(1)}, u32[]{:S(2)}, u32[]{:S(2)}) collective-permute-start(bf16[40,2176]{1,0:T(8,128)(2,1)} %get-tuple-element.26), channel_id=1, source_target_pairs={{1,0},{9,8},{2,1},{10,9},{3,2},{11,10},{0,3},{8,11},{17,16},{25,24... | collective-permute-start | bytes 522248 | tf_op jit(solution)/shard_map/ppermute | solution.py:50
  22.5 22.5 %copy-start.2 = (bf16[160,2048]{1,0:T(8,128)(2,1)}, bf16[160,2048]{1,0:T(8,128)(2,1)S(1)}, u32[]{:S(2)}) copy-start(bf16[160,2048]{1,0:T(8,128)(2,1)S(1)} %pad_maximum_fusion.1.refs_6_) | copy-start | bytes 1966084
  25.6 24.4 %copy-start.1 = (bf16[160,2176]{1,0:T(8,128)(2,1)}, bf16[160,2176]{1,0:T(8,128)(2,1)S(1)}, u32[]{:S(2)}) copy-start(bf16[160,2176]{1,0:T(8,128)(2,1)S(1)} %pad_maximum_fusion.refs_1_) | copy-start | bytes 2088964
  25.6 15.7 %collective-permute-start.8 = (bf16[160,2176]{1,0:T(8,128)(2,1)S(1)}, bf16[160,2176]{1,0:T(8,128)(2,1)S(1)}, u32[]{:S(2)}, u32[]{:S(2)}) collective-permute-start(bf16[160,2176]{1,0:T(8,128)(2,1)S(1)} %pad_maximum_fusion.refs_1_), channel_id=1, source_target_pairs={{20,0},{28,8},{21,1},{29,9},{22,2},{30,10},{23,3},{31,11},{0,16},{... | collective-permute-start | bytes 2088968 | tf_op jit(solution)/shard_map/ppermute | solution.py:56
  26.1 15.3 %collective-permute-start.6 = (bf16[160,2176]{1,0:T(8,128)(2,1)S(1)}, bf16[160,2176]{1,0:T(8,128)(2,1)S(1)}, u32[]{:S(2)}, u32[]{:S(2)}) collective-permute-start(bf16[160,2176]{1,0:T(8,128)(2,1)S(1)} %pad_maximum_fusion.refs_1_), channel_id=1, source_target_pairs={{16,0},{24,8},{17,1},{25,9},{18,2},{26,10},{19,3},{27,11},{4,16},{... | collective-permute-start | bytes 2088968 | tf_op jit(solution)/shard_map/ppermute | solution.py:56
  28.3 15.8 %collective-permute-start.12 = (bf16[160,2048]{1,0:T(8,128)(2,1)S(1)}, bf16[160,2048]{1,0:T(8,128)(2,1)S(1)}, u32[]{:S(2)}, u32[]{:S(2)}) collective-permute-start(bf16[160,2048]{1,0:T(8,128)(2,1)S(1)} %pad_maximum_fusion.1.refs_6_), channel_id=1, source_target_pairs={{3,0},{11,8},{0,1},{8,9},{1,2},{9,10},{2,3},{10,11},{19,16},{27,24... | collective-permute-start | bytes 1966088 | tf_op jit(solution)/shard_map/ppermute | solution.py:50
  30.9 18.2 %collective-permute-start.10 = (bf16[160,2048]{1,0:T(8,128)(2,1)S(1)}, bf16[160,2048]{1,0:T(8,128)(2,1)S(1)}, u32[]{:S(2)}, u32[]{:S(2)}) collective-permute-start(bf16[160,2048]{1,0:T(8,128)(2,1)S(1)} %pad_maximum_fusion.1.refs_6_), channel_id=1, source_target_pairs={{1,0},{9,8},{2,1},{10,9},{3,2},{11,10},{0,3},{8,11},{17,16},{25,24... | collective-permute-start | bytes 1966088 | tf_op jit(solution)/shard_map/ppermute | solution.py:50
  41.2 8.1 %copy-start.3 = (bf16[160,2176]{1,0:T(8,128)(2,1)}, bf16[160,2176]{1,0:T(8,128)(2,1)S(1)}, u32[]{:S(2)}) copy-start(bf16[160,2176]{1,0:T(8,128)(2,1)S(1)} %collective-permute-done.8.refs_5_) | copy-start | bytes 2088964
  41.3 14.3 %collective-permute-start.9 = (bf16[80,2176]{1,0:T(8,128)(2,1)S(1)}, bf16[80,2176]{1,0:T(8,128)(2,1)S(1)}, u32[]{:S(2)}, u32[]{:S(2)}) collective-permute-start(bf16[80,2176]{1,0:T(8,128)(2,1)S(1)} %slice.17), channel_id=1, source_target_pairs={{20,0},{28,8},{21,1},{29,9},{22,2},{30,10},{23,3},{31,11},{0,16},{... | collective-permute-start | bytes 1044488 | tf_op jit(solution)/shard_map/ppermute | solution.py:56
  41.4 8.0 %copy-start.4 = (bf16[160,2176]{1,0:T(8,128)(2,1)}, bf16[160,2176]{1,0:T(8,128)(2,1)S(1)}, u32[]{:S(2)}) copy-start(bf16[160,2176]{1,0:T(8,128)(2,1)S(1)} %collective-permute-done.6.refs_2_) | copy-start | bytes 2088964
  41.4 14.2 %collective-permute-start.7 = (bf16[80,2176]{1,0:T(8,128)(2,1)S(1)}, bf16[80,2176]{1,0:T(8,128)(2,1)S(1)}, u32[]{:S(2)}, u32[]{:S(2)}) collective-permute-start(bf16[80,2176]{1,0:T(8,128)(2,1)S(1)} %slice.16), channel_id=1, source_target_pairs={{16,0},{24,8},{17,1},{25,9},{18,2},{26,10},{19,3},{27,11},{4,16},{... | collective-permute-start | bytes 1044488 | tf_op jit(solution)/shard_map/ppermute | solution.py:56
  44.1 5.3 %copy-start.6 = (bf16[160,2048]{1,0:T(8,128)(2,1)}, bf16[160,2048]{1,0:T(8,128)(2,1)S(1)}, u32[]{:S(2)}) copy-start(bf16[160,2048]{1,0:T(8,128)(2,1)S(1)} %collective-permute-done.12.refs_10_) | copy-start | bytes 1966084
  45.0 8.7 %collective-permute-start.13 = (bf16[80,2048]{1,0:T(8,128)(2,1)}, bf16[80,2048]{1,0:T(8,128)(2,1)S(1)}, u32[]{:S(2)}, u32[]{:S(2)}) collective-permute-start(bf16[80,2048]{1,0:T(8,128)(2,1)} %slice.19), channel_id=1, source_target_pairs={{3,0},{11,8},{0,1},{8,9},{1,2},{9,10},{2,3},{10,11},{19,16},{27,24... | collective-permute-start | bytes 983048 | tf_op jit(solution)/shard_map/ppermute | solution.py:50
  49.1 0.9 copy-start.7
  49.1 6.5 %collective-permute-start.11 = (bf16[80,2048]{1,0:T(8,128)(2,1)S(1)}, bf16[80,2048]{1,0:T(8,128)(2,1)S(1)}, u32[]{:S(2)}, u32[]{:S(2)}) collective-permute-start(bf16[80,2048]{1,0:T(8,128)(2,1)S(1)} %slice.18), channel_id=1, source_target_pairs={{1,0},{9,8},{2,1},{10,9},{3,2},{11,10},{0,3},{8,11},{17,16},{25,24... | collective-permute-start | bytes 983048 | tf_op jit(solution)/shard_map/ppermute | solution.py:50
  68.0 39.1 %copy-start = (f32[640,640]{1,0:T(8,128)S(1)}, f32[640,640]{1,0:T(8,128)}, u32[]{:S(2)}) copy-start(f32[640,640]{1,0:T(8,128)} %get-tuple-element.38.refs_6_) | copy-start | bytes 4915204
  68.0 2.5 %collective-permute-start.14 = (f32[32,352]{1,0:T(8,128)S(1)}, f32[32,352]{1,0:T(8,128)S(1)}, u32[]{:S(2)}, u32[]{:S(2)}) collective-permute-start(f32[32,352]{1,0:T(8,128)S(1)} %get-tuple-element.31), channel_id=1, source_target_pairs={{8,0},{0,8},{9,1},{1,9},{10,2},{2,10},{11,3},{3,11},{24,16},{16,24... | collective-permute-start | bytes 135176 | tf_op jit(solution)/shard_map/ppermute | solution.py:62
  71.3 22.9 %all-to-all-start = ((f32[8,88,128]{2,1,0:T(8,128)}), f32[8,88,128]{2,1,0:T(8,128)S(1)}, u32[]{:S(2)}, u32[]{:S(2)}) async-start(f32[8,88,128]{2,1,0:T(8,128)} %get-tuple-element.32), calls=%async_computation | async-start | bytes 720896 | tf_op jit(solution)/shard_map/all_to_all | solution.py:68
  94.6 1.4 collective-permute-start.15
Sparse Core Ops, SparseCore 0:
  9.8 48.1 all-gather.1

commit v8 on v7

--- a/solution.py
+++ b/solution.py
@@ -29,7 +29,7 @@
     (z, y, x, c) for z in range(NZ) for y in range(NY) for x in range(NX) for c in range(NC)
 ]
 LINES = [
-    [device(z, y, x, c) for z in range(NZ)]
+    [device(z + 2 * c, y, x, c) for z in (0, 4, 1, 5, 2, 6, 3, 7)]
     for y in range(NY)
     for x in range(NX)
     for c in range(NC)

time: 144 us -> 143 us (level)
  waiting for transfers between devices: 38.7 us -> 35.8 us
  blocking collectives: 33.4 us -> 34.9 us
    all_to_all x1, waiting for transfers between devices: 14.4 us -> 11.3 us  [exchange(): lax.all_to_all(chunks, AXES, 0, 0, axis_index_groups=groups, tiled=True)]
where the time goes in v8:
time: 143 us; the launch traced here: 142 us
  waiting for transfers between devices  35.8 us (25%)
  blocking collectives  34.9 us (24%)
  starting transfers between devices  34.7 us (24%)
  Pallas kernels  20.1 us (14%)
  between operations  14.2 us (10%)
  local copies, waits for them, and re-layouts  1.56 us (1%)
    all_to_all x3, blocking collectives, exchange(): lax.all_to_all(chunks, AXES, 0, 0, axis_index_groups=groups, tiled=True)  34.9 us
    ppermute x7, starting transfers between devices, from_x(): lax.ppermute(value, AXES, [(device(z, y, x + k, c), device(z, y, x, c)) f...  12 us
    ppermute x7, waiting for transfers between devices, from_y(): lax.ppermute(value, AXES, [(device(z, y + k, x, c), device(z, y, x, c)) f...  11.5 us
    ppermute x7, starting transfers between devices, from_y(): lax.ppermute(value, AXES, [(device(z, y + k, x, c), device(z, y, x, c)) f...  11.4 us
    all_to_all x1, waiting for transfers between devices, exchange(): lax.all_to_all(chunks, AXES, 0, 0, axis_index_groups=groups, tiled=True)  11.3 us
    pallas_call x7, Pallas kernels, small_kernel(): pl.pallas_call(body, out_shape=out, in_specs=specs or [VM] * len(args), o...  10.1 us
    pallas_call x1, Pallas kernels, local(): pl.pallas_call(functools.partial(tile_kernel, *sizes), out_shape=(shape(p...  9.98 us
    all_to_all x1, starting transfers between devices, exchange(): lax.all_to_all(chunks, AXES, 0, 0, axis_index_groups=groups, tiled=True)  9.59 us
  transfers between devices with their start and end apart: 18, of which 9 were waited for; matrix products, arithmetic and copies ran while one was open for 1% of the time, Pallas kernels for 0%

profile of v8, /device:TPU:1, one launch (start us, length us, event | category | flops | bytes accessed | tf_op | source)
XLA Modules:
  0.0 142.4 jit_solution(864277296039963949)
XLA Ops:
  7.2 0.0 all-gather.2.cloned.1.call-start
  7.2 2.1 %prepare.1 = (bf16[40,4224]{1,0:T(8,128)(2,1)}, bf16[40,2176]{1,0:T(8,128)(2,1)}, bf16[40,2048]{1,0:T(8,128)(2,1)}) custom-call(f32[40,4096]{1,0:T(8,128)} %s_hbm.1, f32[32,40]{1,0:T(8,128)} %bitcast.7), custom_call_target="tpu_custom_call" | custom-call | tf_op jit(solution)/shard_map/prepare/pallas_call | solution.py:86
  9.4 0.0 copy-start.5
  9.4 0.0 all-gather.2.cloned.1.call-update
  9.4 2.2 %collective-permute-start.5 = (bf16[40,2048]{1,0:T(8,128)(2,1)}, bf16[40,2048]{1,0:T(8,128)(2,1)S(1)}, u32[]{:S(2)}, u32[]{:S(2)}) collective-permute-start(bf16[40,2048]{1,0:T(8,128)(2,1)} %get-tuple-element.27), channel_id=1, source_target_pairs={{20,0},{28,8},{21,1},{29,9},{22,2},{30,10},{23,3},{31,11},{0,16},{... | collective-permute-start | bytes 491528 | tf_op jit(solution)/shard_map/ppermute | solution.py:56
  11.6 2.6 %collective-permute-start.4 = (bf16[40,2048]{1,0:T(8,128)(2,1)}, bf16[40,2048]{1,0:T(8,128)(2,1)S(1)}, u32[]{:S(2)}, u32[]{:S(2)}) collective-permute-start(bf16[40,2048]{1,0:T(8,128)(2,1)} %get-tuple-element.27), channel_id=1, source_target_pairs={{4,0},{12,8},{5,1},{13,9},{6,2},{14,10},{7,3},{15,11},{20,16},{28,... | collective-permute-start | bytes 491528 | tf_op jit(solution)/shard_map/ppermute | solution.py:56
  14.2 1.1 collective-permute-start.3
  15.3 1.2 collective-permute-start.2
  16.5 2.5 %collective-permute-start.1 = (bf16[40,2176]{1,0:T(8,128)(2,1)}, bf16[40,2176]{1,0:T(8,128)(2,1)S(1)}, u32[]{:S(2)}, u32[]{:S(2)}) collective-permute-start(bf16[40,2176]{1,0:T(8,128)(2,1)} %get-tuple-element.26), channel_id=1, source_target_pairs={{2,0},{10,8},{3,1},{11,9},{0,2},{8,10},{1,3},{9,11},{18,16},{26,24... | collective-permute-start | bytes 522248 | tf_op jit(solution)/shard_map/ppermute | solution.py:50
  18.9 0.0 collective-permute-done.5
  18.9 1.2 collective-permute-start
  20.1 1.4 %collective-permute-done.4 = bf16[40,2048]{1,0:T(8,128)(2,1)S(1)} collective-permute-done((bf16[40,2048]{1,0:T(8,128)(2,1)}, bf16[40,2048]{1,0:T(8,128)(2,1)S(1)}, u32[]{:S(2)}, u32[]{:S(2)}) %collective-permute-start.4) | collective-permute-done | bytes 163872 | tf_op jit(solution)/shard_map/ppermute | solution.py:56
  21.5 0.0 collective-permute-done.3
  21.5 1.0 pad_maximum_fusion.1.refs_6_
  22.5 0.0 copy-start.2
  22.5 0.0 collective-permute-done.2
  22.5 3.0 %collective-permute-done.1 = bf16[40,2176]{1,0:T(8,128)(2,1)S(1)} collective-permute-done((bf16[40,2176]{1,0:T(8,128)(2,1)}, bf16[40,2176]{1,0:T(8,128)(2,1)S(1)}, u32[]{:S(2)}, u32[]{:S(2)}) %collective-permute-start.1) | collective-permute-done | bytes 174112 | tf_op jit(solution)/shard_map/ppermute | solution.py:50
  25.5 0.0 collective-permute-done
  25.5 0.0 copy-done.5
  25.5 0.1 pad_maximum_fusion.refs_1_
  25.6 0.0 copy-start.1
  25.6 0.5 collective-permute-start.8
  26.1 2.3 %collective-permute-start.6 = (bf16[160,2176]{1,0:T(8,128)(2,1)S(1)}, bf16[160,2176]{1,0:T(8,128)(2,1)S(1)}, u32[]{:S(2)}, u32[]{:S(2)}) collective-permute-start(bf16[160,2176]{1,0:T(8,128)(2,1)S(1)} %pad_maximum_fusion.refs_1_), channel_id=1, source_target_pairs={{16,0},{24,8},{17,1},{25,9},{18,2},{26,10},{19,3},{27,11},{4,16},{... | collective-permute-start | bytes 2088968 | tf_op jit(solution)/shard_map/ppermute | solution.py:56
  28.3 2.6 %collective-permute-start.12 = (bf16[160,2048]{1,0:T(8,128)(2,1)S(1)}, bf16[160,2048]{1,0:T(8,128)(2,1)S(1)}, u32[]{:S(2)}, u32[]{:S(2)}) collective-permute-start(bf16[160,2048]{1,0:T(8,128)(2,1)S(1)} %pad_maximum_fusion.1.refs_6_), channel_id=1, source_target_pairs={{3,0},{11,8},{0,1},{8,9},{1,2},{9,10},{2,3},{10,11},{19,16},{27,24... | collective-permute-start | bytes 1966088 | tf_op jit(solution)/shard_map/ppermute | solution.py:50
  30.9 0.3 collective-permute-start.10
  31.2 10.1 %collective-permute-done.8.refs_5_ = bf16[160,2176]{1,0:T(8,128)(2,1)S(1)} collective-permute-done((bf16[160,2176]{1,0:T(8,128)(2,1)S(1)}, bf16[160,2176]{1,0:T(8,128)(2,1)S(1)}, u32[]{:S(2)}, u32[]{:S(2)}) %collective-permute-start.8) | collective-permute-done | bytes 696352 | tf_op jit(solution)/shard_map/ppermute | solution.py:56
  41.3 0.1 collective-permute-start.9
  41.4 0.0 collective-permute-done.6.refs_2_
  41.4 0.0 copy-start.4
  41.4 2.7 %collective-permute-start.7 = (bf16[80,2176]{1,0:T(8,128)(2,1)S(1)}, bf16[80,2176]{1,0:T(8,128)(2,1)S(1)}, u32[]{:S(2)}, u32[]{:S(2)}) collective-permute-start(bf16[80,2176]{1,0:T(8,128)(2,1)S(1)} %slice.16), channel_id=1, source_target_pairs={{16,0},{24,8},{17,1},{25,9},{18,2},{26,10},{19,3},{27,11},{4,16},{... | collective-permute-start | bytes 1044488 | tf_op jit(solution)/shard_map/ppermute | solution.py:56
  44.1 0.0 collective-permute-done.12.refs_10_
  44.2 0.8 slice.19
  45.0 0.0 copy-done.2
  45.0 4.1 %collective-permute-start.13 = (bf16[80,2048]{1,0:T(8,128)(2,1)}, bf16[80,2048]{1,0:T(8,128)(2,1)S(1)}, u32[]{:S(2)}, u32[]{:S(2)}) collective-permute-start(bf16[80,2048]{1,0:T(8,128)(2,1)} %slice.19), channel_id=1, source_target_pairs={{3,0},{11,8},{0,1},{8,9},{1,2},{9,10},{2,3},{10,11},{19,16},{27,24... | collective-permute-start | bytes 983048 | tf_op jit(solution)/shard_map/ppermute | solution.py:50
  49.1 0.0 collective-permute-done.10.refs_7_
  49.1 0.3 collective-permute-start.11
  49.4 0.0 copy-done.3
  49.4 0.0 copy-done.4
  49.4 0.0 copy-done.6
  49.4 0.5 copy-done.7
  49.9 0.1 pad_add_fusion.at_ref
  50.0 3.7 %collective-permute-done.13.refs_9_ = bf16[80,2048]{1,0:T(8,128)(2,1)S(1)} collective-permute-done((bf16[80,2048]{1,0:T(8,128)(2,1)}, bf16[80,2048]{1,0:T(8,128)(2,1)S(1)}, u32[]{:S(2)}, u32[]{:S(2)}) %collective-permute-start.13) | collective-permute-done | bytes 327712 | tf_op jit(solution)/shard_map/ppermute | solution.py:50
  53.7 1.9 %collective-permute-done.11.refs_8_ = bf16[80,2048]{1,0:T(8,128)(2,1)S(1)} collective-permute-done((bf16[80,2048]{1,0:T(8,128)(2,1)S(1)}, bf16[80,2048]{1,0:T(8,128)(2,1)S(1)}, u32[]{:S(2)}, u32[]{:S(2)}) %collective-permute-start.11) | collective-permute-done | bytes 327712 | tf_op jit(solution)/shard_map/ppermute | solution.py:50
  55.6 0.0 collective-permute-done.9.refs_4_
  55.6 0.0 collective-permute-done.7.refs_3_
  55.6 2.4 %all-gather.2.cloned.1.call-done.refs_0_ = bf16[640,4224]{1,0:T(8,128)(2,1)} async-done(((bf16[40,4224]{1,0:T(8,128)(2,1)}), bf16[640,4224]{1,0:T(8,128)(2,1)}) %all-gather.2.cloned.1.call-update) | async-done | bytes 5406736 | tf_op jit(solution)/shard_map/all_gather | solution.py:367
  58.0 10.0 %tile.1 = (f32[640,640]{1,0:T(8,128)}, f32[64,352]{1,0:T(8,128)S(1)}, f32[32,352]{1,0:T(8,128)S(1)}, f32[32,640]{1,0:T(8,128)S(1)}, f32[32,640]{1,0:T(8,128)S(1)}, /*index=5*/f32[32,32]{1,0:T(8,128)}) custom-call(s32[4]{0:T(128)S(1)} %pad_add_fusion.at_ref, bf16[640,4224]{1,0:T(8,128)(2,1)} %all-gather.2.cloned.1.call-done.refs_0_, ...), custom_call_target="tpu_custom_call" | custom-call | flops 6710886400 | bytes 10485760 | tf_op jit(solution)/shard_map/tile/pallas_call | solution.py:376
  68.0 1.6 %collective-permute-start.14 = (f32[32,352]{1,0:T(8,128)S(1)}, f32[32,352]{1,0:T(8,128)S(1)}, u32[]{:S(2)}, u32[]{:S(2)}) collective-permute-start(f32[32,352]{1,0:T(8,128)S(1)} %get-tuple-element.31), channel_id=1, source_target_pairs={{8,0},{0,8},{9,1},{1,9},{10,2},{2,10},{11,3},{3,11},{24,16},{16,24... | collective-permute-start | bytes 135176 | tf_op jit(solution)/shard_map/ppermute | solution.py:62
  69.6 0.9 collective-permute-done.14.far_ref
  70.5 0.8 share.1
  71.3 9.6 %all-to-all-start = ((f32[8,88,128]{2,1,0:T(8,128)}), f32[8,88,128]{2,1,0:T(8,128)S(1)}, u32[]{:S(2)}, u32[]{:S(2)}) async-start(f32[8,88,128]{2,1,0:T(8,128)} %get-tuple-element.32), calls=%async_computation | async-start | bytes 720896 | tf_op jit(solution)/shard_map/all_to_all | solution.py:68
  80.9 11.3 %all-to-all-done.part_ref = f32[8,88,128]{2,1,0:T(8,128)S(1)} async-done(((f32[8,88,128]{2,1,0:T(8,128)}), f32[8,88,128]{2,1,0:T(8,128)S(1)}, u32[]{:S(2)}, u32[]{:S(2)}) %all-to-all-start) | async-done | bytes 360480 | tf_op jit(solution)/shard_map/all_to_all | solution.py:68
  92.2 0.4 line.1
  92.6 0.0 collective-permute-start.15
  92.6 0.1 constant_dynamic-slice_fusion.own_ref
  92.7 1.1 collective-permute-done.15.far_ref.refs_3_
  93.8 0.1 spread.1
  93.9 11.1 %all_to_all.20.refs_0_ = f32[16,32,104]{2,1,0:T(8,128)S(1)} all-to-all(f32[16,32,104]{2,1,0:T(8,128)S(1)} %spread.1), channel_id=1, replica_groups={{0,1,2,3,16,17,18,19,4,5,6,7,20,21,22,23},{8,9,10,11,24,25,26,27,12,13,..., dimensions={0} | all-to-all | bytes 425984 | tf_op jit(solution)/shard_map/all_to_all | solution.py:68
  105.1 0.0 copy-done
  105.1 4.8 %step.1 = (f32[16,32,72]{2,1,0:T(8,128)S(1)}, f32[32,40]{1,0:T(8,128)S(1)}, f32[32,40]{1,0:T(8,128)S(1)}, f32[32,40]{1,0:T(8,128)S(1)}, f32[32,32]{1,0:T(8,128)S(1)}) custom-call(s32[4]{0:T(128)S(1)} %pad_add_fusion.at_ref, f32[16,32,104]{2,1,0:T(8,128)S(1)} %all_to_all.20.refs_0_, f32[32,32]{1,0:T(8,128)S(1)} %get-tuple-element.35.refs_1_, ...), custom_call_target="tpu_custom_call" | custom-call | tf_op jit(solution)/shard_map/step/pallas_call | solution.py:86
  109.9 10.2 %all_to_all.21.got_ref = f32[16,32,72]{2,1,0:T(8,128)S(1)} all-to-all(f32[16,32,72]{2,1,0:T(8,128)S(1)} %get-tuple-element.39), channel_id=1, replica_groups={{0,1,2,3,16,17,18,19,4,5,6,7,20,21,22,23},{8,9,10,11,24,25,26,27,12,13,..., dimensions={0} | all-to-all | bytes 294912 | tf_op jit(solution)/shard_map/all_to_all | solution.py:68
  120.1 0.1 image.1
  120.2 13.6 %all_to_all.22.got_ref = f32[16,8,128]{2,1,0:T(8,128)S(1)} all-to-all(f32[16,8,128]{2,1,0:T(8,128)S(1)} %get-tuple-element.41), channel_id=1, replica_groups={{0,32,64,96,128,160,192,224,8,40,72,104,136,168,200,232},{1,33,65,97,12..., dimensions={0} | all-to-all | bytes 131072 | tf_op jit(solution)/shard_map/all_to_all | solution.py:68
  133.7 1.8 %last.1 = (f32[32,40]{1,0:T(8,128)}, f32[32,40]{1,0:T(8,128)}) custom-call(f32[16,8,128]{2,1,0:T(8,128)S(1)} %all_to_all.22.got_ref, f32[32,32]{1,0:T(8,128)S(1)} %get-tuple-element.42.rr, f32[32,40]{1,0:T(8,128)S(1)} %get-tuple-element.40.d_ref.d_own, f32[32,40]{1,0:T(8,128)S(1)} %get-tuple-element.43.image, f32[32,40]{1,0:T(8,128)S(1)} %get-tuple-element.44.weights, ...), custom_call_target="tpu_custom_call" | custom-call | tf_op jit(solution)/shard_map/last/pallas_call | solution.py:86
  (8 shorter events, 0.1 us)
Async XLA Ops:
  7.2 50.9 %all-gather.2.cloned.1.call-start = ((), (), s32[]{:S(2)}) async-start(), calls=%async_computation.4 | async-start | bytes 5744640 | tf_op jit(solution)/shard_map/all_gather | solution.py:367
  9.4 16.2 %copy-start.5 = (bf16[40,2176]{1,0:T(8,128)(2,1)S(1)}, bf16[40,2176]{1,0:T(8,128)(2,1)}, u32[]{:S(2)}) copy-start(bf16[40,2176]{1,0:T(8,128)(2,1)} %get-tuple-element.26) | copy-start | bytes 522244
  9.4 9.6 %collective-permute-start.5 = (bf16[40,2048]{1,0:T(8,128)(2,1)}, bf16[40,2048]{1,0:T(8,128)(2,1)S(1)}, u32[]{:S(2)}, u32[]{:S(2)}) collective-permute-start(bf16[40,2048]{1,0:T(8,128)(2,1)} %get-tuple-element.27), channel_id=1, source_target_pairs={{20,0},{28,8},{21,1},{29,9},{22,2},{30,10},{23,3},{31,11},{0,16},{... | collective-permute-start | bytes 491528 | tf_op jit(solution)/shard_map/ppermute | solution.py:56
  11.6 9.9 %collective-permute-start.4 = (bf16[40,2048]{1,0:T(8,128)(2,1)}, bf16[40,2048]{1,0:T(8,128)(2,1)S(1)}, u32[]{:S(2)}, u32[]{:S(2)}) collective-permute-start(bf16[40,2048]{1,0:T(8,128)(2,1)} %get-tuple-element.27), channel_id=1, source_target_pairs={{4,0},{12,8},{5,1},{13,9},{6,2},{14,10},{7,3},{15,11},{20,16},{28,... | collective-permute-start | bytes 491528 | tf_op jit(solution)/shard_map/ppermute | solution.py:56
  14.2 7.3 %collective-permute-start.3 = (bf16[40,2048]{1,0:T(8,128)(2,1)}, bf16[40,2048]{1,0:T(8,128)(2,1)S(1)}, u32[]{:S(2)}, u32[]{:S(2)}) collective-permute-start(bf16[40,2048]{1,0:T(8,128)(2,1)} %get-tuple-element.27), channel_id=1, source_target_pairs={{16,0},{24,8},{17,1},{25,9},{18,2},{26,10},{19,3},{27,11},{4,16},{... | collective-permute-start | bytes 491528 | tf_op jit(solution)/shard_map/ppermute | solution.py:56
  15.3 7.2 %collective-permute-start.2 = (bf16[40,2176]{1,0:T(8,128)(2,1)}, bf16[40,2176]{1,0:T(8,128)(2,1)S(1)}, u32[]{:S(2)}, u32[]{:S(2)}) collective-permute-start(bf16[40,2176]{1,0:T(8,128)(2,1)} %get-tuple-element.26), channel_id=1, source_target_pairs={{3,0},{11,8},{0,1},{8,9},{1,2},{9,10},{2,3},{10,11},{19,16},{27,24... | collective-permute-start | bytes 522248 | tf_op jit(solution)/shard_map/ppermute | solution.py:50
  16.5 9.0 %collective-permute-start.1 = (bf16[40,2176]{1,0:T(8,128)(2,1)}, bf16[40,2176]{1,0:T(8,128)(2,1)S(1)}, u32[]{:S(2)}, u32[]{:S(2)}) collective-permute-start(bf16[40,2176]{1,0:T(8,128)(2,1)} %get-tuple-element.26), channel_id=1, source_target_pairs={{2,0},{10,8},{3,1},{11,9},{0,2},{8,10},{1,3},{9,11},{18,16},{26,24... | collective-permute-start | bytes 522248 | tf_op jit(solution)/shard_map/ppermute | solution.py:50
  18.9 6.6 %collective-permute-start = (bf16[40,2176]{1,0:T(8,128)(2,1)}, bf16[40,2176]{1,0:T(8,128)(2,1)S(1)}, u32[]{:S(2)}, u32[]{:S(2)}) collective-permute-start(bf16[40,2176]{1,0:T(8,128)(2,1)} %get-tuple-element.26), channel_id=1, source_target_pairs={{1,0},{9,8},{2,1},{10,9},{3,2},{11,10},{0,3},{8,11},{17,16},{25,24... | collective-permute-start | bytes 522248 | tf_op jit(solution)/shard_map/ppermute | solution.py:50
  22.5 22.5 %copy-start.2 = (bf16[160,2048]{1,0:T(8,128)(2,1)}, bf16[160,2048]{1,0:T(8,128)(2,1)S(1)}, u32[]{:S(2)}) copy-start(bf16[160,2048]{1,0:T(8,128)(2,1)S(1)} %pad_maximum_fusion.1.refs_6_) | copy-start | bytes 1966084
  25.6 24.4 %copy-start.1 = (bf16[160,2176]{1,0:T(8,128)(2,1)}, bf16[160,2176]{1,0:T(8,128)(2,1)S(1)}, u32[]{:S(2)}) copy-start(bf16[160,2176]{1,0:T(8,128)(2,1)S(1)} %pad_maximum_fusion.refs_1_) | copy-start | bytes 2088964
  25.6 15.7 %collective-permute-start.8 = (bf16[160,2176]{1,0:T(8,128)(2,1)S(1)}, bf16[160,2176]{1,0:T(8,128)(2,1)S(1)}, u32[]{:S(2)}, u32[]{:S(2)}) collective-permute-start(bf16[160,2176]{1,0:T(8,128)(2,1)S(1)} %pad_maximum_fusion.refs_1_), channel_id=1, source_target_pairs={{20,0},{28,8},{21,1},{29,9},{22,2},{30,10},{23,3},{31,11},{0,16},{... | collective-permute-start | bytes 2088968 | tf_op jit(solution)/shard_map/ppermute | solution.py:56
  26.1 15.3 %collective-permute-start.6 = (bf16[160,2176]{1,0:T(8,128)(2,1)S(1)}, bf16[160,2176]{1,0:T(8,128)(2,1)S(1)}, u32[]{:S(2)}, u32[]{:S(2)}) collective-permute-start(bf16[160,2176]{1,0:T(8,128)(2,1)S(1)} %pad_maximum_fusion.refs_1_), channel_id=1, source_target_pairs={{16,0},{24,8},{17,1},{25,9},{18,2},{26,10},{19,3},{27,11},{4,16},{... | collective-permute-start | bytes 2088968 | tf_op jit(solution)/shard_map/ppermute | solution.py:56
  28.3 15.8 %collective-permute-start.12 = (bf16[160,2048]{1,0:T(8,128)(2,1)S(1)}, bf16[160,2048]{1,0:T(8,128)(2,1)S(1)}, u32[]{:S(2)}, u32[]{:S(2)}) collective-permute-start(bf16[160,2048]{1,0:T(8,128)(2,1)S(1)} %pad_maximum_fusion.1.refs_6_), channel_id=1, source_target_pairs={{3,0},{11,8},{0,1},{8,9},{1,2},{9,10},{2,3},{10,11},{19,16},{27,24... | collective-permute-start | bytes 1966088 | tf_op jit(solution)/shard_map/ppermute | solution.py:50
  30.9 18.2 %collective-permute-start.10 = (bf16[160,2048]{1,0:T(8,128)(2,1)S(1)}, bf16[160,2048]{1,0:T(8,128)(2,1)S(1)}, u32[]{:S(2)}, u32[]{:S(2)}) collective-permute-start(bf16[160,2048]{1,0:T(8,128)(2,1)S(1)} %pad_maximum_fusion.1.refs_6_), channel_id=1, source_target_pairs={{1,0},{9,8},{2,1},{10,9},{3,2},{11,10},{0,3},{8,11},{17,16},{25,24... | collective-permute-start | bytes 1966088 | tf_op jit(solution)/shard_map/ppermute | solution.py:50
  41.2 8.1 %copy-start.3 = (bf16[160,2176]{1,0:T(8,128)(2,1)}, bf16[160,2176]{1,0:T(8,128)(2,1)S(1)}, u32[]{:S(2)}) copy-start(bf16[160,2176]{1,0:T(8,128)(2,1)S(1)} %collective-permute-done.8.refs_5_) | copy-start | bytes 2088964
  41.3 14.3 %collective-permute-start.9 = (bf16[80,2176]{1,0:T(8,128)(2,1)S(1)}, bf16[80,2176]{1,0:T(8,128)(2,1)S(1)}, u32[]{:S(2)}, u32[]{:S(2)}) collective-permute-start(bf16[80,2176]{1,0:T(8,128)(2,1)S(1)} %slice.17), channel_id=1, source_target_pairs={{20,0},{28,8},{21,1},{29,9},{22,2},{30,10},{23,3},{31,11},{0,16},{... | collective-permute-start | bytes 1044488 | tf_op jit(solution)/shard_map/ppermute | solution.py:56
  41.4 8.0 %copy-start.4 = (bf16[160,2176]{1,0:T(8,128)(2,1)}, bf16[160,2176]{1,0:T(8,128)(2,1)S(1)}, u32[]{:S(2)}) copy-start(bf16[160,2176]{1,0:T(8,128)(2,1)S(1)} %collective-permute-done.6.refs_2_) | copy-start | bytes 2088964
  41.4 14.2 %collective-permute-start.7 = (bf16[80,2176]{1,0:T(8,128)(2,1)S(1)}, bf16[80,2176]{1,0:T(8,128)(2,1)S(1)}, u32[]{:S(2)}, u32[]{:S(2)}) collective-permute-start(bf16[80,2176]{1,0:T(8,128)(2,1)S(1)} %slice.16), channel_id=1, source_target_pairs={{16,0},{24,8},{17,1},{25,9},{18,2},{26,10},{19,3},{27,11},{4,16},{... | collective-permute-start | bytes 1044488 | tf_op jit(solution)/shard_map/ppermute | solution.py:56
  44.1 5.3 %copy-start.6 = (bf16[160,2048]{1,0:T(8,128)(2,1)}, bf16[160,2048]{1,0:T(8,128)(2,1)S(1)}, u32[]{:S(2)}) copy-start(bf16[160,2048]{1,0:T(8,128)(2,1)S(1)} %collective-permute-done.12.refs_10_) | copy-start | bytes 1966084
  45.0 8.7 %collective-permute-start.13 = (bf16[80,2048]{1,0:T(8,128)(2,1)}, bf16[80,2048]{1,0:T(8,128)(2,1)S(1)}, u32[]{:S(2)}, u32[]{:S(2)}) collective-permute-start(bf16[80,2048]{1,0:T(8,128)(2,1)} %slice.19), channel_id=1, source_target_pairs={{3,0},{11,8},{0,1},{8,9},{1,2},{9,10},{2,3},{10,11},{19,16},{27,24... | collective-permute-start | bytes 983048 | tf_op jit(solution)/shard_map/ppermute | solution.py:50
  49.1 0.9 copy-start.7
  49.1 6.5 %collective-permute-start.11 = (bf16[80,2048]{1,0:T(8,128)(2,1)S(1)}, bf16[80,2048]{1,0:T(8,128)(2,1)S(1)}, u32[]{:S(2)}, u32[]{:S(2)}) collective-permute-start(bf16[80,2048]{1,0:T(8,128)(2,1)S(1)} %slice.18), channel_id=1, source_target_pairs={{1,0},{9,8},{2,1},{10,9},{3,2},{11,10},{0,3},{8,11},{17,16},{25,24... | collective-permute-start | bytes 983048 | tf_op jit(solution)/shard_map/ppermute | solution.py:50
  68.0 37.0 %copy-start = (f32[640,640]{1,0:T(8,128)S(1)}, f32[640,640]{1,0:T(8,128)}, u32[]{:S(2)}) copy-start(f32[640,640]{1,0:T(8,128)} %get-tuple-element.38.refs_6_) | copy-start | bytes 4915204
  68.0 2.5 %collective-permute-start.14 = (f32[32,352]{1,0:T(8,128)S(1)}, f32[32,352]{1,0:T(8,128)S(1)}, u32[]{:S(2)}, u32[]{:S(2)}) collective-permute-start(f32[32,352]{1,0:T(8,128)S(1)} %get-tuple-element.31), channel_id=1, source_target_pairs={{8,0},{0,8},{9,1},{1,9},{10,2},{2,10},{11,3},{3,11},{24,16},{16,24... | collective-permute-start | bytes 135176 | tf_op jit(solution)/shard_map/ppermute | solution.py:62
  71.3 20.9 %all-to-all-start = ((f32[8,88,128]{2,1,0:T(8,128)}), f32[8,88,128]{2,1,0:T(8,128)S(1)}, u32[]{:S(2)}, u32[]{:S(2)}) async-start(f32[8,88,128]{2,1,0:T(8,128)} %get-tuple-element.32), calls=%async_computation | async-start | bytes 720896 | tf_op jit(solution)/shard_map/all_to_all | solution.py:68
  92.6 1.3 collective-permute-start.15
Sparse Core Ops, SparseCore 0:
  9.8 48.1 all-gather.1

commit v9 on v8

--- a/solution.py
+++ b/solution.py
@@ -29,7 +29,7 @@
     (z, y, x, c) for z in range(NZ) for y in range(NY) for x in range(NX) for c in range(NC)
 ]
 LINES = [
-    [device(z + 2 * c, y, x, c) for z in (0, 4, 1, 5, 2, 6, 3, 7)]
+    [device(z, y, x, c) for z in (0, 4, 1, 5, 2, 6, 3, 7)]
     for y in range(NY)
     for x in range(NX)
     for c in range(NC)

time: 143 us -> 143 us (level)
  waiting for transfers between devices: 35.8 us -> 33.1 us
  starting transfers between devices: 34.7 us -> 36.5 us
    ppermute x2, starting transfers between devices: 1.63 us -> 4.52 us  [other_core(): lax.ppermute(value, AXES, [(device(z, y, x, 1 - c), device(z, y, x, c)) f...]
    all_to_all x1, waiting for transfers between devices: 11.3 us -> 8.86 us  [exchange(): lax.all_to_all(chunks, AXES, 0, 0, axis_index_groups=groups, tiled=True)]
where the time goes in v9:
time: 143 us; the launch traced here: 142 us
  starting transfers between devices  36.5 us (26%)
  blocking collectives  35.8 us (25%)
  waiting for transfers between devices  33.1 us (23%)
  Pallas kernels  20.1 us (14%)
  between operations  14.2 us (10%)
  local copies, waits for them, and re-layouts  1.55 us (1%)
    all_to_all x3, blocking collectives, exchange(): lax.all_to_all(chunks, AXES, 0, 0, axis_index_groups=groups, tiled=True)  35.8 us
    ppermute x7, starting transfers between devices, from_x(): lax.ppermute(value, AXES, [(device(z, y, x + k, c), device(z, y, x, c)) f...  12 us
    ppermute x7, waiting for transfers between devices, from_y(): lax.ppermute(value, AXES, [(device(z, y + k, x, c), device(z, y, x, c)) f...  11.5 us
    ppermute x7, starting transfers between devices, from_y(): lax.ppermute(value, AXES, [(device(z, y + k, x, c), device(z, y, x, c)) f...  11.4 us
    pallas_call x7, Pallas kernels, small_kernel(): pl.pallas_call(body, out_shape=out, in_specs=specs or [VM] * len(args), o...  10.1 us
    pallas_call x1, Pallas kernels, local(): pl.pallas_call(functools.partial(tile_kernel, *sizes), out_shape=(shape(p...  9.98 us
    all_to_all x1, waiting for transfers between devices, exchange(): lax.all_to_all(chunks, AXES, 0, 0, axis_index_groups=groups, tiled=True)  8.86 us
    ppermute x7, waiting for transfers between devices, from_x(): lax.ppermute(value, AXES, [(device(z, y, x + k, c), device(z, y, x, c)) f...  8.56 us
  transfers between devices with their start and end apart: 18, of which 9 were waited for; matrix products, arithmetic and copies ran while one was open for 1% of the time, Pallas kernels for 0%

profile of v9, /device:TPU:1, one launch (start us, length us, event | category | flops | bytes accessed | tf_op | source)
XLA Modules:
  0.0 142.4 jit_solution(14194790183163899189)
XLA Ops:
  7.2 0.0 all-gather.2.cloned.1.call-start
  7.2 2.1 %prepare.1 = (bf16[40,4224]{1,0:T(8,128)(2,1)}, bf16[40,2176]{1,0:T(8,128)(2,1)}, bf16[40,2048]{1,0:T(8,128)(2,1)}) custom-call(f32[40,4096]{1,0:T(8,128)} %s_hbm.1, f32[32,40]{1,0:T(8,128)} %bitcast.7), custom_call_target="tpu_custom_call" | custom-call | tf_op jit(solution)/shard_map/prepare/pallas_call | solution.py:86
  9.4 0.0 copy-start.5
  9.4 0.0 all-gather.2.cloned.1.call-update
  9.4 2.2 %collective-permute-start.5 = (bf16[40,2048]{1,0:T(8,128)(2,1)}, bf16[40,2048]{1,0:T(8,128)(2,1)S(1)}, u32[]{:S(2)}, u32[]{:S(2)}) collective-permute-start(bf16[40,2048]{1,0:T(8,128)(2,1)} %get-tuple-element.27), channel_id=1, source_target_pairs={{20,0},{28,8},{21,1},{29,9},{22,2},{30,10},{23,3},{31,11},{0,16},{... | collective-permute-start | bytes 491528 | tf_op jit(solution)/shard_map/ppermute | solution.py:56
  11.6 2.6 %collective-permute-start.4 = (bf16[40,2048]{1,0:T(8,128)(2,1)}, bf16[40,2048]{1,0:T(8,128)(2,1)S(1)}, u32[]{:S(2)}, u32[]{:S(2)}) collective-permute-start(bf16[40,2048]{1,0:T(8,128)(2,1)} %get-tuple-element.27), channel_id=1, source_target_pairs={{4,0},{12,8},{5,1},{13,9},{6,2},{14,10},{7,3},{15,11},{20,16},{28,... | collective-permute-start | bytes 491528 | tf_op jit(solution)/shard_map/ppermute | solution.py:56
  14.2 1.1 collective-permute-start.3
  15.3 1.2 collective-permute-start.2
  16.5 2.5 %collective-permute-start.1 = (bf16[40,2176]{1,0:T(8,128)(2,1)}, bf16[40,2176]{1,0:T(8,128)(2,1)S(1)}, u32[]{:S(2)}, u32[]{:S(2)}) collective-permute-start(bf16[40,2176]{1,0:T(8,128)(2,1)} %get-tuple-element.26), channel_id=1, source_target_pairs={{2,0},{10,8},{3,1},{11,9},{0,2},{8,10},{1,3},{9,11},{18,16},{26,24... | collective-permute-start | bytes 522248 | tf_op jit(solution)/shard_map/ppermute | solution.py:50
  18.9 0.0 collective-permute-done.5
  18.9 1.2 collective-permute-start
  20.1 1.4 %collective-permute-done.4 = bf16[40,2048]{1,0:T(8,128)(2,1)S(1)} collective-permute-done((bf16[40,2048]{1,0:T(8,128)(2,1)}, bf16[40,2048]{1,0:T(8,128)(2,1)S(1)}, u32[]{:S(2)}, u32[]{:S(2)}) %collective-permute-start.4) | collective-permute-done | bytes 163872 | tf_op jit(solution)/shard_map/ppermute | solution.py:56
  21.5 0.0 collective-permute-done.3
  21.5 1.0 pad_maximum_fusion.1.refs_6_
  22.5 0.0 copy-start.2
  22.5 0.0 collective-permute-done.2
  22.5 3.0 %collective-permute-done.1 = bf16[40,2176]{1,0:T(8,128)(2,1)S(1)} collective-permute-done((bf16[40,2176]{1,0:T(8,128)(2,1)}, bf16[40,2176]{1,0:T(8,128)(2,1)S(1)}, u32[]{:S(2)}, u32[]{:S(2)}) %collective-permute-start.1) | collective-permute-done | bytes 174112 | tf_op jit(solution)/shard_map/ppermute | solution.py:50
  25.5 0.0 collective-permute-done
  25.5 0.0 copy-done.5
  25.5 0.1 pad_maximum_fusion.refs_1_
  25.6 0.0 copy-start.1
  25.6 0.5 collective-permute-start.8
  26.1 2.3 %collective-permute-start.6 = (bf16[160,2176]{1,0:T(8,128)(2,1)S(1)}, bf16[160,2176]{1,0:T(8,128)(2,1)S(1)}, u32[]{:S(2)}, u32[]{:S(2)}) collective-permute-start(bf16[160,2176]{1,0:T(8,128)(2,1)S(1)} %pad_maximum_fusion.refs_1_), channel_id=1, source_target_pairs={{16,0},{24,8},{17,1},{25,9},{18,2},{26,10},{19,3},{27,11},{4,16},{... | collective-permute-start | bytes 2088968 | tf_op jit(solution)/shard_map/ppermute | solution.py:56
  28.3 2.6 %collective-permute-start.12 = (bf16[160,2048]{1,0:T(8,128)(2,1)S(1)}, bf16[160,2048]{1,0:T(8,128)(2,1)S(1)}, u32[]{:S(2)}, u32[]{:S(2)}) collective-permute-start(bf16[160,2048]{1,0:T(8,128)(2,1)S(1)} %pad_maximum_fusion.1.refs_6_), channel_id=1, source_target_pairs={{3,0},{11,8},{0,1},{8,9},{1,2},{9,10},{2,3},{10,11},{19,16},{27,24... | collective-permute-start | bytes 1966088 | tf_op jit(solution)/shard_map/ppermute | solution.py:50
  30.9 0.3 collective-permute-start.10
  31.2 10.1 %collective-permute-done.8.refs_5_ = bf16[160,2176]{1,0:T(8,128)(2,1)S(1)} collective-permute-done((bf16[160,2176]{1,0:T(8,128)(2,1)S(1)}, bf16[160,2176]{1,0:T(8,128)(2,1)S(1)}, u32[]{:S(2)}, u32[]{:S(2)}) %collective-permute-start.8) | collective-permute-done | bytes 696352 | tf_op jit(solution)/shard_map/ppermute | solution.py:56
  41.3 0.1 collective-permute-start.9
  41.4 0.0 collective-permute-done.6.refs_2_
  41.4 0.0 copy-start.4
  41.4 2.7 %collective-permute-start.7 = (bf16[80,2176]{1,0:T(8,128)(2,1)S(1)}, bf16[80,2176]{1,0:T(8,128)(2,1)S(1)}, u32[]{:S(2)}, u32[]{:S(2)}) collective-permute-start(bf16[80,2176]{1,0:T(8,128)(2,1)S(1)} %slice.16), channel_id=1, source_target_pairs={{16,0},{24,8},{17,1},{25,9},{18,2},{26,10},{19,3},{27,11},{4,16},{... | collective-permute-start | bytes 1044488 | tf_op jit(solution)/shard_map/ppermute | solution.py:56
  44.1 0.0 collective-permute-done.12.refs_10_
  44.2 0.8 slice.19
  45.0 0.0 copy-done.2
  45.0 4.1 %collective-permute-start.13 = (bf16[80,2048]{1,0:T(8,128)(2,1)}, bf16[80,2048]{1,0:T(8,128)(2,1)S(1)}, u32[]{:S(2)}, u32[]{:S(2)}) collective-permute-start(bf16[80,2048]{1,0:T(8,128)(2,1)} %slice.19), channel_id=1, source_target_pairs={{3,0},{11,8},{0,1},{8,9},{1,2},{9,10},{2,3},{10,11},{19,16},{27,24... | collective-permute-start | bytes 983048 | tf_op jit(solution)/shard_map/ppermute | solution.py:50
  49.1 0.0 collective-permute-done.10.refs_7_
  49.1 0.3 collective-permute-start.11
  49.4 0.0 copy-done.3
  49.4 0.0 copy-done.4
  49.4 0.0 copy-done.6
  49.4 0.5 copy-done.7
  49.9 0.1 pad_add_fusion.at_ref
  50.0 3.7 %collective-permute-done.13.refs_9_ = bf16[80,2048]{1,0:T(8,128)(2,1)S(1)} collective-permute-done((bf16[80,2048]{1,0:T(8,128)(2,1)}, bf16[80,2048]{1,0:T(8,128)(2,1)S(1)}, u32[]{:S(2)}, u32[]{:S(2)}) %collective-permute-start.13) | collective-permute-done | bytes 327712 | tf_op jit(solution)/shard_map/ppermute | solution.py:50
  53.7 1.9 %collective-permute-done.11.refs_8_ = bf16[80,2048]{1,0:T(8,128)(2,1)S(1)} collective-permute-done((bf16[80,2048]{1,0:T(8,128)(2,1)S(1)}, bf16[80,2048]{1,0:T(8,128)(2,1)S(1)}, u32[]{:S(2)}, u32[]{:S(2)}) %collective-permute-start.11) | collective-permute-done | bytes 327712 | tf_op jit(solution)/shard_map/ppermute | solution.py:50
  55.6 0.0 collective-permute-done.9.refs_4_
  55.6 0.0 collective-permute-done.7.refs_3_
  55.6 2.4 %all-gather.2.cloned.1.call-done.refs_0_ = bf16[640,4224]{1,0:T(8,128)(2,1)} async-done(((bf16[40,4224]{1,0:T(8,128)(2,1)}), bf16[640,4224]{1,0:T(8,128)(2,1)}) %all-gather.2.cloned.1.call-update) | async-done | bytes 5406736 | tf_op jit(solution)/shard_map/all_gather | solution.py:367
  58.0 10.0 %tile.1 = (f32[640,640]{1,0:T(8,128)}, f32[64,352]{1,0:T(8,128)S(1)}, f32[32,352]{1,0:T(8,128)S(1)}, f32[32,640]{1,0:T(8,128)S(1)}, f32[32,640]{1,0:T(8,128)S(1)}, /*index=5*/f32[32,32]{1,0:T(8,128)}) custom-call(s32[4]{0:T(128)S(1)} %pad_add_fusion.at_ref, bf16[640,4224]{1,0:T(8,128)(2,1)} %all-gather.2.cloned.1.call-done.refs_0_, ...), custom_call_target="tpu_custom_call" | custom-call | flops 6710886400 | bytes 10485760 | tf_op jit(solution)/shard_map/tile/pallas_call | solution.py:376
  68.0 1.6 %collective-permute-start.14 = (f32[32,352]{1,0:T(8,128)S(1)}, f32[32,352]{1,0:T(8,128)S(1)}, u32[]{:S(2)}, u32[]{:S(2)}) collective-permute-start(f32[32,352]{1,0:T(8,128)S(1)} %get-tuple-element.31), channel_id=1, source_target_pairs={{8,0},{0,8},{9,1},{1,9},{10,2},{2,10},{11,3},{3,11},{24,16},{16,24... | collective-permute-start | bytes 135176 | tf_op jit(solution)/shard_map/ppermute | solution.py:62
  69.6 0.9 collective-permute-done.14.far_ref
  70.5 0.8 share.1
  71.3 8.5 %all-to-all-start = ((f32[8,88,128]{2,1,0:T(8,128)}), f32[8,88,128]{2,1,0:T(8,128)S(1)}, u32[]{:S(2)}, u32[]{:S(2)}) async-start(f32[8,88,128]{2,1,0:T(8,128)} %get-tuple-element.32), calls=%async_computation | async-start | bytes 720896 | tf_op jit(solution)/shard_map/all_to_all | solution.py:68
  79.8 8.9 %all-to-all-done.part_ref = f32[8,88,128]{2,1,0:T(8,128)S(1)} async-done(((f32[8,88,128]{2,1,0:T(8,128)}), f32[8,88,128]{2,1,0:T(8,128)S(1)}, u32[]{:S(2)}, u32[]{:S(2)}) %all-to-all-start) | async-done | bytes 360480 | tf_op jit(solution)/shard_map/all_to_all | solution.py:68
  88.7 0.4 line.1
  89.0 2.9 %collective-permute-start.15 = (f32[32,384]{1,0:T(8,128)S(1)}, f32[32,384]{1,0:T(8,128)S(1)}, u32[]{:S(2)}, u32[]{:S(2)}) collective-permute-start(f32[32,384]{1,0:T(8,128)S(1)} %get-tuple-element.34.near_ref.refs_2_), channel_id=1, source_target_pairs={{8,0},{0,8},{9,1},{1,9},{10,2},{2,10},{11,3},{3,11},{24,16},{16,24... | collective-permute-start | bytes 147464 | tf_op jit(solution)/shard_map/ppermute | solution.py:62
  92.0 0.1 constant_dynamic-slice_fusion.own_ref
  92.0 0.8 collective-permute-done.15.far_ref.refs_3_
  92.8 0.1 spread.1
  92.9 11.0 %all_to_all.20.refs_0_ = f32[16,32,104]{2,1,0:T(8,128)S(1)} all-to-all(f32[16,32,104]{2,1,0:T(8,128)S(1)} %spread.1), channel_id=1, replica_groups={{0,1,2,3,16,17,18,19,4,5,6,7,20,21,22,23},{8,9,10,11,24,25,26,27,12,13,..., dimensions={0} | all-to-all | bytes 425984 | tf_op jit(solution)/shard_map/all_to_all | solution.py:68
  103.9 0.0 copy-done
  103.9 4.8 %step.1 = (f32[16,32,72]{2,1,0:T(8,128)S(1)}, f32[32,40]{1,0:T(8,128)S(1)}, f32[32,40]{1,0:T(8,128)S(1)}, f32[32,40]{1,0:T(8,128)S(1)}, f32[32,32]{1,0:T(8,128)S(1)}) custom-call(s32[4]{0:T(128)S(1)} %pad_add_fusion.at_ref, f32[16,32,104]{2,1,0:T(8,128)S(1)} %all_to_all.20.refs_0_, f32[32,32]{1,0:T(8,128)S(1)} %get-tuple-element.35.refs_1_, ...), custom_call_target="tpu_custom_call" | custom-call | tf_op jit(solution)/shard_map/step/pallas_call | solution.py:86
  108.7 10.2 %all_to_all.21.got_ref = f32[16,32,72]{2,1,0:T(8,128)S(1)} all-to-all(f32[16,32,72]{2,1,0:T(8,128)S(1)} %get-tuple-element.39), channel_id=1, replica_groups={{0,1,2,3,16,17,18,19,4,5,6,7,20,21,22,23},{8,9,10,11,24,25,26,27,12,13,..., dimensions={0} | all-to-all | bytes 294912 | tf_op jit(solution)/shard_map/all_to_all | solution.py:68
  118.9 0.1 image.1
  119.0 14.7 %all_to_all.22.got_ref = f32[16,8,128]{2,1,0:T(8,128)S(1)} all-to-all(f32[16,8,128]{2,1,0:T(8,128)S(1)} %get-tuple-element.41), channel_id=1, replica_groups={{0,32,64,96,128,160,192,224,8,40,72,104,136,168,200,232},{1,33,65,97,12..., dimensions={0} | all-to-all | bytes 131072 | tf_op jit(solution)/shard_map/all_to_all | solution.py:68
  133.7 1.8 %last.1 = (f32[32,40]{1,0:T(8,128)}, f32[32,40]{1,0:T(8,128)}) custom-call(f32[16,8,128]{2,1,0:T(8,128)S(1)} %all_to_all.22.got_ref, f32[32,32]{1,0:T(8,128)S(1)} %get-tuple-element.42.rr, f32[32,40]{1,0:T(8,128)S(1)} %get-tuple-element.40.d_ref.d_own, f32[32,40]{1,0:T(8,128)S(1)} %get-tuple-element.43.image, f32[32,40]{1,0:T(8,128)S(1)} %get-tuple-element.44.weights, ...), custom_call_target="tpu_custom_call" | custom-call | tf_op jit(solution)/shard_map/last/pallas_call | solution.py:86
  (8 shorter events, 0.1 us)
Async XLA Ops:
  7.2 50.9 %all-gather.2.cloned.1.call-start = ((), (), s32[]{:S(2)}) async-start(), calls=%async_computation.4 | async-start | bytes 5744640 | tf_op jit(solution)/shard_map/all_gather | solution.py:367
  9.4 16.2 %copy-start.5 = (bf16[40,2176]{1,0:T(8,128)(2,1)S(1)}, bf16[40,2176]{1,0:T(8,128)(2,1)}, u32[]{:S(2)}) copy-start(bf16[40,2176]{1,0:T(8,128)(2,1)} %get-tuple-element.26) | copy-start | bytes 522244
  9.4 9.6 %collective-permute-start.5 = (bf16[40,2048]{1,0:T(8,128)(2,1)}, bf16[40,2048]{1,0:T(8,128)(2,1)S(1)}, u32[]{:S(2)}, u32[]{:S(2)}) collective-permute-start(bf16[40,2048]{1,0:T(8,128)(2,1)} %get-tuple-element.27), channel_id=1, source_target_pairs={{20,0},{28,8},{21,1},{29,9},{22,2},{30,10},{23,3},{31,11},{0,16},{... | collective-permute-start | bytes 491528 | tf_op jit(solution)/shard_map/ppermute | solution.py:56
  11.6 9.9 %collective-permute-start.4 = (bf16[40,2048]{1,0:T(8,128)(2,1)}, bf16[40,2048]{1,0:T(8,128)(2,1)S(1)}, u32[]{:S(2)}, u32[]{:S(2)}) collective-permute-start(bf16[40,2048]{1,0:T(8,128)(2,1)} %get-tuple-element.27), channel_id=1, source_target_pairs={{4,0},{12,8},{5,1},{13,9},{6,2},{14,10},{7,3},{15,11},{20,16},{28,... | collective-permute-start | bytes 491528 | tf_op jit(solution)/shard_map/ppermute | solution.py:56
  14.2 7.3 %collective-permute-start.3 = (bf16[40,2048]{1,0:T(8,128)(2,1)}, bf16[40,2048]{1,0:T(8,128)(2,1)S(1)}, u32[]{:S(2)}, u32[]{:S(2)}) collective-permute-start(bf16[40,2048]{1,0:T(8,128)(2,1)} %get-tuple-element.27), channel_id=1, source_target_pairs={{16,0},{24,8},{17,1},{25,9},{18,2},{26,10},{19,3},{27,11},{4,16},{... | collective-permute-start | bytes 491528 | tf_op jit(solution)/shard_map/ppermute | solution.py:56
  15.3 7.2 %collective-permute-start.2 = (bf16[40,2176]{1,0:T(8,128)(2,1)}, bf16[40,2176]{1,0:T(8,128)(2,1)S(1)}, u32[]{:S(2)}, u32[]{:S(2)}) collective-permute-start(bf16[40,2176]{1,0:T(8,128)(2,1)} %get-tuple-element.26), channel_id=1, source_target_pairs={{3,0},{11,8},{0,1},{8,9},{1,2},{9,10},{2,3},{10,11},{19,16},{27,24... | collective-permute-start | bytes 522248 | tf_op jit(solution)/shard_map/ppermute | solution.py:50
  16.5 9.0 %collective-permute-start.1 = (bf16[40,2176]{1,0:T(8,128)(2,1)}, bf16[40,2176]{1,0:T(8,128)(2,1)S(1)}, u32[]{:S(2)}, u32[]{:S(2)}) collective-permute-start(bf16[40,2176]{1,0:T(8,128)(2,1)} %get-tuple-element.26), channel_id=1, source_target_pairs={{2,0},{10,8},{3,1},{11,9},{0,2},{8,10},{1,3},{9,11},{18,16},{26,24... | collective-permute-start | bytes 522248 | tf_op jit(solution)/shard_map/ppermute | solution.py:50
  18.9 6.6 %collective-permute-start = (bf16[40,2176]{1,0:T(8,128)(2,1)}, bf16[40,2176]{1,0:T(8,128)(2,1)S(1)}, u32[]{:S(2)}, u32[]{:S(2)}) collective-permute-start(bf16[40,2176]{1,0:T(8,128)(2,1)} %get-tuple-element.26), channel_id=1, source_target_pairs={{1,0},{9,8},{2,1},{10,9},{3,2},{11,10},{0,3},{8,11},{17,16},{25,24... | collective-permute-start | bytes 522248 | tf_op jit(solution)/shard_map/ppermute | solution.py:50
  22.5 22.5 %copy-start.2 = (bf16[160,2048]{1,0:T(8,128)(2,1)}, bf16[160,2048]{1,0:T(8,128)(2,1)S(1)}, u32[]{:S(2)}) copy-start(bf16[160,2048]{1,0:T(8,128)(2,1)S(1)} %pad_maximum_fusion.1.refs_6_) | copy-start | bytes 1966084
  25.6 24.4 %copy-start.1 = (bf16[160,2176]{1,0:T(8,128)(2,1)}, bf16[160,2176]{1,0:T(8,128)(2,1)S(1)}, u32[]{:S(2)}) copy-start(bf16[160,2176]{1,0:T(8,128)(2,1)S(1)} %pad_maximum_fusion.refs_1_) | copy-start | bytes 2088964
  25.6 15.7 %collective-permute-start.8 = (bf16[160,2176]{1,0:T(8,128)(2,1)S(1)}, bf16[160,2176]{1,0:T(8,128)(2,1)S(1)}, u32[]{:S(2)}, u32[]{:S(2)}) collective-permute-start(bf16[160,2176]{1,0:T(8,128)(2,1)S(1)} %pad_maximum_fusion.refs_1_), channel_id=1, source_target_pairs={{20,0},{28,8},{21,1},{29,9},{22,2},{30,10},{23,3},{31,11},{0,16},{... | collective-permute-start | bytes 2088968 | tf_op jit(solution)/shard_map/ppermute | solution.py:56
  26.1 15.3 %collective-permute-start.6 = (bf16[160,2176]{1,0:T(8,128)(2,1)S(1)}, bf16[160,2176]{1,0:T(8,128)(2,1)S(1)}, u32[]{:S(2)}, u32[]{:S(2)}) collective-permute-start(bf16[160,2176]{1,0:T(8,128)(2,1)S(1)} %pad_maximum_fusion.refs_1_), channel_id=1, source_target_pairs={{16,0},{24,8},{17,1},{25,9},{18,2},{26,10},{19,3},{27,11},{4,16},{... | collective-permute-start | bytes 2088968 | tf_op jit(solution)/shard_map/ppermute | solution.py:56
  28.3 15.8 %collective-permute-start.12 = (bf16[160,2048]{1,0:T(8,128)(2,1)S(1)}, bf16[160,2048]{1,0:T(8,128)(2,1)S(1)}, u32[]{:S(2)}, u32[]{:S(2)}) collective-permute-start(bf16[160,2048]{1,0:T(8,128)(2,1)S(1)} %pad_maximum_fusion.1.refs_6_), channel_id=1, source_target_pairs={{3,0},{11,8},{0,1},{8,9},{1,2},{9,10},{2,3},{10,11},{19,16},{27,24... | collective-permute-start | bytes 1966088 | tf_op jit(solution)/shard_map/ppermute | solution.py:50
  30.9 18.2 %collective-permute-start.10 = (bf16[160,2048]{1,0:T(8,128)(2,1)S(1)}, bf16[160,2048]{1,0:T(8,128)(2,1)S(1)}, u32[]{:S(2)}, u32[]{:S(2)}) collective-permute-start(bf16[160,2048]{1,0:T(8,128)(2,1)S(1)} %pad_maximum_fusion.1.refs_6_), channel_id=1, source_target_pairs={{1,0},{9,8},{2,1},{10,9},{3,2},{11,10},{0,3},{8,11},{17,16},{25,24... | collective-permute-start | bytes 1966088 | tf_op jit(solution)/shard_map/ppermute | solution.py:50
  41.2 8.1 %copy-start.3 = (bf16[160,2176]{1,0:T(8,128)(2,1)}, bf16[160,2176]{1,0:T(8,128)(2,1)S(1)}, u32[]{:S(2)}) copy-start(bf16[160,2176]{1,0:T(8,128)(2,1)S(1)} %collective-permute-done.8.refs_5_) | copy-start | bytes 2088964
  41.3 14.3 %collective-permute-start.9 = (bf16[80,2176]{1,0:T(8,128)(2,1)S(1)}, bf16[80,2176]{1,0:T(8,128)(2,1)S(1)}, u32[]{:S(2)}, u32[]{:S(2)}) collective-permute-start(bf16[80,2176]{1,0:T(8,128)(2,1)S(1)} %slice.17), channel_id=1, source_target_pairs={{20,0},{28,8},{21,1},{29,9},{22,2},{30,10},{23,3},{31,11},{0,16},{... | collective-permute-start | bytes 1044488 | tf_op jit(solution)/shard_map/ppermute | solution.py:56
  41.4 8.0 %copy-start.4 = (bf16[160,2176]{1,0:T(8,128)(2,1)}, bf16[160,2176]{1,0:T(8,128)(2,1)S(1)}, u32[]{:S(2)}) copy-start(bf16[160,2176]{1,0:T(8,128)(2,1)S(1)} %collective-permute-done.6.refs_2_) | copy-start | bytes 2088964
  41.4 14.2 %collective-permute-start.7 = (bf16[80,2176]{1,0:T(8,128)(2,1)S(1)}, bf16[80,2176]{1,0:T(8,128)(2,1)S(1)}, u32[]{:S(2)}, u32[]{:S(2)}) collective-permute-start(bf16[80,2176]{1,0:T(8,128)(2,1)S(1)} %slice.16), channel_id=1, source_target_pairs={{16,0},{24,8},{17,1},{25,9},{18,2},{26,10},{19,3},{27,11},{4,16},{... | collective-permute-start | bytes 1044488 | tf_op jit(solution)/shard_map/ppermute | solution.py:56
  44.1 5.3 %copy-start.6 = (bf16[160,2048]{1,0:T(8,128)(2,1)}, bf16[160,2048]{1,0:T(8,128)(2,1)S(1)}, u32[]{:S(2)}) copy-start(bf16[160,2048]{1,0:T(8,128)(2,1)S(1)} %collective-permute-done.12.refs_10_) | copy-start | bytes 1966084
  45.0 8.7 %collective-permute-start.13 = (bf16[80,2048]{1,0:T(8,128)(2,1)}, bf16[80,2048]{1,0:T(8,128)(2,1)S(1)}, u32[]{:S(2)}, u32[]{:S(2)}) collective-permute-start(bf16[80,2048]{1,0:T(8,128)(2,1)} %slice.19), channel_id=1, source_target_pairs={{3,0},{11,8},{0,1},{8,9},{1,2},{9,10},{2,3},{10,11},{19,16},{27,24... | collective-permute-start | bytes 983048 | tf_op jit(solution)/shard_map/ppermute | solution.py:50
  49.1 0.9 copy-start.7
  49.1 6.5 %collective-permute-start.11 = (bf16[80,2048]{1,0:T(8,128)(2,1)S(1)}, bf16[80,2048]{1,0:T(8,128)(2,1)S(1)}, u32[]{:S(2)}, u32[]{:S(2)}) collective-permute-start(bf16[80,2048]{1,0:T(8,128)(2,1)S(1)} %slice.18), channel_id=1, source_target_pairs={{1,0},{9,8},{2,1},{10,9},{3,2},{11,10},{0,3},{8,11},{17,16},{25,24... | collective-permute-start | bytes 983048 | tf_op jit(solution)/shard_map/ppermute | solution.py:50
  68.0 35.9 %copy-start = (f32[640,640]{1,0:T(8,128)S(1)}, f32[640,640]{1,0:T(8,128)}, u32[]{:S(2)}) copy-start(f32[640,640]{1,0:T(8,128)} %get-tuple-element.38.refs_6_) | copy-start | bytes 4915204
  68.0 2.5 %collective-permute-start.14 = (f32[32,352]{1,0:T(8,128)S(1)}, f32[32,352]{1,0:T(8,128)S(1)}, u32[]{:S(2)}, u32[]{:S(2)}) collective-permute-start(f32[32,352]{1,0:T(8,128)S(1)} %get-tuple-element.31), channel_id=1, source_target_pairs={{8,0},{0,8},{9,1},{1,9},{10,2},{2,10},{11,3},{3,11},{24,16},{16,24... | collective-permute-start | bytes 135176 | tf_op jit(solution)/shard_map/ppermute | solution.py:62
  71.3 17.4 %all-to-all-start = ((f32[8,88,128]{2,1,0:T(8,128)}), f32[8,88,128]{2,1,0:T(8,128)S(1)}, u32[]{:S(2)}, u32[]{:S(2)}) async-start(f32[8,88,128]{2,1,0:T(8,128)} %get-tuple-element.32), calls=%async_computation | async-start | bytes 720896 | tf_op jit(solution)/shard_map/all_to_all | solution.py:68
  89.0 3.8 %collective-permute-start.15 = (f32[32,384]{1,0:T(8,128)S(1)}, f32[32,384]{1,0:T(8,128)S(1)}, u32[]{:S(2)}, u32[]{:S(2)}) collective-permute-start(f32[32,384]{1,0:T(8,128)S(1)} %get-tuple-element.34.near_ref.refs_2_), channel_id=1, source_target_pairs={{8,0},{0,8},{9,1},{1,9},{10,2},{2,10},{11,3},{3,11},{24,16},{16,24... | collective-permute-start | bytes 147464 | tf_op jit(solution)/shard_map/ppermute | solution.py:62
Sparse Core Ops, SparseCore 0:
  9.8 48.1 all-gather.1
